TPU v7x, 32 devices: a whole 2x2x4 slice. The times are simulated.
32 devices in a mesh: grp: 4 (over z), sub: 8 (over y, x, core).
Axes of the slice: x: 2, y: 2, z: 4, core: 2. Of those that a mesh axis runs over, the one named last changes fastest.
Arguments:
- leaf_bases: bfloat16 [384, 256, 128], P(('grp', 'sub')), may hold values from -6 to 6
- leaf_transfers: bfloat16 [384, 128, 128], P(('grp', 'sub')), may hold values from -1 to 2
- leaf_blocks: bfloat16 [384, 6, 128, 128], P(('grp', 'sub')), may hold values from -6 to 6
- leaf_partner_dev: int32 [384, 6], P(('grp', 'sub')), may hold values from 0 to 7, all different within a row; in each aligned block of 12 rows (0 to 11, 12 to 23, ...) at most 12 rows name the same one
- leaf_partner_slot: int32 [384, 6], P(('grp', 'sub')), may hold values from 0 to 11
- parent_blocks: bfloat16 [192, 3, 128, 128], P(('grp', 'sub')), may hold values from -6 to 6
- parent_partner_group: int32 [192, 3], P(('grp', 'sub')), may hold values from 0 to 3, all different within a row; in each aligned block of 6 rows (0 to 5, 6 to 11, ...) at most 6 rows name the same one
- parent_partner_slot: int32 [192, 3], P(('grp', 'sub')), may hold values from 0 to 5
- leaf_start: float32 [64, 128], replicated, may hold values from -6 to 6
- parent_start: float32 [64, 128], replicated, may hold values from -6 to 6
Outputs:
- new_leaf_bases: bfloat16 [384, 64, 256], P(('grp', 'sub'))
- new_leaf_blocks: bfloat16 [384, 6, 4096], P(('grp', 'sub'))
- new_parent_blocks: bfloat16 [192, 3, 4096], P(('grp', 'sub'))
Inputs may be any that keep to these rules, and one draw needn't show every extreme that they name: `leaf_partner_dev`: one leaf's partners lie on different devices of its group; among the leaves of one device no index appears more than 12 times, and that count is reached on some device. `parent_partner_group`: one parent's partners lie in different groups; among the parents of one device no group appears more than 6 times, and that count is reached on some device.
All inputs are finite; a program needn't handle non-finite values.
Results may differ from a plain program's by a relative error of at most 0.033.
Values may be sent and summed in bfloat16 or wider, within the bound.
No kernel may reach another device: no remote copies, remote signals or barrier semaphores. Data moves between devices by JAX's collectives and lax.ppermute only.
A program may use at most 64 MiB of HBM per device.

v0:
```python
import jax
import jax.numpy as jnp
from jax import lax
from jax.sharding import PartitionSpec as P

TOP_PRECISION = lax.Precision.HIGHEST


def partner(block, axis, apart):
    count = lax.axis_size(axis)
    route = []
    for low in range(count):
        high = low | 1 << apart
        if high != low and high < count:
            route += [(low, high), (high, low)]
    return lax.ppermute(block, axis, route)


def subspace(weight, start_rows):
    basis_rows = jnp.broadcast_to(start_rows, (weight.shape[0],) + start_rows.shape)
    image_rows = jnp.einsum("brn,bnm->brm", basis_rows, weight, precision=TOP_PRECISION)
    image_rows = jnp.einsum("brn,bnm->brm", image_rows, weight, precision=TOP_PRECISION)
    cross_gram = jnp.einsum("brn,bsn->brs", image_rows, image_rows, precision=TOP_PRECISION)
    factor = jnp.linalg.cholesky(cross_gram)
    return jax.scipy.linalg.solve_triangular(factor, image_rows, lower=True)


def shards(
    leaf_bases,
    leaf_transfers,
    leaf_blocks,
    leaf_partner_dev,
    leaf_partner_slot,
    parent_blocks,
    parent_partner_group,
    parent_partner_slot,
    leaf_start,
    parent_start,
):
    leaf_count = leaf_blocks.shape[0]
    leaf_links = leaf_blocks.shape[1]
    half_count = parent_blocks.shape[0]
    parent_links = parent_blocks.shape[1]
    rank_new = leaf_start.shape[0]
    rank_old = leaf_start.shape[1]
    member = lax.axis_index("sub") % 2
    parent_weight = jnp.einsum(
        "pckl,pcml->pkm", parent_blocks, parent_blocks, preferred_element_type=jnp.float32
    )
    partner_weight = partner(parent_weight.astype(jnp.bfloat16), "sub", 0).astype(
        parent_weight.dtype
    )
    descended = jnp.where(
        member == 0,
        jnp.concatenate([parent_weight, partner_weight], axis=0),
        jnp.concatenate([partner_weight, parent_weight], axis=0),
    )
    weight = jnp.einsum(
        "jckl,jcml->jkm", leaf_blocks, leaf_blocks, preferred_element_type=jnp.float32
    )
    transfers = leaf_transfers.astype(jnp.float32)
    carried = jnp.einsum("jka,jab->jkb", transfers, descended, precision=TOP_PRECISION)
    weight = weight + jnp.einsum("jkb,jmb->jkm", carried, transfers, precision=TOP_PRECISION)
    change = subspace(weight, leaf_start).astype(jnp.bfloat16)
    projected = jnp.einsum(
        "jrk,jkm->jrm", change, leaf_transfers, preferred_element_type=jnp.float32
    )
    sent_rows = lax.dynamic_slice_in_dim(projected, (1 - member) * half_count, half_count, 0)
    received_rows = partner(sent_rows.astype(jnp.bfloat16), "sub", 0).astype(sent_rows.dtype)
    kept_rows = lax.dynamic_slice_in_dim(projected, member * half_count, half_count, 0)
    stacked = jnp.where(
        member == 0,
        jnp.concatenate([kept_rows, received_rows], axis=1),
        jnp.concatenate([received_rows, kept_rows], axis=1),
    )
    new_leaf_bases = jnp.einsum(
        "jrk,jnk->jrn", change, leaf_bases, preferred_element_type=jnp.float32
    ).astype(jnp.bfloat16)
    leaf_midpoint = jnp.einsum(
        "jrk,jckl->jcrl", change, leaf_blocks, preferred_element_type=jnp.float32
    ).astype(jnp.bfloat16)
    parent_left = jnp.einsum("prk,pkm->prm", stacked, parent_weight, precision=TOP_PRECISION)
    parent_gram = jnp.einsum("prm,psm->prs", parent_left, stacked, precision=TOP_PRECISION)
    parent_rows = subspace(parent_gram, parent_start)
    parent_change = jnp.einsum(
        "prs,psk->prk", parent_rows, stacked, precision=TOP_PRECISION
    ).astype(jnp.bfloat16)
    parent_midpoint = jnp.einsum(
        "prk,pckl->pcrl", parent_change, parent_blocks, preferred_element_type=jnp.float32
    ).astype(jnp.bfloat16)
    everyone = lax.all_gather(change, "sub", axis=0, tiled=True)
    distant_site = everyone[(leaf_partner_dev * leaf_count + leaf_partner_slot).reshape(-1)]
    distant_site = distant_site.reshape(leaf_count, leaf_links, rank_new, rank_old)
    new_leaf_blocks = jnp.einsum(
        "jcrl,jcsl->jcrs", leaf_midpoint, distant_site, preferred_element_type=jnp.float32
    ).astype(jnp.bfloat16)
    new_leaf_blocks = new_leaf_blocks.reshape(leaf_count, leaf_links, rank_new * rank_new)
    everyone_parents = lax.all_gather(parent_change, "grp", axis=0, tiled=True)
    distant_parents = everyone_parents[
        (parent_partner_group * half_count + parent_partner_slot).reshape(-1)
    ]
    distant_parents = distant_parents.reshape(half_count, parent_links, rank_new, rank_old)
    new_parent_blocks = jnp.einsum(
        "juog,juqg->juoq", parent_midpoint, distant_parents, preferred_element_type=jnp.float32
    ).astype(jnp.bfloat16)
    new_parent_blocks = new_parent_blocks.reshape(half_count, parent_links, rank_new * rank_new)
    return (new_leaf_bases, new_leaf_blocks, new_parent_blocks)


def solution(mesh):
    placed = (
        P(("grp", "sub"), None, None),
        P(("grp", "sub"), None, None),
        P(("grp", "sub"), None, None, None),
        P(("grp", "sub"), None),
        P(("grp", "sub"), None),
        P(("grp", "sub"), None, None, None),
        P(("grp", "sub"), None),
        P(("grp", "sub"), None),
        P(),
        P(),
    )
    return jax.shard_map(
        shards,
        mesh=mesh,
        in_specs=placed,
        out_specs=(
            P(("grp", "sub"), None, None),
            P(("grp", "sub"), None, None),
            P(("grp", "sub"), None, None),
        ),
        check_vma=False,
    )
```

profile of v0, /device:TPU:0, one launch (start us, length us, event | category | flops | bytes accessed | tf_op | source)
XLA Modules:
  0.0 278.2 jit_solution(2701858961509193777)
XLA Ops:
  7.2 0.0 all-gather.2.cloned.1.call-start
  7.2 1.8 fusion.30
  9.0 0.5 collective-permute-start
  9.6 1.7 convolution_bitcast_fusion
  11.3 0.1 copy.38
  11.4 0.1 reshape.105
  11.5 0.6 pad_clamp_fusion
  12.1 1.3 multiply_add_fusion
  13.4 0.8 copy.35
  14.1 0.6 reshape.102
  14.7 0.7 fusion.24
  15.4 0.6 pad_clamp_fusion.1
  16.1 0.6 fusion.2
  16.7 1.0 convolution_add_fusion
  17.6 0.8 fusion.16
  18.4 0.8 fusion.31
  19.3 1.5 fusion.32
  20.8 1.9 copy.33
  22.7 1.9 fusion.9
  24.6 71.8 %custom-call.16 = f32[12,64,64]{2,1,0:T(8,128)} custom-call(f32[12,64,64]{2,1,0:T(8,128)} %fusion.9), custom_call_target="Cholesky" | custom-call | tf_op jit(solution)/shard_map/jit(cholesky)/cholesky | solution.py:24
  96.3 1.1 select_reduce_fusion
  97.4 0.1 compare_reduce_fusion
  97.5 1.9 select_bitcast_fusion
  99.3 60.4 %custom-call.17 = f32[12,1,64,64]{2,3,1,0:T(8,128)} custom-call(f32[12,1,64,64]{3,2,1,0:T(8,128)} %select_bitcast_fusion), custom_call_target="InvertDiagBlocksLowerTriangular" | custom-call | tf_op jit(solution)/shard_map/jit(_solve_triangular)/vmap()/triangular_solve | solution.py:25
  159.7 1.8 convolution_convert_fusion.5
  161.5 1.3 fusion.33
  162.9 0.1 collective-permute-start.1
  163.0 2.4 convolution_convert_fusion.2
  165.5 0.5 fusion.23
  166.0 0.9 fusion.22
  166.9 0.5 fusion.20
  167.4 0.5 fusion.34
  167.9 0.4 fusion.35
  168.4 0.1 copy.36
  168.5 0.7 fusion.15
  169.2 36.0 %custom-call.18 = f32[6,64,64]{2,1,0:T(8,128)S(1)} custom-call(f32[6,64,64]{2,1,0:T(8,128)} %fusion.15), custom_call_target="Cholesky" | custom-call | tf_op jit(solution)/shard_map/jit(cholesky)/cholesky | solution.py:24
  205.2 0.1 compare_reduce_fusion.1
  205.3 0.8 select_bitcast_fusion.1
  206.1 30.9 %custom-call.19 = f32[6,1,64,64]{2,3,1,0:T(8,128)} custom-call(f32[6,1,64,64]{3,2,1,0:T(8,128)} %select_bitcast_fusion.1), custom_call_target="InvertDiagBlocksLowerTriangular" | custom-call | tf_op jit(solution)/shard_map/jit(_solve_triangular)/vmap()/triangular_solve | solution.py:25
  236.9 1.4 fusion.13
  238.4 1.5 convolution_convert_fusion.6
  239.9 16.4 %all_gather.7 = bf16[24,64,128]{2,1,0:T(8,128)(2,1)S(1)} all-gather(bf16[6,64,128]{2,1,0:T(8,128)(2,1)S(1)} %convolution_convert_fusion.6), channel_id=1, replica_groups=mesh['grp'=4,'sub'=8] {'grp'}, dimensions={0}, use_global_device_ids=true | all-gather | bytes 491520 | tf_op jit(solution)/shard_map/all_gather | solution.py:98
  256.2 1.4 gather_fusion.1
  257.7 2.1 convolution_convert_fusion.3
  259.8 1.9 reshape.107
  261.7 3.3 %gather_fusion = bf16[72,64,128]{2,1,0:T(8,128)(2,1)} fusion(bf16[96,64,128]{2,1,0:T(8,128)(2,1)} %all-gather.2.cloned.1.call-done, s32[1024]{0:T(1024)} %pad_clamp_fusion.1), kind=kCustom, calls=%fused_computation | custom fusion | bytes 2359584 | tf_op jit(solution)/shard_map/gather | solution.py:92
  265.0 3.4 %convolution_convert_fusion = bf16[12,6,64,64]{3,2,1,0:T(8,128)(2,1)} fusion(bf16[12,6,64,128]{3,2,1,0:T(8,128)(2,1)} %bitcast.84, bf16[12,6,128,128]{3,2,1,0:T(8,128)(2,1)S(1)} %copy-done, bf16[12,64,128]{2,1,0:T(8,128)(2,1)S(1)} %copy-done.3), kind=kOutput, calls=%fused_computation.2 | convolution fusion | flops 227377152 | bytes 4325376 | tf_op jit(solution)/shard_map/jcrl,jcsl->jcrs/dot_general | solution.py:94
  268.4 2.9 %reshape.104 = bf16[12,6,4096]{2,1,0:T(8,128)(2,1)} reshape(bf16[12,6,64,64]{3,2,1,0:T(8,128)(2,1)} %convolution_convert_fusion) | data formatting | bytes 1179648 | tf_op jit(solution)/shard_map/reshape | solution.py:97
  (39 shorter events, 0.2 us)
Async XLA Ops:
  7.2 2.4 copy-start
  7.2 254.5 %all-gather.2.cloned.1.call-start = ((), (), s32[]{:S(2)}) async-start(), calls=%async_computation | async-start | bytes 1769472 | tf_op jit(solution)/shard_map/all_gather | solution.py:91
  9.0 7.0 %collective-permute-start = (bf16[6,128,128]{2,1,0:T(8,128)(2,1)S(1)}, bf16[6,128,128]{2,1,0:T(8,128)(2,1)S(1)}, u32[]{:S(2)}, u32[]{:S(2)}) collective-permute-start(bf16[6,128,128]{2,1,0:T(8,128)(2,1)S(1)} %get-tuple-element.3), channel_id=1, source_target_pairs={{0,1},{1,0},{2,3},{3,2},{4,5},{5,4},{6,7},{7,6},{8,9},{9,8},{10,11... | collective-permute-start | bytes 589832 | tf_op jit(solution)/shard_map/ppermute | solution.py:16
  9.6 1.7 copy-start.11
  9.6 1.7 copy-start.12
  9.6 6.5 %copy-start.4 = (bf16[12,128,128]{2,1,0:T(8,128)(2,1)S(1)}, bf16[12,128,128]{2,1,0:T(8,128)(2,1)}, u32[]{:S(2)}) copy-start(bf16[12,128,128]{2,1,0:T(8,128)(2,1)} %param.11) | copy-start | bytes 1179652
  15.4 1.3 copy-start.5
  16.7 1.0 copy-start.9
  161.5 1.3 copy-start.2
  162.9 2.5 collective-permute-start.1
  165.4 1.6 copy-start.10
  165.4 2.0 copy-start.6
  165.4 2.5 copy-start.8
  167.9 70.5 %copy-start.7 = (f32[6,64,128]{2,1,0:T(8,128)S(1)}, f32[6,64,128]{2,1,0:T(8,128)}, u32[]{:S(2)}) copy-start(f32[6,64,128]{2,1,0:T(8,128)} %copy-done.6) | copy-start | bytes 589828
  169.2 88.5 %copy-start.1 = (bf16[6,3,128,128]{3,2,1,0:T(8,128)(2,1)S(1)}, bf16[6,3,128,128]{3,2,1,0:T(8,128)(2,1)}, u32[]{:S(2)}) copy-start(bf16[6,3,128,128]{3,2,1,0:T(8,128)(2,1)} %param.15) | copy-start | bytes 1769476
  259.8 5.3 %copy-start.3 = (bf16[12,64,128]{2,1,0:T(8,128)(2,1)S(1)}, bf16[12,64,128]{2,1,0:T(8,128)(2,1)}, u32[]{:S(2)}) copy-start(bf16[12,64,128]{2,1,0:T(8,128)(2,1)} %copy-done.2) | copy-start | bytes 589828
Sparse Core Ops, SparseCore 0:
  163.0 28.3 all-gather.1
where the time goes:
time: 279 us; the launch traced here: 278 us
  other arithmetic  209 us (75%)
  matrix products  24.7 us (9%)
  blocking collectives  16.4 us (6%)
  between operations  14.4 us (5%)
  local copies, waits for them, and re-layouts  13.3 us (5%)
    another operation x7, other arithmetic, subspace(): factor = jnp.linalg.cholesky(cross_gram)  109 us
    another operation x5, other arithmetic, subspace(): return jax.scipy.linalg.solve_triangular(factor, image_rows, lower=True)  93.9 us
    all_gather x1, blocking collectives, shards(): everyone_parents = lax.all_gather(parent_change, 'grp', axis=0, tiled=True)  16.4 us
  transfers between devices with their start and end apart: 3, of which 0 were waited for; matrix products, arithmetic and copies ran while one was open for 32% of the time, Pallas kernels for 0%

commit v1 on v0

v1 whole, which is shorter than its diff:
```python
import jax
import jax.numpy as jnp
from jax import lax
from jax.experimental import pallas as pl
from jax.experimental.pallas import tpu as pltpu
from jax.sharding import PartitionSpec as P

F32 = jnp.float32
BF16 = jnp.bfloat16
PIVOTS = 4
MIB = 1 << 20


def cat(parts, axis):
    return jnp.concatenate(parts, axis=axis)


def halves(value):
    high = value.astype(BF16)
    low = (value - high.astype(F32)).astype(BF16)
    return high, low


def dot(left, right):
    return lax.dot_general(left, right, (((1,), (0,)), ((), ())), preferred_element_type=F32)


def dot_t(left, right):
    return lax.dot_general(left, right, (((1,), (1,)), ((), ())), preferred_element_type=F32)


def fold(value):
    width = value.shape[1] // 2
    return value[:, :width] + value[:, width:]


def wide(value):
    return cat(halves(value), 1)


def tall(value):
    both = wide(value)
    return cat([both, both], 0)


def gram_sum(parts):
    row = cat(parts, 1)
    return dot_t(row, row)


def eliminate(grid, made, rank):
    shape = (8, 128)
    lane = lax.broadcasted_iota(jnp.int32, shape, 1)
    half = jnp.where(lane < rank, 0, rank)
    local = lane - half

    def spread(value, column):
        return jnp.take_along_axis(value, half + column, axis=1)

    for first in range(0, rank, PIVOTS):
        last = first + PIVOTS
        rows = [grid[8 * i : 8 * i + 8, :] for i in range(first, last)]
        corner = [[None] * PIVOTS for _ in range(PIVOTS)]
        for p in range(PIVOTS):
            for q in range(p, PIVOTS):
                corner[p][q] = spread(rows[p], first + q)
        inside = (local >= first) & (local < last)
        rows = [
            jnp.where(inside, (local == first + p).astype(F32), rows[p]) for p in range(PIVOTS)
        ]
        inverse = []
        for p in range(PIVOTS):
            inverse.append(1.0 / corner[p][p])
            for q in range(p + 1, PIVOTS):
                factor = corner[p][q] * inverse[p]
                for s in range(q, PIVOTS):
                    corner[q][s] = corner[q][s] - factor * corner[p][s]
                rows[q] = rows[q] - factor * rows[p]
        scaled = [rows[p] * inverse[p] for p in range(PIVOTS)]
        for i in range(last, rank):
            row = jnp.where(inside, 0.0, grid[8 * i : 8 * i + 8, :])
            for p in range(PIVOTS):
                row = row - spread(scaled[p], i) * rows[p]
            grid[8 * i : 8 * i + 8, :] = row
        for p in range(PIVOTS):
            i = first + p
            done = jnp.where(local < last, rows[p] * lax.rsqrt(corner[p][p]), 0.0)
            made[8 * i : 8 * i + 8, :] = done


def pair_rows(made, stored, pair, rank):
    wide_rank = 2 * rank
    factor = wide(made[pl.ds(pair, rank, stride=8), :])
    both = stored[pair]
    zero = jnp.zeros((rank, both.shape[1]), F32)
    spread = cat([cat([both[:rank], zero], 1), cat([zero, both[rank:]], 1)], 0)
    high, low = halves(spread)
    return dot(factor, cat([high, high], 0)) + dot(factor, cat([low, low], 0))


def store_gram(grid, stored, pair, images, rank):
    both = cat(images, 0)
    stored[pair] = both
    both_wide = wide(both)
    high, low = halves(both)
    full = dot_t(both_wide, cat([cat([high, high], 1), cat([low, low], 1)], 0))
    full = fold(full)
    lane = lax.broadcasted_iota(jnp.int32, (rank, 2 * rank), 1)
    grid[pl.ds(pair, rank, stride=8), :] = jnp.where(lane < rank, full[:rank], full[rank:])


def sent_weights(blocks, weight, held, sems):
    half = weight.shape[0]
    links = blocks.shape[1]
    start = (1 - lax.axis_index("sub") % 2) * half
    copies = [
        pltpu.make_async_copy(blocks.at[start + j], held.at[j], sems.at[j]) for j in range(half)
    ]
    for copy in copies:
        copy.start()
    for j in range(half):
        copies[j].wait()
        weight[j] = gram_sum([held[j, c] for c in range(links)])


def kept_weights(blocks, parents, weight, parent_weight, held, held_parents, sems):
    half = weight.shape[0]
    links = blocks.shape[1]
    start = (lax.axis_index("sub") % 2) * half
    copies = [
        pltpu.make_async_copy(blocks.at[start + j], held.at[j], sems.at[j]) for j in range(half)
    ] + [
        pltpu.make_async_copy(parents.at[j], held_parents.at[j], sems.at[half + j])
        for j in range(half)
    ]
    for copy in copies:
        copy.start()
    for j in range(half):
        copies[j].wait()
        weight[j] = gram_sum([held[j, c] for c in range(links)])
    for j in range(half):
        copies[half + j].wait()
        parent_weight[j] = gram_sum([held_parents[j, c] for c in range(parents.shape[1])])


def leaf_step(own, other, parent, transfers, other_transfers, start, change, stacked, grid, made, stored):
    rank = start.shape[0]
    half = own.shape[0]
    member = lax.axis_index("sub") % 2
    start_wide = wide(start[...])
    for j in range(half):
        own_move = transfers[member * half + j]
        other_move = other_transfers[j]
        carried = fold(dot(cat([own_move, other_move], 0), wide(parent[j])))
        images = []
        size = own_move.shape[0]
        for at, (move, weight) in enumerate(((own_move, own), (other_move, other))):
            full = weight[j] + dot_t(
                wide(carried[at * size : at * size + size]), cat([move, move], 1)
            )
            folded = tall(full)
            image = fold(dot(start_wide, folded))
            images.append(fold(dot(wide(image), folded)))
        store_gram(grid, stored, j, images, rank)
    eliminate(grid, made, rank)
    for j in range(half):
        found = pair_rows(made, stored, j, rank).astype(BF16)
        width = found.shape[1] // 2
        mine, theirs = found[:, :width], found[:, width:]
        change[0, j] = mine
        change[1, j] = theirs
        stacked[j, member] = dot(mine, transfers[member * half + j])
        stacked[j, 1 - member] = dot(theirs, other_transfers[j])


def parent_step(parent, stacked, start, change, grid, made, stored):
    rank = start.shape[0]
    half = parent.shape[0]
    start_wide = wide(start[...])
    for pair in range(half // 2):
        images = []
        for j in (2 * pair, 2 * pair + 1):
            rows = cat([stacked[j, 0], stacked[j, 1]], 0)
            rows_wide = wide(rows)
            high, low = halves(rows)
            left = fold(dot(rows_wide, tall(parent[j])))
            gram = fold(
                dot_t(wide(left), cat([cat([high, high], 1), cat([low, low], 1)], 0))
            )
            folded = tall(gram)
            image = fold(dot(start_wide, folded))
            images.append(fold(dot(wide(image), folded)))
        store_gram(grid, stored, pair, images, rank)
    eliminate(grid, made, rank)
    for pair in range(half // 2):
        found = pair_rows(made, stored, pair, rank)
        width = found.shape[1] // 2
        for at in range(2):
            j = 2 * pair + at
            rows = cat([stacked[j, 0], stacked[j, 1]], 0)
            mixed = wide(found[:, at * width : at * width + width])
            change[j] = fold(dot(mixed, tall(rows))).astype(BF16)


def parted(value, scratch):
    scratch[...] = value.astype(F32)
    count = value.shape[0] // 2
    return cat(
        [scratch[pl.ds(0, count, stride=2), :], scratch[pl.ds(1, count, stride=2), :]], 0
    ).astype(BF16)


def middle_step(
    change, swapped, parent_change, bases, blocks, parents,
    new_bases, leaf_half, parent_half,
    held_bases, held, held_parents, order, sems,
):
    half = change.shape[1]
    count, links = blocks.shape[0], blocks.shape[1]
    member = lax.axis_index("sub") % 2
    where = [member * half + j for j in range(half)] + [(1 - member) * half + j for j in range(half)]
    copies = []
    for at in range(count):
        copies.append(
            (
                pltpu.make_async_copy(bases.at[where[at]], held_bases.at[at], sems.at[2 * at]),
                pltpu.make_async_copy(blocks.at[where[at]], held.at[at], sems.at[2 * at + 1]),
            )
        )
    whole = pltpu.make_async_copy(parents, held_parents, sems.at[2 * count])
    for first, second in copies:
        first.start()
        second.start()
    whole.start()
    for at in range(count):
        rows = change[0, at] if at < half else swapped[1, at - half]
        ordered = parted(rows, order.at[at % 2])
        copies[at][0].wait()
        new_bases[where[at]] = dot_t(rows, held_bases[at]).astype(BF16)
        copies[at][1].wait()
        leaf_half[where[at]] = dot(ordered, cat([held[at, c] for c in range(links)], 1)).astype(BF16)
    whole.wait()
    for j in range(half):
        ordered = parted(parent_change[j], order.at[j % 2])
        parent_half[j] = dot(
            ordered, cat([held_parents[j, c] for c in range(parents.shape[1])], 1)
        ).astype(BF16)


def couple(middle, partner, lanes_low):
    full = dot_t(middle, cat([partner, partner], 0))
    count = full.shape[0] // 2
    return jnp.where(lanes_low, full[:count], full[count:])


def write_rows(out, at, order, links, count):
    for m in range(count):
        out[at, :, m * 128 : m * 128 + 128] = order[8 * m : 8 * m + links, :].astype(BF16)


def leaf_couple(devs, slots, middle, *rest):
    chips = (len(rest) - 4) // 2
    near, far = rest[:chips], rest[chips : 2 * chips]
    out, held, order, sems = rest[2 * chips :]
    count, links = out.shape[0], out.shape[1]
    half = count // 2
    rank = middle.shape[1]
    index = lax.axis_index("sub")
    member, chip = index % 2, index // 2
    copies = []
    for m in range(chips):
        for side, source in ((0, near[m]), (1, far[m])):
            copies.append(
                pltpu.make_async_copy(source, held.at[2 * m + side], sems.at[2 * m + side])
            )
    for copy in copies:
        copy.start()
    for copy in copies:
        copy.wait()
    low = lax.broadcasted_iota(jnp.int32, (rank // 2, 2 * rank), 1) < rank

    @pl.loop(0, count)
    def _(t):
        for c in range(links):
            dev, slot = devs[t, c], slots[t, c]
            side = jnp.where(slot >= half, 1, 0)
            place = slot - side * half
            box = ((dev // 2) ^ chip) * 2 + (side ^ member)
            partner = held[box, (dev % 2) ^ side, place]
            order[pl.ds(c, rank // 2, stride=8), :] = couple(
                middle[t, :, c * 128 : c * 128 + 128], partner, low
            )
        write_rows(out, t, order, links, rank // 2)


def parent_couple(groups, slots, middle, *rest):
    boxes = len(rest) - 2
    held = rest[:boxes]
    out, order = rest[boxes:]
    count, links = out.shape[0], out.shape[1]
    rank = middle.shape[1]
    mine = lax.axis_index("grp")
    low = lax.broadcasted_iota(jnp.int32, (rank // 2, 2 * rank), 1) < rank
    for p in range(count):
        for c in range(links):
            box = groups[p, c] ^ mine
            slot = slots[p, c]
            partner = held[0][slot]
            for m in range(1, boxes):
                partner = jnp.where(box == m, held[m][slot], partner)
            order[p % 2, pl.ds(c, rank // 2, stride=8), :] = couple(
                middle[p, :, c * 128 : c * 128 + 128], partner, low
            )
        write_rows(out, p, order.at[p % 2], links, rank // 2)


VMEM = pl.BlockSpec(memory_space=pltpu.VMEM)
ANY = pl.BlockSpec(memory_space=pl.ANY)
SMEM = pl.BlockSpec(memory_space=pltpu.SMEM)


def call(body, ins, out_shapes, scratch, name, mib, flops, moved):
    many = isinstance(out_shapes, list)
    return pl.pallas_call(
        body,
        out_shape=out_shapes,
        in_specs=ins,
        out_specs=[VMEM] * len(out_shapes) if many else VMEM,
        scratch_shapes=scratch,
        name=name,
        compiler_params=pltpu.CompilerParams(vmem_limit_bytes=mib * MIB),
        cost_estimate=pl.CostEstimate(flops=flops, bytes_accessed=moved, transcendentals=0),
    )


def swap(block, axis, mask):
    count = lax.axis_size(axis)
    return lax.ppermute(block, axis, [(i, i ^ mask) for i in range(count)])


def shards(
    leaf_bases,
    leaf_transfers,
    leaf_blocks,
    leaf_partner_dev,
    leaf_partner_slot,
    parent_blocks,
    parent_partner_group,
    parent_partner_slot,
    leaf_start,
    parent_start,
):
    count, links, old = leaf_blocks.shape[:3]
    half, parent_links = parent_blocks.shape[:2]
    rank = leaf_start.shape[0]
    points = leaf_bases.shape[1]
    chips = lax.axis_size("sub") // 2
    groups = lax.axis_size("grp")
    member = lax.axis_index("sub") % 2
    shape = jax.ShapeDtypeStruct
    dma = pltpu.SemaphoreType.DMA
    square = half * old * old

    moved = lax.dynamic_slice_in_dim(leaf_transfers, (1 - member) * half, half, 0)
    other_transfers = swap(moved, "sub", 1)
    sent = call(
        sent_weights, [ANY], shape((half, old, old), F32),
        [pltpu.VMEM((half, links, old, old), BF16), dma((half,))],
        "sent_weights", 8, 2 * links * square * old, 2 * links * square,
    )(leaf_blocks)
    other = swap(sent, "sub", 1)
    own, parent_weight = call(
        kept_weights, [ANY, ANY], [shape((half, old, old), F32), shape((half, old, old), F32)],
        [
            pltpu.VMEM((half, links, old, old), BF16),
            pltpu.VMEM((half, parent_links, old, old), BF16),
            dma((2 * half,)),
        ],
        "kept_weights", 12, 2 * (links + parent_links) * square * old, 8 * links * square,
    )(leaf_blocks, parent_blocks)
    tables = [
        pltpu.VMEM((8 * rank, 2 * rank), F32),
        pltpu.VMEM((8 * rank, 2 * rank), F32),
        pltpu.VMEM((half, 2 * rank, old), F32),
    ]
    change, stacked = call(
        leaf_step, [VMEM] * 6,
        [shape((2, half, rank, old), BF16), shape((half, 2, rank, old), F32)],
        tables, "leaf_step", 12, 40 * square * old, 8 * square,
    )(own, other, parent_weight, leaf_transfers, other_transfers, leaf_start)

    near = [change]
    far = [swap(change, "sub", 1)]
    for m in range(1, chips):
        near.append(swap(change, "sub", 2 * m))
    parent_change = call(
        parent_step, [VMEM] * 3, shape((half, rank, old), BF16),
        tables, "parent_step", 12, 20 * square * old, 8 * square,
    )(parent_weight, stacked, parent_start)
    for m in range(1, chips):
        far.append(swap(near[m], "sub", 1))
    parents_held = [parent_change]
    for m in range(1, groups):
        parents_held.append(swap(parent_change, "grp", m))
    new_leaf_bases, leaf_half, parent_half = call(
        middle_step, [VMEM] * 3 + [ANY] * 3,
        [
            shape((count, rank, points), BF16),
            shape((count, rank, links * old), BF16),
            shape((half, rank, parent_links * old), BF16),
        ],
        [
            pltpu.VMEM((count, points, old), BF16),
            pltpu.VMEM((count, links, old, old), BF16),
            pltpu.VMEM((half, parent_links, old, old), BF16),
            pltpu.VMEM((2, rank, old), F32),
            dma((2 * count + 1,)),
        ],
        "middle_step", 16, 20 * square * old, 12 * links * square,
    )(change, far[0], parent_change, leaf_bases, leaf_blocks, parent_blocks)
    new_leaf_blocks = call(
        leaf_couple, [SMEM, SMEM, VMEM] + [ANY] * (2 * chips),
        shape((count, links, rank * rank), BF16),
        [
            pltpu.VMEM((2 * chips, 2, half, rank, old), BF16),
            pltpu.VMEM((4 * rank, 2 * rank), F32),
            dma((2 * chips,)),
        ],
        "leaf_couple", 16, 12 * square * old, 12 * square,
    )(leaf_partner_dev, leaf_partner_slot, leaf_half, *near, *far)
    new_parent_blocks = call(
        parent_couple, [SMEM, SMEM, VMEM] + [VMEM] * groups,
        shape((half, parent_links, rank * rank), BF16),
        [pltpu.VMEM((2, 4 * rank, 2 * rank), F32)],
        "parent_couple", 16, 4 * square * old, 4 * square,
    )(parent_partner_group, parent_partner_slot, parent_half, *parents_held)
    return (new_leaf_bases, new_leaf_blocks, new_parent_blocks)


def solution(mesh):
    first = ("grp", "sub")
    placed = (
        P(first, None, None),
        P(first, None, None),
        P(first, None, None, None),
        P(first, None),
        P(first, None),
        P(first, None, None, None),
        P(first, None),
        P(first, None),
        P(),
        P(),
    )
    return jax.shard_map(
        shards,
        mesh=mesh,
        in_specs=placed,
        out_specs=(P(first, None, None),) * 3,
        check_vma=False,
    )
```

time: 279 us -> 72.5 us (0.26)
  other arithmetic: 209 us -> 0 us
  Pallas kernels: 0 us -> 48.3 us
  matrix products: 24.7 us -> 0 us
  blocking collectives: 16.4 us -> 0 us
  between operations: 14.4 us -> 0.81 us
  starting transfers between devices: 0.68 us -> 14.1 us
  local copies, waits for them, and re-layouts: 13.3 us -> 6.08 us
  waiting for transfers between devices: 0.03 us -> 2.85 us
    another operation x12 -> x0, other arithmetic: 203 us -> none  [the longest x7 109 us: subspace(): factor = jnp.linalg.cholesky(cross_gram)]
    pallas_call x0 -> x7, Pallas kernels: none -> 48.3 us  [the longest x1 12.5 us: shards(): call(leaf_step, [VMEM] * 6, [shape((2, half, rank, old), BF16), shape((ha...]
    dot_general x17 -> x0, matrix products: 21.5 us -> none  [the longest x1 3.38 us: shards(): jnp.einsum('jcrl,jcsl->jcrs', leaf_midpoint, distant_site, preferred_elem...]
    all_gather x1 -> x0, blocking collectives: 16.4 us -> none  [shards(): everyone_parents = lax.all_gather(parent_change, 'grp', axis=0, tiled=True)]
    ppermute x2 -> x12, starting transfers between devices: 0.64 us -> 14.1 us  [swap(): return lax.ppermute(block, axis, [(i, i ^ mask) for i in range(count)])]
    reshape x4 -> x0, local copies, waits for them, and re-layouts: 5.49 us -> none  [the longest x1 2.9 us: shards(): new_leaf_blocks.reshape(leaf_count, leaf_links, rank_new * rank_new)]
    unnamed x26 -> x28, local copies, waits for them, and re-layouts: 0.07 us -> 5.07 us
    gather x2 -> x0, local copies, waits for them, and re-layouts: 4.78 us -> none  [the longest x1 3.34 us: shards(): everyone[(leaf_partner_dev * leaf_count + leaf_partner_slot).reshape(-1)]]
  transfers between devices with their start and end apart: 3 -> 12, of which waited for: 0 -> 1; matrix products, arithmetic and copies ran while one was open for 32% -> 4% of each run, Pallas kernels for 0% -> 36%
where the time goes in v1:
time: 72.5 us; the launch traced here: 72.1 us
  Pallas kernels  48.3 us (67%)
  starting transfers between devices  14.1 us (19%)
  local copies, waits for them, and re-layouts  6.08 us (8%)
  waiting for transfers between devices  2.85 us (4%)
  between operations  0.81 us (1%)
    ppermute x12, starting transfers between devices, swap(): return lax.ppermute(block, axis, [(i, i ^ mask) for i in range(count)])  14.1 us
    pallas_call x1, Pallas kernels, shards(): call(leaf_step, [VMEM] * 6, [shape((2, half, rank, old), BF16), shape((ha...  12.5 us
    pallas_call x1, Pallas kernels, shards(): call(parent_step, [VMEM] * 3, shape((half, rank, old), BF16), tables, 'pa...  9.54 us
    pallas_call x1, Pallas kernels, shards(): call(middle_step, [VMEM] * 3 + [ANY] * 3, [shape((count, rank, points), B...  9.25 us
    pallas_call x1, Pallas kernels, shards(): call(leaf_couple, [SMEM, SMEM, VMEM] + [ANY] * (2 * chips), shape((count,...  6.73 us
    unnamed x28, local copies, waits for them, and re-layouts  5.07 us
    pallas_call x1, Pallas kernels, shards(): call(kept_weights, [ANY, ANY], [shape((half, old, old), F32), shape((half...  5.02 us
    pallas_call x1, Pallas kernels, shards(): call(sent_weights, [ANY], shape((half, old, old), F32), [pltpu.VMEM((half...  3.05 us
  transfers between devices with their start and end apart: 12, of which 1 were waited for; matrix products, arithmetic and copies ran while one was open for 4% of the time, Pallas kernels for 36%

profile of v1, /device:TPU:0, one launch (start us, length us, event | category | flops | bytes accessed | tf_op | source)
XLA Modules:
  0.0 72.1 jit_solution(6813606532012401995)
XLA Ops:
  0.6 0.0 copy-start
  0.6 1.7 %copy-done = bf16[12,6,128,128]{3,2,1,0:T(8,128)(2,1)S(1)} copy-done((bf16[12,6,128,128]{3,2,1,0:T(8,128)(2,1)S(1)}, bf16[12,6,128,128]{3,2,1,0:T(8,128)(2,1)}, u32[]{:S(2)}) %copy-start) | copy-done | bytes 2359320
  2.3 3.0 %sent_weights.1 = f32[6,128,128]{2,1,0:T(8,128)S(1)} custom-call(bf16[12,6,128,128]{3,2,1,0:T(8,128)(2,1)S(1)} %copy-done), custom_call_target="tpu_custom_call" | custom-call | flops 150994944 | bytes 1179648 | tf_op jit(solution)/shard_map/sent_weights/pallas_call | solution.py:366
  5.4 0.0 copy-start.7
  5.4 0.5 collective-permute-start
  5.9 1.0 %constant_dynamic-slice_fusion = bf16[6,128,128]{2,1,0:T(8,128)(2,1)S(1)} fusion(bf16[12,128,128]{2,1,0:T(8,128)(2,1)} %transfers.1, s32[]{:T(128)S(6)} %select_n.11), kind=kLoop, calls=%fused_computation | loop fusion | bytes 393220 | tf_op jit(solution)/shard_map/dynamic_slice | solution.py:364
  6.9 0.0 copy-start.8
  6.9 0.0 copy-start.10
  6.9 0.0 copy-start.11
  6.9 0.0 copy-start.9
  7.0 0.1 collective-permute-start.1
  7.1 0.0 copy-done.1
  7.1 0.0 copy-done.2
  7.1 5.0 %kept_weights.1 = (f32[6,128,128]{2,1,0:T(8,128)S(1)}, f32[6,128,128]{2,1,0:T(8,128)S(1)}) custom-call(bf16[12,6,128,128]{3,2,1,0:T(8,128)(2,1)S(1)} %copy-done.1, bf16[6,3,128,128]{3,2,1,0:T(8,128)(2,1)S(1)} %copy-done.2), custom_call_target="tpu_custom_call" | custom-call | flops 226492416 | bytes 4718592 | tf_op jit(solution)/shard_map/kept_weights/pallas_call | solution.py:372
  12.1 0.0 collective-permute-done.1.other_transfers
  12.1 0.0 collective-permute-done.other
  12.2 12.5 %leaf_step.1 = (bf16[2,6,64,128]{3,2,1,0:T(8,128)(2,1)S(1)}, f32[6,2,64,128]{3,2,1,0:T(8,128)S(1)}) custom-call(f32[6,128,128]{2,1,0:T(8,128)S(1)} %get-tuple-element.10.own, f32[6,128,128]{2,1,0:T(8,128)} %collective-permute-done.other, f32[6,128,128]{2,1,0:T(8,128)S(1)} %get-tuple-element.11.parent, bf16[12,128,128]{2,1,0:T(8,128)(2,1)S(1)} %copy-done.4, ...), custom_call_target="tpu_custom_call" | custom-call | flops 503316480 | bytes 786432 | tf_op jit(solution)/shard_map/leaf_step/pallas_call | solution.py:386
  24.7 3.9 %collective-permute-start.5 = (bf16[2,6,64,128]{3,2,1,0:T(8,128)(2,1)S(1)}, bf16[2,6,64,128]{3,2,1,0:T(8,128)(2,1)}, u32[]{:S(2)}, u32[]{:S(2)}) collective-permute-start(bf16[2,6,64,128]{3,2,1,0:T(8,128)(2,1)S(1)} %get-tuple-element.12.change.rest_0_), channel_id=1, source_target_pairs={{0,6},{1,7},{2,4},{3,5},{4,2},{5,3},{6,0},{7,1},{8,14},{9,15},{10,... | collective-permute-start | bytes 589832 | tf_op jit(solution)/shard_map/ppermute | solution.py:338
  28.6 0.5 collective-permute-start.4
  29.1 0.1 collective-permute-start.3
  29.2 0.0 collective-permute-start.2
  29.2 0.0 copy-done.8
  29.2 9.5 %parent_step.1.parent_change.rest_0_ = bf16[6,64,128]{2,1,0:T(8,128)(2,1)S(1)} custom-call(f32[6,128,128]{2,1,0:T(8,128)S(1)} %get-tuple-element.11.parent, f32[6,2,64,128]{3,2,1,0:T(8,128)S(1)} %get-tuple-element.13.stacked, f32[64,128]{1,0:T(8,128)S(1)} %copy-done.8), custom_call_target="tpu_custom_call" | custom-call | flops 251658240 | bytes 786432 | tf_op jit(solution)/shard_map/parent_step/pallas_call | solution.py:396
  38.8 4.1 %collective-permute-start.11 = (bf16[6,64,128]{2,1,0:T(8,128)(2,1)S(1)}, bf16[6,64,128]{2,1,0:T(8,128)(2,1)S(1)}, u32[]{:S(2)}, u32[]{:S(2)}) collective-permute-start(bf16[6,64,128]{2,1,0:T(8,128)(2,1)S(1)} %parent_step.1.parent_change.rest_0_), channel_id=1, source_target_pairs={{0,24},{8,16},{16,8},{24,0},{1,25},{9,17},{17,9},{25,1},{2,26},{10... | collective-permute-start | bytes 294920 | tf_op jit(solution)/shard_map/ppermute | solution.py:338
  42.9 0.0 collective-permute-done.5.rest_3_
  42.9 0.2 collective-permute-start.8
  43.1 0.0 collective-permute-done.4.rest_2_
  43.1 0.3 collective-permute-start.7
  43.4 0.0 collective-permute-done.3.rest_1_
  43.4 0.2 collective-permute-start.6
  43.6 2.8 %collective-permute-done.11.rest_3_ = bf16[6,64,128]{2,1,0:T(8,128)(2,1)S(1)} collective-permute-done((bf16[6,64,128]{2,1,0:T(8,128)(2,1)S(1)}, bf16[6,64,128]{2,1,0:T(8,128)(2,1)S(1)}, u32[]{:S(2)}, u32[]{:S(2)}) %collective-permute-start.11) | collective-permute-done | bytes 98336 | tf_op jit(solution)/shard_map/ppermute | solution.py:338
  46.4 2.7 %collective-permute-start.10 = (bf16[6,64,128]{2,1,0:T(8,128)(2,1)S(1)}, bf16[6,64,128]{2,1,0:T(8,128)(2,1)}, u32[]{:S(2)}, u32[]{:S(2)}) collective-permute-start(bf16[6,64,128]{2,1,0:T(8,128)(2,1)S(1)} %parent_step.1.parent_change.rest_0_), channel_id=1, source_target_pairs={{0,16},{8,24},{16,0},{24,8},{1,17},{9,25},{17,1},{25,9},{2,18},{10... | collective-permute-start | bytes 294920 | tf_op jit(solution)/shard_map/ppermute | solution.py:338
  49.2 0.0 collective-permute-done.2.swapped.rest_4_
  49.2 1.4 %collective-permute-start.9 = (bf16[6,64,128]{2,1,0:T(8,128)(2,1)S(1)}, bf16[6,64,128]{2,1,0:T(8,128)(2,1)}, u32[]{:S(2)}, u32[]{:S(2)}) collective-permute-start(bf16[6,64,128]{2,1,0:T(8,128)(2,1)S(1)} %parent_step.1.parent_change.rest_0_), channel_id=1, source_target_pairs={{0,8},{8,0},{16,24},{24,16},{1,9},{9,1},{17,25},{25,17},{2,10},{10... | collective-permute-start | bytes 294920 | tf_op jit(solution)/shard_map/ppermute | solution.py:338
  50.6 0.7 copy.15.groups
  51.2 0.7 copy.16.slots
  51.9 0.0 copy-done.9
  51.9 0.1 copy.13.devs
  52.0 0.8 %copy.14.slots = s32[12,6]{1,0:T(8,128)S(1)} copy(s32[12,6]{0,1:T(8,128)} %param.14) | data formatting | bytes 576 | tf_op args[4]
  52.8 1.1 %copy-done.3 = bf16[12,256,128]{2,1,0:T(8,128)(2,1)S(1)} copy-done((bf16[12,256,128]{2,1,0:T(8,128)(2,1)S(1)}, bf16[12,256,128]{2,1,0:T(8,128)(2,1)}, u32[]{:S(2)}) %copy-start.3) | copy-done | bytes 786456
  53.9 9.3 %middle_step.1 = (bf16[12,64,256]{2,1,0:T(8,128)(2,1)}, bf16[12,64,768]{2,1,0:T(8,128)(2,1)S(1)}, bf16[6,64,384]{2,1,0:T(8,128)(2,1)S(1)}) custom-call(bf16[2,6,64,128]{3,2,1,0:T(8,128)(2,1)S(1)} %get-tuple-element.12.change.rest_0_, bf16[2,6,64,128]{3,2,1,0:T(8,128)(2,1)S(1)} %collective-permute-done.2.swapped.rest_4_, ...), custom_call_target="tpu_custom_call" | custom-call | flops 251658240 | bytes 7077888 | tf_op jit(solution)/shard_map/middle_step/pallas_call | solution.py:405
  63.2 0.0 collective-permute-done.10.rest_2_
  63.2 0.0 collective-permute-done.9.rest_1_
  63.2 2.2 %parent_couple.1 = bf16[6,3,4096]{2,1,0:T(4,128)(2,1)} custom-call(s32[6,3]{1,0:T(8,128)S(1)} %copy-done.5, s32[6,3]{1,0:T(8,128)S(1)} %copy-done.6, bf16[6,64,384]{2,1,0:T(8,128)(2,1)S(1)} %get-tuple-element.16.middle, bf16[6,64,128]{2,1,0:T(8,128)(2,1)S(1)} %parent_step.1.parent_change.rest_0_, bf16[6,64,128]{2,1,0:T(8,128)(2,1)} %collective-permute-done.9.rest_1_, ...), custom_call_target="tpu_custom_call" | custom-call | flops 50331648 | bytes 393216 | tf_op jit(solution)/shard_map/parent_couple/pallas_call | solution.py:431
  65.4 0.0 collective-permute-done.8.rest_7_
  65.4 0.0 collective-permute-done.7.rest_6_
  65.4 0.0 collective-permute-done.6.rest_5_
  65.4 6.7 %leaf_couple.1 = bf16[12,6,4096]{2,1,0:T(8,128)(2,1)} custom-call(s32[12,6]{1,0:T(8,128)S(1)} %copy.13.devs, s32[12,6]{1,0:T(8,128)S(1)} %copy.14.slots, bf16[12,64,768]{2,1,0:T(8,128)(2,1)S(1)} %get-tuple-element.15.middle, bf16[2,6,64,128]{3,2,1,0:T(8,128)(2,1)S(1)} %get-tuple-element.12.change.rest_0_, ...), custom_call_target="tpu_custom_call" | custom-call | flops 150994944 | bytes 1179648 | tf_op jit(solution)/shard_map/leaf_couple/pallas_call | solution.py:421
  (12 shorter events, 0.0 us)
Async XLA Ops:
  0.6 1.7 %copy-start = (bf16[12,6,128,128]{3,2,1,0:T(8,128)(2,1)S(1)}, bf16[12,6,128,128]{3,2,1,0:T(8,128)(2,1)}, u32[]{:S(2)}) copy-start(bf16[12,6,128,128]{3,2,1,0:T(8,128)(2,1)} %blocks.5) | copy-start | bytes 7077892
  2.3 4.8 %copy-start.1 = (bf16[12,6,128,128]{3,2,1,0:T(8,128)(2,1)S(1)}, bf16[12,6,128,128]{3,2,1,0:T(8,128)(2,1)}, u32[]{:S(2)}) copy-start(bf16[12,6,128,128]{3,2,1,0:T(8,128)(2,1)} %blocks.5) | copy-start | bytes 7077892
  2.3 4.8 %copy-start.2 = (bf16[6,3,128,128]{3,2,1,0:T(8,128)(2,1)S(1)}, bf16[6,3,128,128]{3,2,1,0:T(8,128)(2,1)}, u32[]{:S(2)}) copy-start(bf16[6,3,128,128]{3,2,1,0:T(8,128)(2,1)} %parents.3) | copy-start | bytes 1769476
  5.4 6.8 %copy-start.7 = (f32[64,128]{1,0:T(8,128)S(1)}, f32[64,128]{1,0:T(8,128)}, u32[]{:S(2)}) copy-start(f32[64,128]{1,0:T(8,128)} %start.2) | copy-start | bytes 98308
  5.4 6.8 %collective-permute-start = (f32[6,128,128]{2,1,0:T(8,128)S(1)}, f32[6,128,128]{2,1,0:T(8,128)}, u32[]{:S(2)}, u32[]{:S(2)}) collective-permute-start(f32[6,128,128]{2,1,0:T(8,128)S(1)} %sent_weights.1), channel_id=1, source_target_pairs={{0,1},{1,0},{2,3},{3,2},{4,5},{5,4},{6,7},{7,6},{8,9},{9,8},{10,11... | collective-permute-start | bytes 1179656 | tf_op jit(solution)/shard_map/ppermute | solution.py:338
  5.9 6.3 %copy-start.4 = (bf16[12,128,128]{2,1,0:T(8,128)(2,1)S(1)}, bf16[12,128,128]{2,1,0:T(8,128)(2,1)}, u32[]{:S(2)}) copy-start(bf16[12,128,128]{2,1,0:T(8,128)(2,1)} %transfers.1) | copy-start | bytes 1179652
  6.9 22.3 %copy-start.8 = (f32[64,128]{1,0:T(8,128)S(1)}, f32[64,128]{1,0:T(8,128)}, u32[]{:S(2)}) copy-start(f32[64,128]{1,0:T(8,128)} %start.3) | copy-start | bytes 98308
  6.9 43.6 %copy-start.10 = (s32[6,3]{0,1:T(4,128)S(1)}, s32[6,3]{0,1:T(4,128)}, u32[]{:S(2)}) copy-start(s32[6,3]{0,1:T(4,128)} %param.16) | copy-start | bytes 220
  6.9 44.3 %copy-start.11 = (s32[6,3]{0,1:T(4,128)S(1)}, s32[6,3]{0,1:T(4,128)}, u32[]{:S(2)}) copy-start(s32[6,3]{0,1:T(4,128)} %param.17) | copy-start | bytes 220
  6.9 45.0 %copy-start.9 = (s32[12,6]{0,1:T(8,128)S(1)}, s32[12,6]{0,1:T(8,128)}, u32[]{:S(2)}) copy-start(s32[12,6]{0,1:T(8,128)} %param.13) | copy-start | bytes 868
  7.0 5.2 %collective-permute-start.1 = (bf16[6,128,128]{2,1,0:T(8,128)(2,1)S(1)}, bf16[6,128,128]{2,1,0:T(8,128)(2,1)S(1)}, u32[]{:S(2)}, u32[]{:S(2)}) collective-permute-start(bf16[6,128,128]{2,1,0:T(8,128)(2,1)S(1)} %constant_dynamic-slice_fusion), channel_id=1, source_target_pairs={{0,1},{1,0},{2,3},{3,2},{4,5},{5,4},{6,7},{7,6},{8,9},{9,8},{10,11... | collective-permute-start | bytes 589832 | tf_op jit(solution)/shard_map/ppermute | solution.py:338
  24.7 18.2 %collective-permute-start.5 = (bf16[2,6,64,128]{3,2,1,0:T(8,128)(2,1)S(1)}, bf16[2,6,64,128]{3,2,1,0:T(8,128)(2,1)}, u32[]{:S(2)}, u32[]{:S(2)}) collective-permute-start(bf16[2,6,64,128]{3,2,1,0:T(8,128)(2,1)S(1)} %get-tuple-element.12.change.rest_0_), channel_id=1, source_target_pairs={{0,6},{1,7},{2,4},{3,5},{4,2},{5,3},{6,0},{7,1},{8,14},{9,15},{10,... | collective-permute-start | bytes 589832 | tf_op jit(solution)/shard_map/ppermute | solution.py:338
  28.6 14.5 %collective-permute-start.4 = (bf16[2,6,64,128]{3,2,1,0:T(8,128)(2,1)S(1)}, bf16[2,6,64,128]{3,2,1,0:T(8,128)(2,1)}, u32[]{:S(2)}, u32[]{:S(2)}) collective-permute-start(bf16[2,6,64,128]{3,2,1,0:T(8,128)(2,1)S(1)} %get-tuple-element.12.change.rest_0_), channel_id=1, source_target_pairs={{0,4},{1,5},{2,6},{3,7},{4,0},{5,1},{6,2},{7,3},{8,12},{9,13},{10,... | collective-permute-start | bytes 589832 | tf_op jit(solution)/shard_map/ppermute | solution.py:338
  29.1 14.3 %collective-permute-start.3 = (bf16[2,6,64,128]{3,2,1,0:T(8,128)(2,1)S(1)}, bf16[2,6,64,128]{3,2,1,0:T(8,128)(2,1)}, u32[]{:S(2)}, u32[]{:S(2)}) collective-permute-start(bf16[2,6,64,128]{3,2,1,0:T(8,128)(2,1)S(1)} %get-tuple-element.12.change.rest_0_), channel_id=1, source_target_pairs={{0,2},{1,3},{2,0},{3,1},{4,6},{5,7},{6,4},{7,5},{8,10},{9,11},{10,... | collective-permute-start | bytes 589832 | tf_op jit(solution)/shard_map/ppermute | solution.py:338
  29.2 19.9 %collective-permute-start.2 = (bf16[2,6,64,128]{3,2,1,0:T(8,128)(2,1)S(1)}, bf16[2,6,64,128]{3,2,1,0:T(8,128)(2,1)S(1)}, u32[]{:S(2)}, u32[]{:S(2)}) collective-permute-start(bf16[2,6,64,128]{3,2,1,0:T(8,128)(2,1)S(1)} %get-tuple-element.12.change.rest_0_), channel_id=1, source_target_pairs={{0,1},{1,0},{2,3},{3,2},{4,5},{5,4},{6,7},{7,6},{8,9},{9,8},{10,11... | collective-permute-start | bytes 589832 | tf_op jit(solution)/shard_map/ppermute | solution.py:338
  38.8 7.6 %collective-permute-start.11 = (bf16[6,64,128]{2,1,0:T(8,128)(2,1)S(1)}, bf16[6,64,128]{2,1,0:T(8,128)(2,1)S(1)}, u32[]{:S(2)}, u32[]{:S(2)}) collective-permute-start(bf16[6,64,128]{2,1,0:T(8,128)(2,1)S(1)} %parent_step.1.parent_change.rest_0_), channel_id=1, source_target_pairs={{0,24},{8,16},{16,8},{24,0},{1,25},{9,17},{17,9},{25,1},{2,26},{10... | collective-permute-start | bytes 294920 | tf_op jit(solution)/shard_map/ppermute | solution.py:338
  42.9 22.5 %collective-permute-start.8 = (bf16[2,6,64,128]{3,2,1,0:T(8,128)(2,1)}, bf16[2,6,64,128]{3,2,1,0:T(8,128)(2,1)}, u32[]{:S(2)}, u32[]{:S(2)}) collective-permute-start(bf16[2,6,64,128]{3,2,1,0:T(8,128)(2,1)} %collective-permute-done.5.rest_3_), channel_id=1, source_target_pairs={{0,1},{1,0},{2,3},{3,2},{4,5},{5,4},{6,7},{7,6},{8,9},{9,8},{10,11... | collective-permute-start | bytes 589832 | tf_op jit(solution)/shard_map/ppermute | solution.py:338
  43.1 22.3 %collective-permute-start.7 = (bf16[2,6,64,128]{3,2,1,0:T(8,128)(2,1)}, bf16[2,6,64,128]{3,2,1,0:T(8,128)(2,1)}, u32[]{:S(2)}, u32[]{:S(2)}) collective-permute-start(bf16[2,6,64,128]{3,2,1,0:T(8,128)(2,1)} %collective-permute-done.4.rest_2_), channel_id=1, source_target_pairs={{0,1},{1,0},{2,3},{3,2},{4,5},{5,4},{6,7},{7,6},{8,9},{9,8},{10,11... | collective-permute-start | bytes 589832 | tf_op jit(solution)/shard_map/ppermute | solution.py:338
  43.4 22.0 %collective-permute-start.6 = (bf16[2,6,64,128]{3,2,1,0:T(8,128)(2,1)}, bf16[2,6,64,128]{3,2,1,0:T(8,128)(2,1)}, u32[]{:S(2)}, u32[]{:S(2)}) collective-permute-start(bf16[2,6,64,128]{3,2,1,0:T(8,128)(2,1)} %collective-permute-done.3.rest_1_), channel_id=1, source_target_pairs={{0,1},{1,0},{2,3},{3,2},{4,5},{5,4},{6,7},{7,6},{8,9},{9,8},{10,11... | collective-permute-start | bytes 589832 | tf_op jit(solution)/shard_map/ppermute | solution.py:338
  46.4 16.7 %collective-permute-start.10 = (bf16[6,64,128]{2,1,0:T(8,128)(2,1)S(1)}, bf16[6,64,128]{2,1,0:T(8,128)(2,1)}, u32[]{:S(2)}, u32[]{:S(2)}) collective-permute-start(bf16[6,64,128]{2,1,0:T(8,128)(2,1)S(1)} %parent_step.1.parent_change.rest_0_), channel_id=1, source_target_pairs={{0,16},{8,24},{16,0},{24,8},{1,17},{9,25},{17,1},{25,9},{2,18},{10... | collective-permute-start | bytes 294920 | tf_op jit(solution)/shard_map/ppermute | solution.py:338
  49.2 14.0 %collective-permute-start.9 = (bf16[6,64,128]{2,1,0:T(8,128)(2,1)S(1)}, bf16[6,64,128]{2,1,0:T(8,128)(2,1)}, u32[]{:S(2)}, u32[]{:S(2)}) collective-permute-start(bf16[6,64,128]{2,1,0:T(8,128)(2,1)S(1)} %parent_step.1.parent_change.rest_0_), channel_id=1, source_target_pairs={{0,8},{8,0},{16,24},{24,16},{1,9},{9,1},{17,25},{25,17},{2,10},{10... | collective-permute-start | bytes 294920 | tf_op jit(solution)/shard_map/ppermute | solution.py:338
  52.8 1.1 %copy-start.3 = (bf16[12,256,128]{2,1,0:T(8,128)(2,1)S(1)}, bf16[12,256,128]{2,1,0:T(8,128)(2,1)}, u32[]{:S(2)}) copy-start(bf16[12,256,128]{2,1,0:T(8,128)(2,1)} %bases.1) | copy-start | bytes 2359300
  53.9 9.3 %copy-start.5 = (s32[6,3]{1,0:T(8,128)S(1)}, s32[6,3]{1,0:T(8,128)}, u32[]{:S(2)}) copy-start(s32[6,3]{1,0:T(8,128)} %copy.15.groups) | copy-start | bytes 220
  53.9 9.3 %copy-start.6 = (s32[6,3]{1,0:T(8,128)S(1)}, s32[6,3]{1,0:T(8,128)}, u32[]{:S(2)}) copy-start(s32[6,3]{1,0:T(8,128)} %copy.16.slots) | copy-start | bytes 220

commit v2 on v1

v2 whole, which is shorter than its diff:
```python
import functools

import jax
import jax.numpy as jnp
from jax import lax
from jax.experimental import pallas as pl
from jax.experimental.pallas import tpu as pltpu
from jax.sharding import PartitionSpec as P

F32 = jnp.float32
BF16 = jnp.bfloat16
PIVOTS = 8
PANEL = 16
MIB = 1 << 20


def cat(parts, axis):
    return jnp.concatenate(parts, axis=axis)


def halves(value):
    high = value.astype(BF16)
    low = (value - high.astype(F32)).astype(BF16)
    return high, low


def dot(left, right):
    return lax.dot_general(left, right, (((1,), (0,)), ((), ())), preferred_element_type=F32)


def dot_t(left, right):
    return lax.dot_general(left, right, (((1,), (1,)), ((), ())), preferred_element_type=F32)


def fold(value):
    width = value.shape[1] // 2
    return value[:, :width] + value[:, width:]


def wide(value):
    return cat(halves(value), 1)


def tall(value):
    both = wide(value)
    return cat([both, both], 0)


def gram_sum(parts):
    row = cat(parts, 1)
    return dot_t(row, row)


def thirds(value):
    high, rest = halves_left(value)
    middle, rest = halves_left(rest)
    return high, middle, rest.astype(BF16)


def halves_left(value):
    high = value.astype(BF16)
    return high, value - high.astype(F32)


def eliminate(grid, made, turned, rank, pairs):
    shape = (8, 128)
    lane = lax.broadcasted_iota(jnp.int32, shape, 1)
    half = jnp.where(lane < rank, 0, rank)
    local = lane - half

    def spread(value, column):
        return jnp.take_along_axis(value, half + column, axis=1)

    for top in range(0, rank, PANEL):
        end = top + PANEL
        panel = [grid[8 * i : 8 * i + 8, :] for i in range(top, end)]
        for first in range(top, end, PIVOTS):
            last = first + PIVOTS
            rows = panel[first - top : last - top]
            corner = [[None] * PIVOTS for _ in range(PIVOTS)]
            for p in range(PIVOTS):
                for q in range(p, PIVOTS):
                    corner[p][q] = spread(rows[p], first + q)
            inside = (local >= first) & (local < last)
            rows = [
                jnp.where(inside, (local == first + p).astype(F32), rows[p])
                for p in range(PIVOTS)
            ]
            inverse = []
            for p in range(PIVOTS):
                inverse.append(1.0 / corner[p][p])
                for q in range(p + 1, PIVOTS):
                    factor = corner[p][q] * inverse[p]
                    for s in range(q, PIVOTS):
                        corner[q][s] = corner[q][s] - factor * corner[p][s]
                    rows[q] = rows[q] - factor * rows[p]
            scaled = [rows[p] * inverse[p] for p in range(PIVOTS)]
            for i in range(last, end):
                row = jnp.where(inside, 0.0, panel[i - top])
                for p in range(PIVOTS):
                    row = row - spread(scaled[p], i) * rows[p]
                panel[i - top] = row
            for p in range(PIVOTS):
                i = first + p
                done = jnp.where(local < last, rows[p] * lax.rsqrt(corner[p][p]), 0.0)
                made[8 * i : 8 * i + 8, :] = done
                if end < rank:
                    kept = rows[p]
                    if last < end:
                        kept = jnp.where((local < last) | (local >= end), kept, 0.0)
                    grid[8 * i : 8 * i + 8, :] = kept
                    at = 8 * (i - top)
                    turned[at : at + 8, :] = scaled[p]
        if end < rank:
            lane_below = lax.broadcasted_iota(jnp.int32, (rank - end, 2 * rank), 1)
            low = lane_below < rank
            local_below = lane_below - jnp.where(low, 0, rank)
            past = (local_below >= top) & (local_below < end)
            for pair in range(pairs):
                a, b, c = thirds(turned[pl.ds(pair, PANEL, stride=8), :])
                x, y, z = thirds(grid[pl.ds(8 * top + pair, PANEL, stride=8), :])
                full = lax.dot_general(
                    cat([a, a, a, b, b, c], 0), cat([x, y, z, x, y, x], 0),
                    (((0,), (0,)), ((), ())), preferred_element_type=F32,
                )
                full = jnp.where(low, full[end:rank], full[rank + end :])
                spot = pl.ds(8 * end + pair, rank - end, stride=8)
                grid[spot, :] = jnp.where(past, 0.0, grid[spot, :]) - full


def pair_rows(made, stored, pair, rank):
    wide_rank = 2 * rank
    factor = wide(made[pl.ds(pair, rank, stride=8), :])
    both = stored[pair]
    zero = jnp.zeros((rank, both.shape[1]), F32)
    spread = cat([cat([both[:rank], zero], 1), cat([zero, both[rank:]], 1)], 0)
    high, low = halves(spread)
    return dot(factor, cat([high, high], 0)) + dot(factor, cat([low, low], 0))


def store_gram(grid, stored, pair, images, rank):
    both = cat(images, 0)
    stored[pair] = both
    both_wide = wide(both)
    high, low = halves(both)
    full = dot_t(both_wide, cat([cat([high, high], 1), cat([low, low], 1)], 0))
    full = fold(full)
    lane = lax.broadcasted_iota(jnp.int32, (rank, 2 * rank), 1)
    grid[pl.ds(pair, rank, stride=8), :] = jnp.where(lane < rank, full[:rank], full[rank:])


def sent_weights(blocks, weight):
    half = weight.shape[0]
    start = (1 - lax.axis_index("sub") % 2) * half
    for j in range(half):
        weight[j] = gram_sum([blocks[start + j, c] for c in range(blocks.shape[1])])


def kept_weights(blocks, parents, weight, parent_weight):
    half = weight.shape[0]
    start = (lax.axis_index("sub") % 2) * half
    for j in range(half):
        weight[j] = gram_sum([blocks[start + j, c] for c in range(blocks.shape[1])])
        parent_weight[j] = gram_sum([parents[j, c] for c in range(parents.shape[1])])


def images_of(starts, weights):
    folded = [tall(weight) for weight in weights]
    images = [fold(dot(starts, each)) for each in folded]
    return [fold(dot(wide(image), each)) for image, each in zip(images, folded)]


def leaf_step(own, other, parent, transfers, other_transfers, start, change, stacked, grid, made, turned, stored):
    rank = start.shape[0]
    half = own.shape[0]
    member = lax.axis_index("sub") % 2
    first = member * half
    moves = [(transfers[first + j], other_transfers[first + j]) for j in range(half)]
    size = parent.shape[1]
    carried = [fold(dot(cat(moves[j], 0), wide(parent[j]))) for j in range(half)]
    weights = []
    for j in range(half):
        for at, base in enumerate((own[j], other[j])):
            part = wide(carried[j][at * size : at * size + size])
            weights.append(base + dot_t(part, cat([moves[j][at]] * 2, 1)))
    images = images_of(wide(start[...]), weights)
    for j in range(half):
        store_gram(grid, stored, j, images[2 * j : 2 * j + 2], rank)
    eliminate(grid, made, turned, rank, half)
    found = [pair_rows(made, stored, j, rank).astype(BF16) for j in range(half)]
    for j in range(half):
        width = found[j].shape[1] // 2
        mine, theirs = found[j][:, :width], found[j][:, width:]
        change[0, j] = mine
        change[1, j] = theirs
        stacked[j, member] = dot(mine, moves[j][0])
        stacked[j, 1 - member] = dot(theirs, moves[j][1])


def parent_step(parent, stacked, start, change, grid, made, turned, stored):
    rank = start.shape[0]
    half = parent.shape[0]
    rows = [cat([stacked[j, 0], stacked[j, 1]], 0) for j in range(half)]
    left = [fold(dot(wide(rows[j]), tall(parent[j]))) for j in range(half)]
    grams = []
    for j in range(half):
        high, low = halves(rows[j])
        right = cat([cat([high, high], 1), cat([low, low], 1)], 0)
        grams.append(fold(dot_t(wide(left[j]), right)))
    images = images_of(wide(start[...]), grams)
    for pair in range(half // 2):
        store_gram(grid, stored, pair, images[2 * pair : 2 * pair + 2], rank)
    eliminate(grid, made, turned, rank, half // 2)
    found = [pair_rows(made, stored, pair, rank) for pair in range(half // 2)]
    for j in range(half):
        width = found[0].shape[1] // 2
        at = j % 2 * width
        mixed = wide(found[j // 2][:, at : at + width])
        rows = tall(cat([stacked[j, 0], stacked[j, 1]], 0))
        change[j] = fold(dot(mixed, rows)).astype(BF16)


def parted(value, scratch):
    scratch[...] = value.astype(F32)
    count = value.shape[0] // 2
    return cat(
        [scratch[pl.ds(0, count, stride=2), :], scratch[pl.ds(1, count, stride=2), :]], 0
    ).astype(BF16)


def middle_step(
    change, swapped, parent_change, bases, blocks, parents, _,
    new_bases, leaf_half, parent_half, token,
    order, order_parents,
):
    token[...] = jnp.zeros(token.shape, token.dtype)
    half, links = parents.shape[0], blocks.shape[1]
    member = lax.axis_index("sub") % 2
    for at in range(2 * half):
        j = at % half
        spot = (member if at < half else 1 - member) * half + j
        rows = change[0, j] if at < half else swapped[1, j]
        ordered = parted(rows, order.at[at % 4])
        new_bases[spot] = dot_t(rows, bases[spot]).astype(BF16)
        leaf_half[spot] = dot(ordered, cat([blocks[spot, c] for c in range(links)], 1)).astype(BF16)
    for j in range(half):
        ordered = parted(parent_change[j], order_parents.at[j % 2])
        parent_half[j] = dot(
            ordered, cat([parents[j, c] for c in range(parents.shape[1])], 1)
        ).astype(BF16)


def pack(*refs):
    *parts, out = refs
    count = parts[0].shape[0]
    for at, part in enumerate(parts):
        out[at * count : at * count + count] = part[...]


def pause(_, token):
    token[...] = jnp.zeros(token.shape, token.dtype)


def couple(middle, partner, lanes_low):
    full = dot_t(middle, cat([partner, partner], 0))
    count = full.shape[0] // 2
    return jnp.where(lanes_low, full[:count], full[count:])


def write_rows(out, at, order, links, count):
    for m in range(count):
        out[at, :, m * 128 : m * 128 + 128] = order[8 * m : 8 * m + links, :].astype(BF16)


def leaf_couple(boxes, devs_in, slots_in, middle, _, *rest):
    held_boxes, (out, token, devs, slots, held, order, sems) = rest[:-7], rest[-7:]
    token[...] = jnp.zeros(token.shape, token.dtype)
    count, links = out.shape[0], out.shape[1]
    half = count // 2
    rank = middle.shape[1]
    index = lax.axis_index("sub")
    member, chip = index % 2, index // 2
    copies = [
        pltpu.make_async_copy(devs_in, devs, sems.at[0]),
        pltpu.make_async_copy(slots_in, slots, sems.at[1]),
    ]
    for copy in copies:
        copy.start()
    for box, source in zip(boxes, held_boxes):
        for at, place in enumerate(box):
            held[place] = source[2 * at : 2 * at + 2]
    for copy in copies:
        copy.wait()
    low = lax.broadcasted_iota(jnp.int32, (rank // 2, 2 * rank), 1) < rank
    for t in range(count):
        for c in range(links):
            dev, slot = devs[c, t], slots[c, t]
            side = jnp.where(slot >= half, 1, 0)
            place = slot - side * half
            box = ((dev // 2) ^ chip) * 2 + (side ^ member)
            partner = held[box, (dev % 2) ^ side, place]
            order[t % 4, pl.ds(c, rank // 2, stride=8), :] = couple(
                middle[t, :, c * 128 : c * 128 + 128], partner, low
            )
        write_rows(out, t, order.at[t % 4], links, rank // 2)


def parent_couple(groups_in, slots_in, middle, _, *rest):
    boxes = len(rest) - 6
    near = rest[:boxes]
    out, groups, slots, held, order, sems = rest[boxes:]
    count, links = out.shape[0], out.shape[1]
    rank = middle.shape[1]
    mine = lax.axis_index("grp")
    copies = [
        pltpu.make_async_copy(groups_in, groups, sems.at[0]),
        pltpu.make_async_copy(slots_in, slots, sems.at[1]),
    ]
    for copy in copies:
        copy.start()
    for m in range(boxes):
        held[m] = near[m][...]
    for copy in copies:
        copy.wait()
    low = lax.broadcasted_iota(jnp.int32, (rank // 2, 2 * rank), 1) < rank
    for p in range(count):
        for c in range(links):
            partner = held[groups[c, p] ^ mine, slots[c, p]]
            order[p % 2, pl.ds(c, rank // 2, stride=8), :] = couple(
                middle[p, :, c * 128 : c * 128 + 128], partner, low
            )
        write_rows(out, p, order.at[p % 2], links, rank // 2)


VMEM = pl.BlockSpec(memory_space=pltpu.VMEM)
ANY = pl.BlockSpec(memory_space=pl.ANY)
HBM = pl.BlockSpec(memory_space=pltpu.HBM)


def call(body, ins, out_shapes, scratch, name, mib, flops, moved):
    many = isinstance(out_shapes, list)
    return pl.pallas_call(
        body,
        out_shape=out_shapes,
        in_specs=ins,
        out_specs=[VMEM] * len(out_shapes) if many else VMEM,
        scratch_shapes=scratch,
        name=name,
        compiler_params=pltpu.CompilerParams(vmem_limit_bytes=mib * MIB),
        cost_estimate=pl.CostEstimate(flops=flops, bytes_accessed=moved, transcendentals=0),
    )


def swap(block, axis, mask):
    count = lax.axis_size(axis)
    return lax.ppermute(block, axis, [(i, i ^ mask) for i in range(count)])


def shards(
    leaf_bases,
    leaf_transfers,
    leaf_blocks,
    leaf_partner_dev,
    leaf_partner_slot,
    parent_blocks,
    parent_partner_group,
    parent_partner_slot,
    leaf_start,
    parent_start,
):
    count, links, old = leaf_blocks.shape[:3]
    half, parent_links = parent_blocks.shape[:2]
    rank = leaf_start.shape[0]
    points = leaf_bases.shape[1]
    chips = lax.axis_size("sub") // 2
    groups = lax.axis_size("grp")
    shape = jax.ShapeDtypeStruct
    dma = pltpu.SemaphoreType.DMA
    square = half * old * old

    weights = shape((half, old, old), F32)
    other_transfers = swap(leaf_transfers, "sub", 1)
    sent = call(
        sent_weights, [VMEM], weights, [],
        "sent_weights", 8, 2 * links * square * old, 2 * links * square,
    )(leaf_blocks)
    other = swap(sent, "sub", 1)
    own, parent_weight = call(
        kept_weights, [VMEM] * 2, [weights, weights], [],
        "kept_weights", 8, 2 * (links + parent_links) * square * old, 8 * links * square,
    )(leaf_blocks, parent_blocks)
    tables = [
        pltpu.VMEM((8 * rank, 2 * rank), F32),
        pltpu.VMEM((8 * rank, 2 * rank), F32),
        pltpu.VMEM((8 * PANEL, 2 * rank), F32),
        pltpu.VMEM((half, 2 * rank, old), F32),
    ]
    change, stacked = call(
        leaf_step, [VMEM] * 6,
        [shape((2, half, rank, old), BF16), shape((half, 2, rank, old), F32)],
        tables, "leaf_step", 8, 40 * square * old, 8 * square,
    )(own, other, parent_weight, leaf_transfers, other_transfers, leaf_start)

    swapped = swap(change, "sub", 1)
    near = [swap(change, "sub", 2 * m) for m in range(1, chips)]
    parent_change = call(
        parent_step, [VMEM] * 3, shape((half, rank, old), BF16),
        tables, "parent_step", 8, 20 * square * old, 8 * square,
    )(parent_weight, stacked, parent_start)
    parents_held = [parent_change] + [
        swap(parent_change, "grp", m) for m in range(1, groups)
    ]
    token = shape((8, 128), F32)
    new_leaf_bases, leaf_half, parent_half, after_middle = call(
        middle_step, [VMEM] * 7,
        [
            shape((count, rank, points), BF16),
            shape((count, rank, links * old), BF16),
            shape((half, rank, parent_links * old), BF16),
            token,
        ],
        [pltpu.VMEM((4, rank, old), F32), pltpu.VMEM((2, rank, old), F32)],
        "middle_step", 8, 20 * square * old, 12 * links * square,
    )(change, swapped, parent_change, leaf_bases, leaf_blocks, parent_blocks, near[0])
    packed = call(
        pack, [VMEM] * (chips - 2), shape((2 * (chips - 2), half, rank, old), BF16), [],
        "pack", 2 + chips, square, square,
    )(*near[1:])
    paused = call(pause, [VMEM], token, [], "pause", 4, 1 << 34, square)(after_middle)
    held = [change, swapped, *near, swap(near[0], "sub", 1), swap(packed, "sub", 1)]
    boxes = [(0,), (1,)] + [(2 * m,) for m in range(1, chips)]
    boxes += [(3,), tuple(2 * m + 1 for m in range(2, chips))]
    table = pltpu.SMEM
    new_leaf_blocks, after_leaves = call(
        functools.partial(leaf_couple, boxes), [ANY, ANY] + [VMEM] * (2 + len(held)),
        [shape((count, links, rank * rank), BF16), token],
        [
            table((links, count), jnp.int32),
            table((links, count), jnp.int32),
            pltpu.VMEM((2 * chips, 2, half, rank, old), BF16),
            pltpu.VMEM((4, 4 * rank, 2 * rank), F32),
            dma((2,)),
        ],
        "leaf_couple", 4 + chips, 1 << 34, 12 * square,
    )(leaf_partner_dev.T, leaf_partner_slot.T, leaf_half, paused, *held)
    new_parent_blocks = call(
        parent_couple, [ANY, ANY] + [VMEM] * (groups + 2),
        shape((half, parent_links, rank * rank), BF16),
        [
            table((parent_links, half), jnp.int32),
            table((parent_links, half), jnp.int32),
            pltpu.VMEM((groups, half, rank, old), BF16),
            pltpu.VMEM((2, 4 * rank, 2 * rank), F32),
            dma((2,)),
        ],
        "parent_couple", 4 + groups, square, 4 * square,
    )(parent_partner_group.T, parent_partner_slot.T, parent_half, after_leaves, *parents_held)
    return (new_leaf_bases, new_leaf_blocks, new_parent_blocks)


def solution(mesh):
    first = ("grp", "sub")
    placed = (
        P(first, None, None),
        P(first, None, None),
        P(first, None, None, None),
        P(first, None),
        P(first, None),
        P(first, None, None, None),
        P(first, None),
        P(first, None),
        P(),
        P(),
    )
    return jax.shard_map(
        shards,
        mesh=mesh,
        in_specs=placed,
        out_specs=(P(first, None, None),) * 3,
        check_vma=False,
    )
```

time: 72.5 us -> 34 us (0.47)
  Pallas kernels: 48.3 us -> 15.3 us
  local copies, waits for them, and re-layouts: 6.08 us -> 2.38 us
  waiting for transfers between devices: 2.85 us -> 0.81 us
    pallas_call x5 -> x7, Pallas kernels: 26.2 us -> 7.47 us  [the longest x1 3.01 us: shards(): call(functools.partial(leaf_couple, boxes), [ANY, ANY] + [VMEM] * (2 + le...]
    pallas_call x1, Pallas kernels: 12.5 us -> 4.13 us  [shards(): call(leaf_step, [VMEM] * 6, [shape((2, half, rank, old), BF16), shape((ha...]
    pallas_call x1, Pallas kernels: 9.54 us -> 3.73 us  [shards(): call(parent_step, [VMEM] * 3, shape((half, rank, old), BF16), tables, 'pa...]
    unnamed x28 -> x22, local copies, waits for them, and re-layouts: 5.07 us -> 2.38 us
    ppermute x12 -> x11, waiting for transfers between devices: 2.85 us -> 0.81 us  [swap(): return lax.ppermute(block, axis, [(i, i ^ mask) for i in range(count)])]
    dynamic_slice x1 -> x0, local copies, waits for them, and re-layouts: 1.01 us -> none  [shards(): lax.dynamic_slice_in_dim(leaf_transfers, (1 - member) * half, half, 0)]
    ppermute x12 -> x11, starting transfers between devices: 14.1 us -> 14.5 us  [swap(): return lax.ppermute(block, axis, [(i, i ^ mask) for i in range(count)])]
  transfers between devices with their start and end apart: 12 -> 11, of which waited for: 1 -> 2; matrix products, arithmetic and copies ran while one was open for 4% -> 0% of each run, Pallas kernels for 36% -> 26%
where the time goes in v2:
time: 34 us; the launch traced here: 33.8 us
  Pallas kernels  15.3 us (45%)
  starting transfers between devices  14.5 us (43%)
  local copies, waits for them, and re-layouts  2.38 us (7%)
  waiting for transfers between devices  0.81 us (2%)
  between operations  0.79 us (2%)
    ppermute x11, starting transfers between devices, swap(): return lax.ppermute(block, axis, [(i, i ^ mask) for i in range(count)])  14.5 us
    pallas_call x1, Pallas kernels, shards(): call(leaf_step, [VMEM] * 6, [shape((2, half, rank, old), BF16), shape((ha...  4.13 us
    pallas_call x1, Pallas kernels, shards(): call(parent_step, [VMEM] * 3, shape((half, rank, old), BF16), tables, 'pa...  3.73 us
    pallas_call x1, Pallas kernels, shards(): call(functools.partial(leaf_couple, boxes), [ANY, ANY] + [VMEM] * (2 + le...  3.01 us
    unnamed x22, local copies, waits for them, and re-layouts  2.38 us
    pallas_call x1, Pallas kernels, shards(): call(parent_couple, [ANY, ANY] + [VMEM] * (groups + 2), shape((half, pare...  1.8 us
    pallas_call x1, Pallas kernels, shards(): call(middle_step, [VMEM] * 7, [shape((count, rank, points), BF16), shape(...  1.49 us
    ppermute x11, waiting for transfers between devices, swap(): return lax.ppermute(block, axis, [(i, i ^ mask) for i in range(count)])  0.81 us
  transfers between devices with their start and end apart: 11, of which 2 were waited for; matrix products, arithmetic and copies ran while one was open for 0% of the time, Pallas kernels for 26%

profile of v2, /device:TPU:0, one launch (start us, length us, event | category | flops | bytes accessed | tf_op | source)
XLA Modules:
  0.0 33.8 jit_solution(3344619003552231802)
XLA Ops:
  0.6 0.0 copy-start
  0.6 1.7 %copy-done = bf16[12,6,128,128]{3,2,1,0:T(8,128)(2,1)S(1)} copy-done((bf16[12,6,128,128]{3,2,1,0:T(8,128)(2,1)S(1)}, bf16[12,6,128,128]{3,2,1,0:T(8,128)(2,1)}, u32[]{:S(2)}) %copy-start) | copy-done | bytes 2359320
  2.3 0.0 copy-start.4
  2.3 0.0 copy-start.2
  2.3 0.0 copy-start.5
  2.3 0.5 %sent_weights.1 = f32[6,128,128]{2,1,0:T(8,128)S(1)} custom-call(bf16[12,6,128,128]{3,2,1,0:T(8,128)(2,1)S(1)} %copy-done), custom_call_target="tpu_custom_call" | custom-call | flops 150994944 | bytes 1179648 | tf_op jit(solution)/shard_map/sent_weights/pallas_call | solution.py:383
  2.8 0.0 copy-start.8
  2.8 0.5 %collective-permute-start = (f32[6,128,128]{2,1,0:T(8,128)S(1)}, f32[6,128,128]{2,1,0:T(8,128)S(1)}, u32[]{:S(2)}, u32[]{:S(2)}) collective-permute-start(f32[6,128,128]{2,1,0:T(8,128)S(1)} %sent_weights.1), channel_id=1, source_target_pairs={{0,1},{1,0},{2,3},{3,2},{4,5},{5,4},{6,7},{7,6},{8,9},{9,8},{10,11... | collective-permute-start | bytes 1179656 | tf_op jit(solution)/shard_map/ppermute | solution.py:356
  3.3 0.0 copy-done.4
  3.3 0.4 %collective-permute-start.1 = (bf16[12,128,128]{2,1,0:T(8,128)(2,1)S(1)}, bf16[12,128,128]{2,1,0:T(8,128)(2,1)S(1)}, u32[]{:S(2)}, u32[]{:S(2)}) collective-permute-start(bf16[12,128,128]{2,1,0:T(8,128)(2,1)S(1)} %copy-done.4), channel_id=1, source_target_pairs={{0,1},{1,0},{2,3},{3,2},{4,5},{5,4},{6,7},{7,6},{8,9},{9,8},{10,11... | collective-permute-start | bytes 1179656 | tf_op jit(solution)/shard_map/ppermute | solution.py:356
  3.7 0.0 copy-done.2
  3.8 0.7 %kept_weights.1 = (f32[6,128,128]{2,1,0:T(8,128)S(1)}, f32[6,128,128]{2,1,0:T(8,128)S(1)}) custom-call(bf16[12,6,128,128]{3,2,1,0:T(8,128)(2,1)S(1)} %copy-done, bf16[6,3,128,128]{3,2,1,0:T(8,128)(2,1)S(1)} %copy-done.2), custom_call_target="tpu_custom_call" | custom-call | flops 226492416 | bytes 4718592 | tf_op jit(solution)/shard_map/kept_weights/pallas_call | solution.py:388
  4.4 0.0 copy-start.1
  4.5 0.0 copy-start.3
  4.5 0.2 collective-permute-done.other
  4.7 0.6 %collective-permute-done.1.other_transfers = bf16[12,128,128]{2,1,0:T(8,128)(2,1)S(1)} collective-permute-done((bf16[12,128,128]{2,1,0:T(8,128)(2,1)S(1)}, bf16[12,128,128]{2,1,0:T(8,128)(2,1)S(1)}, u32[]{:S(2)}, u32[]{:S(2)}) %collective-permute-start.1) | collective-permute-done | bytes 393248 | tf_op jit(solution)/shard_map/ppermute | solution.py:356
  5.2 0.0 copy-done.5
  5.2 4.1 %leaf_step.1 = (bf16[2,6,64,128]{3,2,1,0:T(8,128)(2,1)S(1)}, f32[6,2,64,128]{3,2,1,0:T(8,128)S(1)}) custom-call(f32[6,128,128]{2,1,0:T(8,128)S(1)} %get-tuple-element.13.own, f32[6,128,128]{2,1,0:T(8,128)S(1)} %collective-permute-done.other, f32[6,128,128]{2,1,0:T(8,128)S(1)} %get-tuple-element.14.parent, bf16[12,128,128]{2,1,0:T(8,128)(2,1)S(1)} %copy-done.4, ...), custom_call_target="tpu_custom_call" | custom-call | flops 503316480 | bytes 786432 | tf_op jit(solution)/shard_map/leaf_step/pallas_call | solution.py:398
  9.4 3.0 %collective-permute-start.4 = (bf16[2,6,64,128]{3,2,1,0:T(8,128)(2,1)S(1)}, bf16[2,6,64,128]{3,2,1,0:T(8,128)(2,1)S(1)}, u32[]{:S(2)}, u32[]{:S(2)}) collective-permute-start(bf16[2,6,64,128]{3,2,1,0:T(8,128)(2,1)S(1)} %get-tuple-element.15.change.rest_0_), channel_id=1, source_target_pairs={{0,4},{1,5},{2,6},{3,7},{4,0},{5,1},{6,2},{7,3},{8,12},{9,13},{10,... | collective-permute-start | bytes 589832 | tf_op jit(solution)/shard_map/ppermute | solution.py:356
  12.3 1.4 %collective-permute-start.5 = (bf16[2,6,64,128]{3,2,1,0:T(8,128)(2,1)S(1)}, bf16[2,6,64,128]{3,2,1,0:T(8,128)(2,1)S(1)}, u32[]{:S(2)}, u32[]{:S(2)}) collective-permute-start(bf16[2,6,64,128]{3,2,1,0:T(8,128)(2,1)S(1)} %get-tuple-element.15.change.rest_0_), channel_id=1, source_target_pairs={{0,6},{1,7},{2,4},{3,5},{4,2},{5,3},{6,0},{7,1},{8,14},{9,15},{10,... | collective-permute-start | bytes 589832 | tf_op jit(solution)/shard_map/ppermute | solution.py:356
  13.7 0.1 collective-permute-start.3
  13.9 0.0 collective-permute-start.2
  13.9 0.0 copy-done.8
  13.9 3.7 %parent_step.1.parent_change.rest_0_ = bf16[6,64,128]{2,1,0:T(8,128)(2,1)S(1)} custom-call(f32[6,128,128]{2,1,0:T(8,128)S(1)} %get-tuple-element.14.parent, f32[6,2,64,128]{3,2,1,0:T(8,128)S(1)} %get-tuple-element.16.stacked, f32[64,128]{1,0:T(8,128)S(1)} %copy-done.8), custom_call_target="tpu_custom_call" | custom-call | flops 251658240 | bytes 786432 | tf_op jit(solution)/shard_map/parent_step/pallas_call | solution.py:406
  17.6 4.1 %collective-permute-start.10 = (bf16[6,64,128]{2,1,0:T(8,128)(2,1)S(1)}, bf16[6,64,128]{2,1,0:T(8,128)(2,1)S(1)}, u32[]{:S(2)}, u32[]{:S(2)}) collective-permute-start(bf16[6,64,128]{2,1,0:T(8,128)(2,1)S(1)} %parent_step.1.parent_change.rest_0_), channel_id=1, source_target_pairs={{0,24},{8,16},{16,8},{24,0},{1,25},{9,17},{17,9},{25,1},{2,26},{10... | collective-permute-start | bytes 294920 | tf_op jit(solution)/shard_map/ppermute | solution.py:356
  21.7 0.0 collective-permute-done.4.refs_0_.rest_3_
  21.7 1.8 %collective-permute-start.8 = (bf16[6,64,128]{2,1,0:T(8,128)(2,1)S(1)}, bf16[6,64,128]{2,1,0:T(8,128)(2,1)S(1)}, u32[]{:S(2)}, u32[]{:S(2)}) collective-permute-start(bf16[6,64,128]{2,1,0:T(8,128)(2,1)S(1)} %parent_step.1.parent_change.rest_0_), channel_id=1, source_target_pairs={{0,8},{8,0},{16,24},{24,16},{1,9},{9,1},{17,25},{25,17},{2,10},{10... | collective-permute-start | bytes 294920 | tf_op jit(solution)/shard_map/ppermute | solution.py:356
  23.5 0.0 collective-permute-done.5.refs_1_.rest_4_
  23.5 2.6 %collective-permute-start.9 = (bf16[6,64,128]{2,1,0:T(8,128)(2,1)S(1)}, bf16[6,64,128]{2,1,0:T(8,128)(2,1)S(1)}, u32[]{:S(2)}, u32[]{:S(2)}) collective-permute-start(bf16[6,64,128]{2,1,0:T(8,128)(2,1)S(1)} %parent_step.1.parent_change.rest_0_), channel_id=1, source_target_pairs={{0,16},{8,24},{16,0},{24,8},{1,17},{9,25},{17,1},{25,9},{2,18},{10... | collective-permute-start | bytes 294920 | tf_op jit(solution)/shard_map/ppermute | solution.py:356
  26.1 0.0 collective-permute-done.3._.rest_2_
  26.2 0.1 collective-permute-start.7
  26.2 0.0 collective-permute-done.2.swapped.rest_1_
  26.2 0.5 %collective-permute-start.6 = (bf16[2,6,64,128]{3,2,1,0:T(8,128)(2,1)S(1)}, bf16[2,6,64,128]{3,2,1,0:T(8,128)(2,1)S(1)}, u32[]{:S(2)}, u32[]{:S(2)}) collective-permute-start(bf16[2,6,64,128]{3,2,1,0:T(8,128)(2,1)S(1)} %collective-permute-done.3._.rest_2_), channel_id=1, source_target_pairs={{0,1},{1,0},{2,3},{3,2},{4,5},{5,4},{6,7},{7,6},{8,9},{9,8},{10,11... | collective-permute-start | bytes 589832 | tf_op jit(solution)/shard_map/ppermute | solution.py:356
  26.7 0.0 copy-done.1
  26.7 0.0 copy-done.3
  26.7 1.5 %middle_step.1 = (bf16[12,64,256]{2,1,0:T(8,128)(2,1)}, bf16[12,64,768]{2,1,0:T(8,128)(2,1)S(1)}, bf16[6,64,384]{2,1,0:T(8,128)(2,1)S(1)}, f32[8,128]{1,0:T(8,128)S(1)}) custom-call(bf16[2,6,64,128]{3,2,1,0:T(8,128)(2,1)S(1)} %get-tuple-element.15.change.rest_0_, bf16[2,6,64,128]{3,2,1,0:T(8,128)(2,1)S(1)} %collective-permute-done.2.swapped.rest_1_, ...), custom_call_target="tpu_custom_call" | custom-call | flops 251658240 | bytes 7077888 | tf_op jit(solution)/shard_map/middle_step/pallas_call | solution.py:414
  28.2 0.0 copy-start.9
  28.2 0.0 collective-permute-done.6.rest_5_
  28.2 0.0 collective-permute-done.7.rest_6_
  28.3 0.7 %copy-done.9 = s32[12,6]{0,1:T(8,128)S(1)} copy-done((s32[12,6]{0,1:T(8,128)S(1)}, s32[12,6]{0,1:T(8,128)}, u32[]{:S(2)}) %copy-start.9) | copy-done | bytes 312
  28.9 0.0 copy-done.10
  28.9 3.0 %leaf_couple.1 = (bf16[12,6,4096]{2,1,0:T(8,128)(2,1)}, f32[8,128]{1,0:T(8,128)S(1)}) custom-call(s32[6,12]{1,0:T(8,128)S(1)} %bitcast.6, s32[6,12]{1,0:T(8,128)S(1)} %bitcast.7, bf16[12,64,768]{2,1,0:T(8,128)(2,1)S(1)} %get-tuple-element.18.middle, f32[8,128]{1,0:T(8,128)S(1)} %pause.1._, bf16[2,6,64,128]{3,2,1,0:T(8,128)(2,1)S(1)} %get-tuple-element.15.change.rest_0_, ...), custom_call_target="tpu_custom_call" | custom-call | flops 17179869184 | bytes 1179648 | tf_op jit(solution)/shard_map/leaf_couple/pallas_call | solution.py:434
  32.0 0.0 collective-permute-done.10.rest_3_
  32.0 0.0 collective-permute-done.8.rest_1_
  32.0 0.0 collective-permute-done.9.rest_2_
  32.0 0.0 copy-done.6
  32.0 0.0 copy-done.7
  32.0 1.8 %parent_couple.1 = bf16[6,3,4096]{2,1,0:T(4,128)(2,1)} custom-call(s32[3,6]{1,0:T(4,128)S(1)} %bitcast.4, s32[3,6]{1,0:T(4,128)S(1)} %bitcast.5, bf16[6,64,384]{2,1,0:T(8,128)(2,1)S(1)} %get-tuple-element.21.middle, f32[8,128]{1,0:T(8,128)S(1)} %get-tuple-element.22._, bf16[6,64,128]{2,1,0:T(8,128)(2,1)S(1)} %parent_step.1.parent_change.rest_0_, ...), custom_call_target="tpu_custom_call" | custom-call | flops 98304 | bytes 393216 | tf_op jit(solution)/shard_map/parent_couple/pallas_call | solution.py:446
  (5 shorter events, 0.0 us)
Async XLA Ops:
  0.6 1.7 %copy-start = (bf16[12,6,128,128]{3,2,1,0:T(8,128)(2,1)S(1)}, bf16[12,6,128,128]{3,2,1,0:T(8,128)(2,1)}, u32[]{:S(2)}) copy-start(bf16[12,6,128,128]{3,2,1,0:T(8,128)(2,1)} %blocks.5) | copy-start | bytes 7077892
  2.3 1.0 %copy-start.4 = (bf16[12,128,128]{2,1,0:T(8,128)(2,1)S(1)}, bf16[12,128,128]{2,1,0:T(8,128)(2,1)}, u32[]{:S(2)}) copy-start(bf16[12,128,128]{2,1,0:T(8,128)(2,1)} %transfers.1) | copy-start | bytes 1179652
  2.3 1.4 %copy-start.2 = (bf16[6,3,128,128]{3,2,1,0:T(8,128)(2,1)S(1)}, bf16[6,3,128,128]{3,2,1,0:T(8,128)(2,1)}, u32[]{:S(2)}) copy-start(bf16[6,3,128,128]{3,2,1,0:T(8,128)(2,1)} %parents.3) | copy-start | bytes 1769476
  2.3 2.9 %copy-start.5 = (f32[64,128]{1,0:T(8,128)S(1)}, f32[64,128]{1,0:T(8,128)}, u32[]{:S(2)}) copy-start(f32[64,128]{1,0:T(8,128)} %start.2) | copy-start | bytes 98308
  2.8 11.1 %copy-start.8 = (f32[64,128]{1,0:T(8,128)S(1)}, f32[64,128]{1,0:T(8,128)}, u32[]{:S(2)}) copy-start(f32[64,128]{1,0:T(8,128)} %start.3) | copy-start | bytes 98308
  2.8 1.9 %collective-permute-start = (f32[6,128,128]{2,1,0:T(8,128)S(1)}, f32[6,128,128]{2,1,0:T(8,128)S(1)}, u32[]{:S(2)}, u32[]{:S(2)}) collective-permute-start(f32[6,128,128]{2,1,0:T(8,128)S(1)} %sent_weights.1), channel_id=1, source_target_pairs={{0,1},{1,0},{2,3},{3,2},{4,5},{5,4},{6,7},{7,6},{8,9},{9,8},{10,11... | collective-permute-start | bytes 1179656 | tf_op jit(solution)/shard_map/ppermute | solution.py:356
  3.3 1.9 %collective-permute-start.1 = (bf16[12,128,128]{2,1,0:T(8,128)(2,1)S(1)}, bf16[12,128,128]{2,1,0:T(8,128)(2,1)S(1)}, u32[]{:S(2)}, u32[]{:S(2)}) collective-permute-start(bf16[12,128,128]{2,1,0:T(8,128)(2,1)S(1)} %copy-done.4), channel_id=1, source_target_pairs={{0,1},{1,0},{2,3},{3,2},{4,5},{5,4},{6,7},{7,6},{8,9},{9,8},{10,11... | collective-permute-start | bytes 1179656 | tf_op jit(solution)/shard_map/ppermute | solution.py:356
  4.4 22.3 %copy-start.1 = (bf16[12,6,128,128]{3,2,1,0:T(8,128)(2,1)S(1)}, bf16[12,6,128,128]{3,2,1,0:T(8,128)(2,1)}, u32[]{:S(2)}) copy-start(bf16[12,6,128,128]{3,2,1,0:T(8,128)(2,1)} %blocks.5) | copy-start | bytes 7077892
  4.5 22.3 %copy-start.3 = (bf16[12,256,128]{2,1,0:T(8,128)(2,1)S(1)}, bf16[12,256,128]{2,1,0:T(8,128)(2,1)}, u32[]{:S(2)}) copy-start(bf16[12,256,128]{2,1,0:T(8,128)(2,1)} %bases.1) | copy-start | bytes 2359300
  9.4 12.4 %collective-permute-start.4 = (bf16[2,6,64,128]{3,2,1,0:T(8,128)(2,1)S(1)}, bf16[2,6,64,128]{3,2,1,0:T(8,128)(2,1)S(1)}, u32[]{:S(2)}, u32[]{:S(2)}) collective-permute-start(bf16[2,6,64,128]{3,2,1,0:T(8,128)(2,1)S(1)} %get-tuple-element.15.change.rest_0_), channel_id=1, source_target_pairs={{0,4},{1,5},{2,6},{3,7},{4,0},{5,1},{6,2},{7,3},{8,12},{9,13},{10,... | collective-permute-start | bytes 589832 | tf_op jit(solution)/shard_map/ppermute | solution.py:356
  12.3 11.2 %collective-permute-start.5 = (bf16[2,6,64,128]{3,2,1,0:T(8,128)(2,1)S(1)}, bf16[2,6,64,128]{3,2,1,0:T(8,128)(2,1)S(1)}, u32[]{:S(2)}, u32[]{:S(2)}) collective-permute-start(bf16[2,6,64,128]{3,2,1,0:T(8,128)(2,1)S(1)} %get-tuple-element.15.change.rest_0_), channel_id=1, source_target_pairs={{0,6},{1,7},{2,4},{3,5},{4,2},{5,3},{6,0},{7,1},{8,14},{9,15},{10,... | collective-permute-start | bytes 589832 | tf_op jit(solution)/shard_map/ppermute | solution.py:356
  13.7 12.4 %collective-permute-start.3 = (bf16[2,6,64,128]{3,2,1,0:T(8,128)(2,1)S(1)}, bf16[2,6,64,128]{3,2,1,0:T(8,128)(2,1)S(1)}, u32[]{:S(2)}, u32[]{:S(2)}) collective-permute-start(bf16[2,6,64,128]{3,2,1,0:T(8,128)(2,1)S(1)} %get-tuple-element.15.change.rest_0_), channel_id=1, source_target_pairs={{0,2},{1,3},{2,0},{3,1},{4,6},{5,7},{6,4},{7,5},{8,10},{9,11},{10,... | collective-permute-start | bytes 589832 | tf_op jit(solution)/shard_map/ppermute | solution.py:356
  13.9 12.4 %collective-permute-start.2 = (bf16[2,6,64,128]{3,2,1,0:T(8,128)(2,1)S(1)}, bf16[2,6,64,128]{3,2,1,0:T(8,128)(2,1)S(1)}, u32[]{:S(2)}, u32[]{:S(2)}) collective-permute-start(bf16[2,6,64,128]{3,2,1,0:T(8,128)(2,1)S(1)} %get-tuple-element.15.change.rest_0_), channel_id=1, source_target_pairs={{0,1},{1,0},{2,3},{3,2},{4,5},{5,4},{6,7},{7,6},{8,9},{9,8},{10,11... | collective-permute-start | bytes 589832 | tf_op jit(solution)/shard_map/ppermute | solution.py:356
  17.6 14.4 %collective-permute-start.10 = (bf16[6,64,128]{2,1,0:T(8,128)(2,1)S(1)}, bf16[6,64,128]{2,1,0:T(8,128)(2,1)S(1)}, u32[]{:S(2)}, u32[]{:S(2)}) collective-permute-start(bf16[6,64,128]{2,1,0:T(8,128)(2,1)S(1)} %parent_step.1.parent_change.rest_0_), channel_id=1, source_target_pairs={{0,24},{8,16},{16,8},{24,0},{1,25},{9,17},{17,9},{25,1},{2,26},{10... | collective-permute-start | bytes 294920 | tf_op jit(solution)/shard_map/ppermute | solution.py:356
  21.7 10.2 %collective-permute-start.8 = (bf16[6,64,128]{2,1,0:T(8,128)(2,1)S(1)}, bf16[6,64,128]{2,1,0:T(8,128)(2,1)S(1)}, u32[]{:S(2)}, u32[]{:S(2)}) collective-permute-start(bf16[6,64,128]{2,1,0:T(8,128)(2,1)S(1)} %parent_step.1.parent_change.rest_0_), channel_id=1, source_target_pairs={{0,8},{8,0},{16,24},{24,16},{1,9},{9,1},{17,25},{25,17},{2,10},{10... | collective-permute-start | bytes 294920 | tf_op jit(solution)/shard_map/ppermute | solution.py:356
  23.5 8.5 %collective-permute-start.9 = (bf16[6,64,128]{2,1,0:T(8,128)(2,1)S(1)}, bf16[6,64,128]{2,1,0:T(8,128)(2,1)S(1)}, u32[]{:S(2)}, u32[]{:S(2)}) collective-permute-start(bf16[6,64,128]{2,1,0:T(8,128)(2,1)S(1)} %parent_step.1.parent_change.rest_0_), channel_id=1, source_target_pairs={{0,16},{8,24},{16,0},{24,8},{1,17},{9,25},{17,1},{25,9},{2,18},{10... | collective-permute-start | bytes 294920 | tf_op jit(solution)/shard_map/ppermute | solution.py:356
  26.2 2.1 %collective-permute-start.7 = (bf16[4,6,64,128]{3,2,1,0:T(8,128)(2,1)S(1)}, bf16[4,6,64,128]{3,2,1,0:T(8,128)(2,1)S(1)}, u32[]{:S(2)}, u32[]{:S(2)}) collective-permute-start(bf16[4,6,64,128]{3,2,1,0:T(8,128)(2,1)S(1)} %pack.1), channel_id=1, source_target_pairs={{0,1},{1,0},{2,3},{3,2},{4,5},{5,4},{6,7},{7,6},{8,9},{9,8},{10,11... | collective-permute-start | bytes 1179656 | tf_op jit(solution)/shard_map/ppermute | solution.py:356
  26.2 2.0 %collective-permute-start.6 = (bf16[2,6,64,128]{3,2,1,0:T(8,128)(2,1)S(1)}, bf16[2,6,64,128]{3,2,1,0:T(8,128)(2,1)S(1)}, u32[]{:S(2)}, u32[]{:S(2)}) collective-permute-start(bf16[2,6,64,128]{3,2,1,0:T(8,128)(2,1)S(1)} %collective-permute-done.3._.rest_2_), channel_id=1, source_target_pairs={{0,1},{1,0},{2,3},{3,2},{4,5},{5,4},{6,7},{7,6},{8,9},{9,8},{10,11... | collective-permute-start | bytes 589832 | tf_op jit(solution)/shard_map/ppermute | solution.py:356
  28.2 0.7 %copy-start.9 = (s32[12,6]{0,1:T(8,128)S(1)}, s32[12,6]{0,1:T(8,128)}, u32[]{:S(2)}) copy-start(s32[12,6]{0,1:T(8,128)} %param.13) | copy-start | bytes 868
  28.2 0.7 %copy-start.10 = (s32[12,6]{0,1:T(8,128)S(1)}, s32[12,6]{0,1:T(8,128)}, u32[]{:S(2)}) copy-start(s32[12,6]{0,1:T(8,128)} %param.14) | copy-start | bytes 868
  28.9 3.1 %copy-start.6 = (s32[6,3]{0,1:T(4,128)S(1)}, s32[6,3]{0,1:T(4,128)}, u32[]{:S(2)}) copy-start(s32[6,3]{0,1:T(4,128)} %param.16) | copy-start | bytes 220
  28.9 3.1 %copy-start.7 = (s32[6,3]{0,1:T(4,128)S(1)}, s32[6,3]{0,1:T(4,128)}, u32[]{:S(2)}) copy-start(s32[6,3]{0,1:T(4,128)} %param.17) | copy-start | bytes 220

commit v3 on v2

--- a/solution.py
+++ b/solution.py
@@ -156,8 +156,18 @@
         weight[j] = gram_sum([blocks[start + j, c] for c in range(blocks.shape[1])])
 
 
-def kept_weights(blocks, parents, weight, parent_weight):
+def kept_weights(
+    blocks, parents, devs, slots, groups, parent_slots,
+    weight, parent_weight, leaf_table, parent_table,
+):
     half = weight.shape[0]
+    index = lax.axis_index("sub")
+    member, chip = index & 1, index >> 1
+    dev, slot = devs[...], slots[...]
+    side = jnp.where(slot >= half, 1, 0)
+    box = ((dev >> 1) ^ chip) * 2 + (side ^ member)
+    leaf_table[...] = (box * 2 + ((dev & 1) ^ side)) * half + slot - side * half
+    parent_table[...] = (groups[...] ^ lax.axis_index("grp")) * half + parent_slots[...]
     start = (lax.axis_index("sub") % 2) * half
     for j in range(half):
         weight[j] = gram_sum([blocks[start + j, c] for c in range(blocks.shape[1])])
@@ -228,30 +238,42 @@
     ).astype(BF16)
 
 
-def middle_step(
-    change, swapped, parent_change, bases, blocks, parents, _,
-    new_bases, leaf_half, parent_half, token,
+def middle_own(
+    change, parent_change, bases, blocks, parents, _,
+    own_bases, own_half, parent_half, token,
     order, order_parents,
 ):
     token[...] = jnp.zeros(token.shape, token.dtype)
     half, links = parents.shape[0], blocks.shape[1]
-    member = lax.axis_index("sub") % 2
-    for at in range(2 * half):
-        j = at % half
-        spot = (member if at < half else 1 - member) * half + j
-        rows = change[0, j] if at < half else swapped[1, j]
-        ordered = parted(rows, order.at[at % 4])
-        new_bases[spot] = dot_t(rows, bases[spot]).astype(BF16)
-        leaf_half[spot] = dot(ordered, cat([blocks[spot, c] for c in range(links)], 1)).astype(BF16)
-    for j in range(half):
-        ordered = parted(parent_change[j], order_parents.at[j % 2])
+    first = (lax.axis_index("sub") % 2) * half
+    for j in range(half):
+        rows = change[0, j]
+        ordered = parted(rows, order.at[j % 4])
+        own_bases[j] = dot_t(rows, bases[first + j]).astype(BF16)
+        own_half[j] = dot(ordered, cat([blocks[first + j, c] for c in range(links)], 1)).astype(BF16)
+    for j in range(half):
+        ordered = parted(parent_change[j], order_parents.at[j % 4])
         parent_half[j] = dot(
             ordered, cat([parents[j, c] for c in range(parents.shape[1])], 1)
         ).astype(BF16)
 
 
+def middle_other(swapped, bases, blocks, own_bases, _, new_bases, other_half, order):
+    half, links = own_bases.shape[0], blocks.shape[1]
+    member = lax.axis_index("sub") % 2
+    first = (1 - member) * half
+    new_bases[pl.ds(member * half, half)] = own_bases[...]
+    for j in range(half):
+        rows = swapped[1, j]
+        ordered = parted(rows, order.at[j % 4])
+        new_bases[first + j] = dot_t(rows, bases[first + j]).astype(BF16)
+        other_half[j] = dot(
+            ordered, cat([blocks[first + j, c] for c in range(links)], 1)
+        ).astype(BF16)
+
+
 def pack(*refs):
-    *parts, out = refs
+    _, *parts, out = refs
     count = parts[0].shape[0]
     for at, part in enumerate(parts):
         out[at * count : at * count + count] = part[...]
@@ -261,10 +283,10 @@
     token[...] = jnp.zeros(token.shape, token.dtype)
 
 
-def couple(middle, partner, lanes_low):
-    full = dot_t(middle, cat([partner, partner], 0))
+def couple(middle, partner):
+    full = dot_t(middle, partner)
     count = full.shape[0] // 2
-    return jnp.where(lanes_low, full[:count], full[count:])
+    return cat([full[:count], full[count:]], 1)
 
 
 def write_rows(out, at, order, links, count):
@@ -272,62 +294,45 @@
         out[at, :, m * 128 : m * 128 + 128] = order[8 * m : 8 * m + links, :].astype(BF16)
 
 
-def leaf_couple(boxes, devs_in, slots_in, middle, _, *rest):
-    held_boxes, (out, token, devs, slots, held, order, sems) = rest[:-7], rest[-7:]
+def leaf_couple(boxes, table_in, own_half, other_half, _, *rest):
+    held_boxes, (out, token, table, held, order, sem) = rest[:-6], rest[-6:]
+    count, links = out.shape[0], out.shape[1]
+    half, rank = own_half.shape[:2]
+    member = lax.axis_index("sub") % 2
+    copy = pltpu.make_async_copy(table_in, table, sem)
+    copy.start()
     token[...] = jnp.zeros(token.shape, token.dtype)
-    count, links = out.shape[0], out.shape[1]
-    half = count // 2
-    rank = middle.shape[1]
-    index = lax.axis_index("sub")
-    member, chip = index % 2, index // 2
-    copies = [
-        pltpu.make_async_copy(devs_in, devs, sems.at[0]),
-        pltpu.make_async_copy(slots_in, slots, sems.at[1]),
-    ]
-    for copy in copies:
-        copy.start()
+    size = 2 * held_boxes[0].shape[1]
     for box, source in zip(boxes, held_boxes):
         for at, place in enumerate(box):
-            held[place] = source[2 * at : 2 * at + 2]
-    for copy in copies:
-        copy.wait()
-    low = lax.broadcasted_iota(jnp.int32, (rank // 2, 2 * rank), 1) < rank
-    for t in range(count):
+            part = source[2 * at : 2 * at + 2]
+            held[place * size : place * size + size] = part.reshape((size,) + part.shape[2:])
+    copy.wait()
+    for at in range(count):
+        own = at < half
+        middle = own_half if own else other_half
+        j = at % half
+        t = (member if own else 1 - member) * half + j
         for c in range(links):
-            dev, slot = devs[c, t], slots[c, t]
-            side = jnp.where(slot >= half, 1, 0)
-            place = slot - side * half
-            box = ((dev // 2) ^ chip) * 2 + (side ^ member)
-            partner = held[box, (dev % 2) ^ side, place]
-            order[t % 4, pl.ds(c, rank // 2, stride=8), :] = couple(
-                middle[t, :, c * 128 : c * 128 + 128], partner, low
+            order[at % 4, pl.ds(c, rank // 2, stride=8), :] = couple(
+                middle[j, :, c * 128 : c * 128 + 128], held[table[c, t]]
             )
-        write_rows(out, t, order.at[t % 4], links, rank // 2)
-
-
-def parent_couple(groups_in, slots_in, middle, _, *rest):
-    boxes = len(rest) - 6
-    near = rest[:boxes]
-    out, groups, slots, held, order, sems = rest[boxes:]
+        write_rows(out, t, order.at[at % 4], links, rank // 2)
+
+
+def parent_couple(table_in, middle, _, *rest):
+    near, (out, table, held, order, sem) = rest[:-5], rest[-5:]
     count, links = out.shape[0], out.shape[1]
     rank = middle.shape[1]
-    mine = lax.axis_index("grp")
-    copies = [
-        pltpu.make_async_copy(groups_in, groups, sems.at[0]),
-        pltpu.make_async_copy(slots_in, slots, sems.at[1]),
-    ]
-    for copy in copies:
-        copy.start()
-    for m in range(boxes):
-        held[m] = near[m][...]
-    for copy in copies:
-        copy.wait()
-    low = lax.broadcasted_iota(jnp.int32, (rank // 2, 2 * rank), 1) < rank
+    copy = pltpu.make_async_copy(table_in, table, sem)
+    copy.start()
+    for m in range(len(near)):
+        held[m * count : m * count + count] = near[m][...]
+    copy.wait()
     for p in range(count):
         for c in range(links):
-            partner = held[groups[c, p] ^ mine, slots[c, p]]
             order[p % 2, pl.ds(c, rank // 2, stride=8), :] = couple(
-                middle[p, :, c * 128 : c * 128 + 128], partner, low
+                middle[p, :, c * 128 : c * 128 + 128], held[table[c, p]]
             )
         write_rows(out, p, order.at[p % 2], links, rank // 2)
 
@@ -385,10 +390,15 @@
         "sent_weights", 8, 2 * links * square * old, 2 * links * square,
     )(leaf_blocks)
     other = swap(sent, "sub", 1)
-    own, parent_weight = call(
-        kept_weights, [VMEM] * 2, [weights, weights], [],
+    own, parent_weight, leaf_table, parent_table = call(
+        kept_weights, [VMEM] * 6,
+        [weights, weights, shape((links, count), jnp.int32), shape((parent_links, half), jnp.int32)],
+        [],
         "kept_weights", 8, 2 * (links + parent_links) * square * old, 8 * links * square,
-    )(leaf_blocks, parent_blocks)
+    )(
+        leaf_blocks, parent_blocks,
+        leaf_partner_dev.T, leaf_partner_slot.T, parent_partner_group.T, parent_partner_slot.T,
+    )
     tables = [
         pltpu.VMEM((8 * rank, 2 * rank), F32),
         pltpu.VMEM((8 * rank, 2 * rank), F32),
@@ -411,50 +421,51 @@
         swap(parent_change, "grp", m) for m in range(1, groups)
     ]
     token = shape((8, 128), F32)
-    new_leaf_bases, leaf_half, parent_half, after_middle = call(
-        middle_step, [VMEM] * 7,
+    half_shape = shape((half, rank, links * old), BF16)
+    own_bases, own_half, parent_half, after_middle = call(
+        middle_own, [VMEM] * 6,
         [
-            shape((count, rank, points), BF16),
-            shape((count, rank, links * old), BF16),
-            shape((half, rank, parent_links * old), BF16),
-            token,
+            shape((half, rank, points), BF16), half_shape,
+            shape((half, rank, parent_links * old), BF16), token,
         ],
-        [pltpu.VMEM((4, rank, old), F32), pltpu.VMEM((2, rank, old), F32)],
-        "middle_step", 8, 20 * square * old, 12 * links * square,
-    )(change, swapped, parent_change, leaf_bases, leaf_blocks, parent_blocks, near[0])
+        [pltpu.VMEM((4, rank, old), F32), pltpu.VMEM((4, rank, old), F32)],
+        "middle_own", 8, 1 << 34, square,
+    )(change, parent_change, leaf_bases, leaf_blocks, parent_blocks, swapped)
     packed = call(
-        pack, [VMEM] * (chips - 2), shape((2 * (chips - 2), half, rank, old), BF16), [],
-        "pack", 2 + chips, square, square,
-    )(*near[1:])
-    paused = call(pause, [VMEM], token, [], "pause", 4, 1 << 34, square)(after_middle)
-    held = [change, swapped, *near, swap(near[0], "sub", 1), swap(packed, "sub", 1)]
+        pack, [VMEM] * chips, shape((2 * chips - 2, half, rank, old), BF16), [],
+        "pack", 4 + chips, 1 << 34, square,
+    )(after_middle, *near)
+    new_leaf_bases, other_half = call(
+        middle_other, [VMEM] * 5, [shape((count, rank, points), BF16), half_shape],
+        [pltpu.VMEM((4, rank, old), F32)],
+        "middle_other", 8, square, square,
+    )(swapped, leaf_bases, leaf_blocks, own_bases, packed)
+    paused = call(pause, [VMEM], token, [], "pause", 4, 1 << 34, square)(packed)
+    held = [change, swapped, *near, swap(packed, "sub", 1)]
     boxes = [(0,), (1,)] + [(2 * m,) for m in range(1, chips)]
-    boxes += [(3,), tuple(2 * m + 1 for m in range(2, chips))]
-    table = pltpu.SMEM
+    boxes += [tuple(2 * m + 1 for m in range(1, chips))]
     new_leaf_blocks, after_leaves = call(
-        functools.partial(leaf_couple, boxes), [ANY, ANY] + [VMEM] * (2 + len(held)),
+        functools.partial(leaf_couple, boxes), [ANY] + [VMEM] * (3 + len(held)),
         [shape((count, links, rank * rank), BF16), token],
         [
-            table((links, count), jnp.int32),
-            table((links, count), jnp.int32),
-            pltpu.VMEM((2 * chips, 2, half, rank, old), BF16),
+            pltpu.SMEM((links, count), jnp.int32),
+            pltpu.VMEM((2 * chips * count, rank, old), BF16),
             pltpu.VMEM((4, 4 * rank, 2 * rank), F32),
-            dma((2,)),
+            dma(()),
         ],
         "leaf_couple", 4 + chips, 1 << 34, 12 * square,
-    )(leaf_partner_dev.T, leaf_partner_slot.T, leaf_half, paused, *held)
+    )(leaf_table, own_half, other_half, paused, *held)
     new_parent_blocks = call(
-        parent_couple, [ANY, ANY] + [VMEM] * (groups + 2),
+        parent_couple, [ANY] + [VMEM] * (groups + 2),
         shape((half, parent_links, rank * rank), BF16),
         [
-            table((parent_links, half), jnp.int32),
-            table((parent_links, half), jnp.int32),
-            pltpu.VMEM((groups, half, rank, old), BF16),
+            pltpu.SMEM((parent_links, half), jnp.int32),
+            pltpu.VMEM((groups * half, rank, old), BF16),
             pltpu.VMEM((2, 4 * rank, 2 * rank), F32),
-            dma((2,)),
+            dma(()),
         ],
         "parent_couple", 4 + groups, square, 4 * square,
-    )(parent_partner_group.T, parent_partner_slot.T, parent_half, after_leaves, *parents_held)
+    )(parent_table, parent_half, after_leaves, *parents_held)
     return (new_leaf_bases, new_leaf_blocks, new_parent_blocks)
 
 

time: 34 us -> 31.7 us (0.932)
  starting transfers between devices: 14.5 us -> 10.4 us
  waiting for transfers between devices: 0.81 us -> 3.9 us
  local copies, waits for them, and re-layouts: 2.38 us -> 1.71 us
  Pallas kernels: 15.3 us -> 14.8 us
    ppermute x11 -> x10, starting transfers between devices: 14.5 us -> 10.4 us  [swap(): return lax.ppermute(block, axis, [(i, i ^ mask) for i in range(count)])]
    ppermute x11 -> x10, waiting for transfers between devices: 0.81 us -> 3.9 us  [swap(): return lax.ppermute(block, axis, [(i, i ^ mask) for i in range(count)])]
    unnamed x22, local copies, waits for them, and re-layouts: 2.38 us -> 1.71 us
    pallas_call x6 -> x7, Pallas kernels: 7.01 us -> 6.4 us  [the longest x1 2.33 us: shards(): call(functools.partial(leaf_couple, boxes), [ANY] + [VMEM] * (3 + len(hel...]
  transfers between devices with their start and end apart: 11 -> 10, of which waited for: 2 -> 5; matrix products, arithmetic and copies ran while one was open for 0% -> 0% of each run, Pallas kernels for 26% -> 27%
where the time goes in v3:
time: 31.7 us; the launch traced here: 31.5 us
  Pallas kernels  14.8 us (47%)
  starting transfers between devices  10.4 us (33%)
  waiting for transfers between devices  3.9 us (12%)
  local copies, waits for them, and re-layouts  1.71 us (5%)
  between operations  0.8 us (3%)
    ppermute x10, starting transfers between devices, swap(): return lax.ppermute(block, axis, [(i, i ^ mask) for i in range(count)])  10.4 us
    pallas_call x1, Pallas kernels, shards(): call(leaf_step, [VMEM] * 6, [shape((2, half, rank, old), BF16), shape((ha...  4.14 us
    ppermute x10, waiting for transfers between devices, swap(): return lax.ppermute(block, axis, [(i, i ^ mask) for i in range(count)])  3.9 us
    pallas_call x1, Pallas kernels, shards(): call(parent_step, [VMEM] * 3, shape((half, rank, old), BF16), tables, 'pa...  3.73 us
    pallas_call x1, Pallas kernels, shards(): call(functools.partial(leaf_couple, boxes), [ANY] + [VMEM] * (3 + len(hel...  2.33 us
    unnamed x22, local copies, waits for them, and re-layouts  1.71 us
    pallas_call x1, Pallas kernels, shards(): call(parent_couple, [ANY] + [VMEM] * (groups + 2), shape((half, parent_li...  1.64 us
    pallas_call x1, Pallas kernels, shards(): call(middle_other, [VMEM] * 5, [shape((count, rank, points), BF16), half_...  1.16 us
  transfers between devices with their start and end apart: 10, of which 5 were waited for; matrix products, arithmetic and copies ran while one was open for 0% of the time, Pallas kernels for 27%

profile of v3, /device:TPU:0, one launch (start us, length us, event | category | flops | bytes accessed | tf_op | source)
XLA Modules:
  0.0 31.5 jit_solution(10833927818178052892)
XLA Ops:
  0.6 0.0 copy-start
  0.6 1.7 %copy-done = bf16[12,6,128,128]{3,2,1,0:T(8,128)(2,1)S(1)} copy-done((bf16[12,6,128,128]{3,2,1,0:T(8,128)(2,1)S(1)}, bf16[12,6,128,128]{3,2,1,0:T(8,128)(2,1)}, u32[]{:S(2)}) %copy-start) | copy-done | bytes 2359320
  2.3 0.0 copy-start.4
  2.3 0.0 copy-start.3
  2.3 0.0 copy-start.8
  2.3 0.0 copy-start.9
  2.3 0.0 copy-start.5
  2.3 0.5 %sent_weights.1 = f32[6,128,128]{2,1,0:T(8,128)S(1)} custom-call(bf16[12,6,128,128]{3,2,1,0:T(8,128)(2,1)S(1)} %copy-done), custom_call_target="tpu_custom_call" | custom-call | flops 150994944 | bytes 1179648 | tf_op jit(solution)/shard_map/sent_weights/pallas_call | solution.py:388
  2.8 0.5 %collective-permute-start = (f32[6,128,128]{2,1,0:T(8,128)S(1)}, f32[6,128,128]{2,1,0:T(8,128)S(1)}, u32[]{:S(2)}, u32[]{:S(2)}) collective-permute-start(f32[6,128,128]{2,1,0:T(8,128)S(1)} %sent_weights.1), channel_id=1, source_target_pairs={{0,1},{1,0},{2,3},{3,2},{4,5},{5,4},{6,7},{7,6},{8,9},{9,8},{10,11... | collective-permute-start | bytes 1179656 | tf_op jit(solution)/shard_map/ppermute | solution.py:361
  3.3 0.0 copy-done.4
  3.3 0.4 %collective-permute-start.1 = (bf16[12,128,128]{2,1,0:T(8,128)(2,1)S(1)}, bf16[12,128,128]{2,1,0:T(8,128)(2,1)S(1)}, u32[]{:S(2)}, u32[]{:S(2)}) collective-permute-start(bf16[12,128,128]{2,1,0:T(8,128)(2,1)S(1)} %copy-done.4), channel_id=1, source_target_pairs={{0,1},{1,0},{2,3},{3,2},{4,5},{5,4},{6,7},{7,6},{8,9},{9,8},{10,11... | collective-permute-start | bytes 1179656 | tf_op jit(solution)/shard_map/ppermute | solution.py:361
  3.8 0.0 copy-done.3
  3.8 0.0 copy-done.6
  3.8 0.0 copy-done.7
  3.8 0.0 copy-done.8
  3.8 0.0 copy-done.9
  3.8 0.0 copy-start.10
  3.8 0.0 copy-start.1
  3.8 0.0 copy-start.2
  3.8 0.7 %kept_weights.1 = (f32[6,128,128]{2,1,0:T(8,128)S(1)}, f32[6,128,128]{2,1,0:T(8,128)S(1)}, s32[6,12]{1,0:T(8,128)S(1)}, s32[3,6]{1,0:T(4,128)S(1)}) custom-call(bf16[12,6,128,128]{3,2,1,0:T(8,128)(2,1)S(1)} %copy-done, bf16[6,3,128,128]{3,2,1,0:T(8,128)(2,1)S(1)} %copy-done.3, s32[6,12]{1,0:T(8,128)S(1)} %bitcast.4, s32[6,12]{1,0:T(8,128)S(1)} %bitcast.5, ...), custom_call_target="tpu_custom_call" | custom-call | flops 226492416 | bytes 4718592 | tf_op jit(solution)/shard_map/kept_weights/pallas_call | solution.py:393
  4.5 0.2 collective-permute-done.other
  4.7 0.6 %collective-permute-done.1.other_transfers = bf16[12,128,128]{2,1,0:T(8,128)(2,1)S(1)} collective-permute-done((bf16[12,128,128]{2,1,0:T(8,128)(2,1)S(1)}, bf16[12,128,128]{2,1,0:T(8,128)(2,1)S(1)}, u32[]{:S(2)}, u32[]{:S(2)}) %collective-permute-start.1) | collective-permute-done | bytes 393248 | tf_op jit(solution)/shard_map/ppermute | solution.py:361
  5.3 0.0 copy-done.5
  5.3 4.1 %leaf_step.1 = (bf16[2,6,64,128]{3,2,1,0:T(8,128)(2,1)S(1)}, f32[6,2,64,128]{3,2,1,0:T(8,128)S(1)}) custom-call(f32[6,128,128]{2,1,0:T(8,128)S(1)} %get-tuple-element.17.own, f32[6,128,128]{2,1,0:T(8,128)S(1)} %collective-permute-done.other, f32[6,128,128]{2,1,0:T(8,128)S(1)} %get-tuple-element.18.parent, bf16[12,128,128]{2,1,0:T(8,128)(2,1)S(1)} %copy-done.4, ...), custom_call_target="tpu_custom_call" | custom-call | flops 503316480 | bytes 786432 | tf_op jit(solution)/shard_map/leaf_step/pallas_call | solution.py:408
  9.4 0.4 %collective-permute-start.2 = (bf16[2,6,64,128]{3,2,1,0:T(8,128)(2,1)S(1)}, bf16[2,6,64,128]{3,2,1,0:T(8,128)(2,1)S(1)}, u32[]{:S(2)}, u32[]{:S(2)}) collective-permute-start(bf16[2,6,64,128]{3,2,1,0:T(8,128)(2,1)S(1)} %get-tuple-element.19.change.rest_0_), channel_id=1, source_target_pairs={{0,1},{1,0},{2,3},{3,2},{4,5},{5,4},{6,7},{7,6},{8,9},{9,8},{10,11... | collective-permute-start | bytes 589832 | tf_op jit(solution)/shard_map/ppermute | solution.py:361
  9.8 2.6 %collective-permute-start.3 = (bf16[2,6,64,128]{3,2,1,0:T(8,128)(2,1)S(1)}, bf16[2,6,64,128]{3,2,1,0:T(8,128)(2,1)S(1)}, u32[]{:S(2)}, u32[]{:S(2)}) collective-permute-start(bf16[2,6,64,128]{3,2,1,0:T(8,128)(2,1)S(1)} %get-tuple-element.19.change.rest_0_), channel_id=1, source_target_pairs={{0,2},{1,3},{2,0},{3,1},{4,6},{5,7},{6,4},{7,5},{8,10},{9,11},{10,... | collective-permute-start | bytes 589832 | tf_op jit(solution)/shard_map/ppermute | solution.py:361
  12.5 1.5 %collective-permute-start.4 = (bf16[2,6,64,128]{3,2,1,0:T(8,128)(2,1)S(1)}, bf16[2,6,64,128]{3,2,1,0:T(8,128)(2,1)S(1)}, u32[]{:S(2)}, u32[]{:S(2)}) collective-permute-start(bf16[2,6,64,128]{3,2,1,0:T(8,128)(2,1)S(1)} %get-tuple-element.19.change.rest_0_), channel_id=1, source_target_pairs={{0,4},{1,5},{2,6},{3,7},{4,0},{5,1},{6,2},{7,3},{8,12},{9,13},{10,... | collective-permute-start | bytes 589832 | tf_op jit(solution)/shard_map/ppermute | solution.py:361
  14.0 0.0 collective-permute-start.5
  14.0 0.0 copy-done.10
  14.0 3.7 %parent_step.1.parent_change.rest_0_ = bf16[6,64,128]{2,1,0:T(8,128)(2,1)S(1)} custom-call(f32[6,128,128]{2,1,0:T(8,128)S(1)} %get-tuple-element.18.parent, f32[6,2,64,128]{3,2,1,0:T(8,128)S(1)} %get-tuple-element.20.stacked, f32[64,128]{1,0:T(8,128)S(1)} %copy-done.10), custom_call_target="tpu_custom_call" | custom-call | flops 251658240 | bytes 786432 | tf_op jit(solution)/shard_map/parent_step/pallas_call | solution.py:416
  17.7 2.1 %collective-permute-start.7 = (bf16[6,64,128]{2,1,0:T(8,128)(2,1)S(1)}, bf16[6,64,128]{2,1,0:T(8,128)(2,1)S(1)}, u32[]{:S(2)}, u32[]{:S(2)}) collective-permute-start(bf16[6,64,128]{2,1,0:T(8,128)(2,1)S(1)} %parent_step.1.parent_change.rest_0_), channel_id=1, source_target_pairs={{0,8},{8,0},{16,24},{24,16},{1,9},{9,1},{17,25},{25,17},{2,10},{10... | collective-permute-start | bytes 294920 | tf_op jit(solution)/shard_map/ppermute | solution.py:361
  19.9 0.0 collective-permute-done.2._.swapped.rest_1_
  19.9 2.6 %collective-permute-start.8 = (bf16[6,64,128]{2,1,0:T(8,128)(2,1)S(1)}, bf16[6,64,128]{2,1,0:T(8,128)(2,1)S(1)}, u32[]{:S(2)}, u32[]{:S(2)}) collective-permute-start(bf16[6,64,128]{2,1,0:T(8,128)(2,1)S(1)} %parent_step.1.parent_change.rest_0_), channel_id=1, source_target_pairs={{0,16},{8,24},{16,0},{24,8},{1,17},{9,25},{17,1},{25,9},{2,18},{10... | collective-permute-start | bytes 294920 | tf_op jit(solution)/shard_map/ppermute | solution.py:361
  22.5 0.0 copy-done.1
  22.5 0.0 copy-done.2
  22.5 0.5 %middle_own.1 = (bf16[6,64,256]{2,1,0:T(8,128)(2,1)S(1)}, bf16[6,64,768]{2,1,0:T(8,128)(2,1)S(1)}, bf16[6,64,384]{2,1,0:T(8,128)(2,1)S(1)}, f32[8,128]{1,0:T(8,128)S(1)}) custom-call(bf16[2,6,64,128]{3,2,1,0:T(8,128)(2,1)S(1)} %get-tuple-element.19.change.rest_0_, bf16[6,64,128]{2,1,0:T(8,128)(2,1)S(1)} %parent_step.1.parent_change.rest_0_, ...), custom_call_target="tpu_custom_call" | custom-call | flops 17179869184 | bytes 98304 | tf_op jit(solution)/shard_map/middle_own/pallas_call | solution.py:425
  23.0 0.0 collective-permute-done.3.refs_1_.rest_2_
  23.0 0.1 collective-permute-start.9
  23.1 0.5 %collective-permute-done.4.refs_2_.rest_3_ = bf16[2,6,64,128]{3,2,1,0:T(8,128)(2,1)S(1)} collective-permute-done((bf16[2,6,64,128]{3,2,1,0:T(8,128)(2,1)S(1)}, bf16[2,6,64,128]{3,2,1,0:T(8,128)(2,1)S(1)}, u32[]{:S(2)}, u32[]{:S(2)}) %collective-permute-start.4) | collective-permute-done | bytes 196640 | tf_op jit(solution)/shard_map/ppermute | solution.py:361
  23.6 0.0 collective-permute-done.5.refs_3_.rest_4_
  23.6 0.1 collective-permute-start.6
  23.7 1.2 %middle_other.1 = (bf16[12,64,256]{2,1,0:T(8,128)(2,1)}, bf16[6,64,768]{2,1,0:T(8,128)(2,1)S(1)}) custom-call(bf16[2,6,64,128]{3,2,1,0:T(8,128)(2,1)S(1)} %collective-permute-done.2._.swapped.rest_1_, bf16[12,256,128]{2,1,0:T(8,128)(2,1)S(1)} %copy-done.2, bf16[12,6,128,128]{3,2,1,0:T(8,128)(2,1)S(1)} %copy-done.1, ...), custom_call_target="tpu_custom_call" | custom-call | flops 98304 | bytes 98304 | tf_op jit(solution)/shard_map/middle_other/pallas_call | solution.py:438
  24.9 0.8 %collective-permute-done.6.rest_5_ = bf16[6,6,64,128]{3,2,1,0:T(8,128)(2,1)S(1)} collective-permute-done((bf16[6,6,64,128]{3,2,1,0:T(8,128)(2,1)S(1)}, bf16[6,6,64,128]{3,2,1,0:T(8,128)(2,1)S(1)}, u32[]{:S(2)}, u32[]{:S(2)}) %collective-permute-start.6) | collective-permute-done | bytes 589856 | tf_op jit(solution)/shard_map/ppermute | solution.py:361
  25.7 2.3 %leaf_couple.1 = (bf16[12,6,4096]{2,1,0:T(8,128)(2,1)}, f32[8,128]{1,0:T(8,128)S(1)}) custom-call(s32[6,12]{1,0:T(8,128)S(1)} %get-tuple-element.24.table_in, bf16[6,64,768]{2,1,0:T(8,128)(2,1)S(1)} %get-tuple-element.25.own_half, bf16[6,64,768]{2,1,0:T(8,128)(2,1)S(1)} %get-tuple-element.26.other_half, f32[8,128]{1,0:T(8,128)S(1)} %pause.1._, ...), custom_call_target="tpu_custom_call" | custom-call | flops 17179869184 | bytes 1179648 | tf_op jit(solution)/shard_map/leaf_couple/pallas_call | solution.py:447
  28.0 0.0 collective-permute-done.7.rest_1_
  28.0 1.8 %collective-permute-done.8.rest_2_ = bf16[6,64,128]{2,1,0:T(8,128)(2,1)S(1)} collective-permute-done((bf16[6,64,128]{2,1,0:T(8,128)(2,1)S(1)}, bf16[6,64,128]{2,1,0:T(8,128)(2,1)S(1)}, u32[]{:S(2)}, u32[]{:S(2)}) %collective-permute-start.8) | collective-permute-done | bytes 98336 | tf_op jit(solution)/shard_map/ppermute | solution.py:361
  29.9 0.0 collective-permute-done.9.rest_3_
  29.9 1.6 %parent_couple.1 = bf16[6,3,4096]{2,1,0:T(4,128)(2,1)} custom-call(s32[3,6]{1,0:T(4,128)S(1)} %get-tuple-element.28.table_in, bf16[6,64,384]{2,1,0:T(8,128)(2,1)S(1)} %get-tuple-element.29.middle, f32[8,128]{1,0:T(8,128)S(1)} %get-tuple-element.30._, bf16[6,64,128]{2,1,0:T(8,128)(2,1)S(1)} %parent_step.1.parent_change.rest_0_, ...), custom_call_target="tpu_custom_call" | custom-call | flops 98304 | bytes 393216 | tf_op jit(solution)/shard_map/parent_couple/pallas_call | solution.py:458
  (4 shorter events, 0.0 us)
Async XLA Ops:
  0.6 1.7 %copy-start = (bf16[12,6,128,128]{3,2,1,0:T(8,128)(2,1)S(1)}, bf16[12,6,128,128]{3,2,1,0:T(8,128)(2,1)}, u32[]{:S(2)}) copy-start(bf16[12,6,128,128]{3,2,1,0:T(8,128)(2,1)} %blocks.7) | copy-start | bytes 7077892
  2.3 1.0 %copy-start.4 = (bf16[12,128,128]{2,1,0:T(8,128)(2,1)S(1)}, bf16[12,128,128]{2,1,0:T(8,128)(2,1)}, u32[]{:S(2)}) copy-start(bf16[12,128,128]{2,1,0:T(8,128)(2,1)} %transfers.1) | copy-start | bytes 1179652
  2.3 1.4 %copy-start.3 = (bf16[6,3,128,128]{3,2,1,0:T(8,128)(2,1)S(1)}, bf16[6,3,128,128]{3,2,1,0:T(8,128)(2,1)}, u32[]{:S(2)}) copy-start(bf16[6,3,128,128]{3,2,1,0:T(8,128)(2,1)} %parents.3) | copy-start | bytes 1769476
  2.3 1.4 %copy-start.6 = (s32[12,6]{0,1:T(8,128)S(1)}, s32[12,6]{0,1:T(8,128)}, u32[]{:S(2)}) copy-start(s32[12,6]{0,1:T(8,128)} %param.13) | copy-start | bytes 868
  2.3 1.5 %copy-start.7 = (s32[12,6]{0,1:T(8,128)S(1)}, s32[12,6]{0,1:T(8,128)}, u32[]{:S(2)}) copy-start(s32[12,6]{0,1:T(8,128)} %param.14) | copy-start | bytes 868
  2.3 1.4 %copy-start.8 = (s32[6,3]{0,1:T(4,128)S(1)}, s32[6,3]{0,1:T(4,128)}, u32[]{:S(2)}) copy-start(s32[6,3]{0,1:T(4,128)} %param.16) | copy-start | bytes 220
  2.3 1.4 %copy-start.9 = (s32[6,3]{0,1:T(4,128)S(1)}, s32[6,3]{0,1:T(4,128)}, u32[]{:S(2)}) copy-start(s32[6,3]{0,1:T(4,128)} %param.17) | copy-start | bytes 220
  2.3 2.9 %copy-start.5 = (f32[64,128]{1,0:T(8,128)S(1)}, f32[64,128]{1,0:T(8,128)}, u32[]{:S(2)}) copy-start(f32[64,128]{1,0:T(8,128)} %start.2) | copy-start | bytes 98308
  2.8 1.9 %collective-permute-start = (f32[6,128,128]{2,1,0:T(8,128)S(1)}, f32[6,128,128]{2,1,0:T(8,128)S(1)}, u32[]{:S(2)}, u32[]{:S(2)}) collective-permute-start(f32[6,128,128]{2,1,0:T(8,128)S(1)} %sent_weights.1), channel_id=1, source_target_pairs={{0,1},{1,0},{2,3},{3,2},{4,5},{5,4},{6,7},{7,6},{8,9},{9,8},{10,11... | collective-permute-start | bytes 1179656 | tf_op jit(solution)/shard_map/ppermute | solution.py:361
  3.3 1.9 %collective-permute-start.1 = (bf16[12,128,128]{2,1,0:T(8,128)(2,1)S(1)}, bf16[12,128,128]{2,1,0:T(8,128)(2,1)S(1)}, u32[]{:S(2)}, u32[]{:S(2)}) collective-permute-start(bf16[12,128,128]{2,1,0:T(8,128)(2,1)S(1)} %copy-done.4), channel_id=1, source_target_pairs={{0,1},{1,0},{2,3},{3,2},{4,5},{5,4},{6,7},{7,6},{8,9},{9,8},{10,11... | collective-permute-start | bytes 1179656 | tf_op jit(solution)/shard_map/ppermute | solution.py:361
  3.8 10.2 %copy-start.10 = (f32[64,128]{1,0:T(8,128)S(1)}, f32[64,128]{1,0:T(8,128)}, u32[]{:S(2)}) copy-start(f32[64,128]{1,0:T(8,128)} %start.3) | copy-start | bytes 98308
  3.8 18.7 %copy-start.1 = (bf16[12,6,128,128]{3,2,1,0:T(8,128)(2,1)S(1)}, bf16[12,6,128,128]{3,2,1,0:T(8,128)(2,1)}, u32[]{:S(2)}) copy-start(bf16[12,6,128,128]{3,2,1,0:T(8,128)(2,1)} %blocks.7) | copy-start | bytes 7077892
  3.8 18.7 %copy-start.2 = (bf16[12,256,128]{2,1,0:T(8,128)(2,1)S(1)}, bf16[12,256,128]{2,1,0:T(8,128)(2,1)}, u32[]{:S(2)}) copy-start(bf16[12,256,128]{2,1,0:T(8,128)(2,1)} %bases.3) | copy-start | bytes 2359300
  9.4 10.4 %collective-permute-start.2 = (bf16[2,6,64,128]{3,2,1,0:T(8,128)(2,1)S(1)}, bf16[2,6,64,128]{3,2,1,0:T(8,128)(2,1)S(1)}, u32[]{:S(2)}, u32[]{:S(2)}) collective-permute-start(bf16[2,6,64,128]{3,2,1,0:T(8,128)(2,1)S(1)} %get-tuple-element.19.change.rest_0_), channel_id=1, source_target_pairs={{0,1},{1,0},{2,3},{3,2},{4,5},{5,4},{6,7},{7,6},{8,9},{9,8},{10,11... | collective-permute-start | bytes 589832 | tf_op jit(solution)/shard_map/ppermute | solution.py:361
  9.8 13.2 %collective-permute-start.3 = (bf16[2,6,64,128]{3,2,1,0:T(8,128)(2,1)S(1)}, bf16[2,6,64,128]{3,2,1,0:T(8,128)(2,1)S(1)}, u32[]{:S(2)}, u32[]{:S(2)}) collective-permute-start(bf16[2,6,64,128]{3,2,1,0:T(8,128)(2,1)S(1)} %get-tuple-element.19.change.rest_0_), channel_id=1, source_target_pairs={{0,2},{1,3},{2,0},{3,1},{4,6},{5,7},{6,4},{7,5},{8,10},{9,11},{10,... | collective-permute-start | bytes 589832 | tf_op jit(solution)/shard_map/ppermute | solution.py:361
  12.5 11.1 %collective-permute-start.4 = (bf16[2,6,64,128]{3,2,1,0:T(8,128)(2,1)S(1)}, bf16[2,6,64,128]{3,2,1,0:T(8,128)(2,1)S(1)}, u32[]{:S(2)}, u32[]{:S(2)}) collective-permute-start(bf16[2,6,64,128]{3,2,1,0:T(8,128)(2,1)S(1)} %get-tuple-element.19.change.rest_0_), channel_id=1, source_target_pairs={{0,4},{1,5},{2,6},{3,7},{4,0},{5,1},{6,2},{7,3},{8,12},{9,13},{10,... | collective-permute-start | bytes 589832 | tf_op jit(solution)/shard_map/ppermute | solution.py:361
  14.0 9.6 %collective-permute-start.5 = (bf16[2,6,64,128]{3,2,1,0:T(8,128)(2,1)S(1)}, bf16[2,6,64,128]{3,2,1,0:T(8,128)(2,1)S(1)}, u32[]{:S(2)}, u32[]{:S(2)}) collective-permute-start(bf16[2,6,64,128]{3,2,1,0:T(8,128)(2,1)S(1)} %get-tuple-element.19.change.rest_0_), channel_id=1, source_target_pairs={{0,6},{1,7},{2,4},{3,5},{4,2},{5,3},{6,0},{7,1},{8,14},{9,15},{10,... | collective-permute-start | bytes 589832 | tf_op jit(solution)/shard_map/ppermute | solution.py:361
  17.7 10.3 %collective-permute-start.7 = (bf16[6,64,128]{2,1,0:T(8,128)(2,1)S(1)}, bf16[6,64,128]{2,1,0:T(8,128)(2,1)S(1)}, u32[]{:S(2)}, u32[]{:S(2)}) collective-permute-start(bf16[6,64,128]{2,1,0:T(8,128)(2,1)S(1)} %parent_step.1.parent_change.rest_0_), channel_id=1, source_target_pairs={{0,8},{8,0},{16,24},{24,16},{1,9},{9,1},{17,25},{25,17},{2,10},{10... | collective-permute-start | bytes 294920 | tf_op jit(solution)/shard_map/ppermute | solution.py:361
  19.9 10.0 %collective-permute-start.8 = (bf16[6,64,128]{2,1,0:T(8,128)(2,1)S(1)}, bf16[6,64,128]{2,1,0:T(8,128)(2,1)S(1)}, u32[]{:S(2)}, u32[]{:S(2)}) collective-permute-start(bf16[6,64,128]{2,1,0:T(8,128)(2,1)S(1)} %parent_step.1.parent_change.rest_0_), channel_id=1, source_target_pairs={{0,16},{8,24},{16,0},{24,8},{1,17},{9,25},{17,1},{25,9},{2,18},{10... | collective-permute-start | bytes 294920 | tf_op jit(solution)/shard_map/ppermute | solution.py:361
  23.0 6.9 %collective-permute-start.9 = (bf16[6,64,128]{2,1,0:T(8,128)(2,1)S(1)}, bf16[6,64,128]{2,1,0:T(8,128)(2,1)S(1)}, u32[]{:S(2)}, u32[]{:S(2)}) collective-permute-start(bf16[6,64,128]{2,1,0:T(8,128)(2,1)S(1)} %parent_step.1.parent_change.rest_0_), channel_id=1, source_target_pairs={{0,24},{8,16},{16,8},{24,0},{1,25},{9,17},{17,9},{25,1},{2,26},{10... | collective-permute-start | bytes 294920 | tf_op jit(solution)/shard_map/ppermute | solution.py:361
  23.6 2.1 %collective-permute-start.6 = (bf16[6,6,64,128]{3,2,1,0:T(8,128)(2,1)S(1)}, bf16[6,6,64,128]{3,2,1,0:T(8,128)(2,1)S(1)}, u32[]{:S(2)}, u32[]{:S(2)}) collective-permute-start(bf16[6,6,64,128]{3,2,1,0:T(8,128)(2,1)S(1)} %pack.1._), channel_id=1, source_target_pairs={{0,1},{1,0},{2,3},{3,2},{4,5},{5,4},{6,7},{7,6},{8,9},{9,8},{10,11... | collective-permute-start | bytes 1769480 | tf_op jit(solution)/shard_map/ppermute | solution.py:361

commit v4 on v3

--- a/solution.py
+++ b/solution.py
@@ -295,40 +295,37 @@
 
 
 def leaf_couple(boxes, table_in, own_half, other_half, _, *rest):
-    held_boxes, (out, token, table, held, order, sem) = rest[:-6], rest[-6:]
+    held_boxes, (out, token, held, order) = rest[:-4], rest[-4:]
+    table = table_in[...]
     count, links = out.shape[0], out.shape[1]
     half, rank = own_half.shape[:2]
     member = lax.axis_index("sub") % 2
-    copy = pltpu.make_async_copy(table_in, table, sem)
-    copy.start()
     token[...] = jnp.zeros(token.shape, token.dtype)
     size = 2 * held_boxes[0].shape[1]
     for box, source in zip(boxes, held_boxes):
         for at, place in enumerate(box):
             part = source[2 * at : 2 * at + 2]
             held[place * size : place * size + size] = part.reshape((size,) + part.shape[2:])
-    copy.wait()
     for at in range(count):
         own = at < half
         middle = own_half if own else other_half
         j = at % half
         t = (member if own else 1 - member) * half + j
+        rows = jnp.where(member == (0 if own else 1), table[:, j : j + 1], table[:, half + j : half + j + 1])
         for c in range(links):
             order[at % 4, pl.ds(c, rank // 2, stride=8), :] = couple(
-                middle[j, :, c * 128 : c * 128 + 128], held[table[c, t]]
+                middle[j, :, c * 128 : c * 128 + 128], held[rows[c, 0]]
             )
         write_rows(out, t, order.at[at % 4], links, rank // 2)
 
 
 def parent_couple(table_in, middle, _, *rest):
-    near, (out, table, held, order, sem) = rest[:-5], rest[-5:]
+    near, (out, held, order) = rest[:-3], rest[-3:]
+    table = table_in[...]
     count, links = out.shape[0], out.shape[1]
     rank = middle.shape[1]
-    copy = pltpu.make_async_copy(table_in, table, sem)
-    copy.start()
     for m in range(len(near)):
         held[m * count : m * count + count] = near[m][...]
-    copy.wait()
     for p in range(count):
         for c in range(links):
             order[p % 2, pl.ds(c, rank // 2, stride=8), :] = couple(
@@ -445,24 +442,20 @@
     boxes = [(0,), (1,)] + [(2 * m,) for m in range(1, chips)]
     boxes += [tuple(2 * m + 1 for m in range(1, chips))]
     new_leaf_blocks, after_leaves = call(
-        functools.partial(leaf_couple, boxes), [ANY] + [VMEM] * (3 + len(held)),
+        functools.partial(leaf_couple, boxes), [VMEM] * (4 + len(held)),
         [shape((count, links, rank * rank), BF16), token],
         [
-            pltpu.SMEM((links, count), jnp.int32),
             pltpu.VMEM((2 * chips * count, rank, old), BF16),
             pltpu.VMEM((4, 4 * rank, 2 * rank), F32),
-            dma(()),
         ],
         "leaf_couple", 4 + chips, 1 << 34, 12 * square,
     )(leaf_table, own_half, other_half, paused, *held)
     new_parent_blocks = call(
-        parent_couple, [ANY] + [VMEM] * (groups + 2),
+        parent_couple, [VMEM] * (groups + 3),
         shape((half, parent_links, rank * rank), BF16),
         [
-            pltpu.SMEM((parent_links, half), jnp.int32),
             pltpu.VMEM((groups * half, rank, old), BF16),
             pltpu.VMEM((2, 4 * rank, 2 * rank), F32),
-            dma(()),
         ],
         "parent_couple", 4 + groups, square, 4 * square,
     )(parent_table, parent_half, after_leaves, *parents_held)

time: 31.7 us -> 31.2 us (0.984)
  Pallas kernels: 14.8 us -> 13.8 us
  waiting for transfers between devices: 3.9 us -> 4.38 us
    pallas_call x2, Pallas kernels: 3.97 us -> 3.02 us  [the longest x1 1.86 us: shards(): call(functools.partial(leaf_couple, boxes), [VMEM] * (4 + len(held)), [sh...]
    ppermute x10, waiting for transfers between devices: 3.9 us -> 4.38 us  [swap(): return lax.ppermute(block, axis, [(i, i ^ mask) for i in range(count)])]
  transfers between devices with their start and end apart: 10 -> 10, of which waited for: 5 -> 5; matrix products, arithmetic and copies ran while one was open for 0% -> 0% of each run, Pallas kernels for 27% -> 26%
where the time goes in v4:
time: 31.2 us; the launch traced here: 31 us
  Pallas kernels  13.8 us (44%)
  starting transfers between devices  10.4 us (33%)
  waiting for transfers between devices  4.38 us (14%)
  local copies, waits for them, and re-layouts  1.71 us (5%)
  between operations  0.79 us (3%)
    ppermute x10, starting transfers between devices, swap(): return lax.ppermute(block, axis, [(i, i ^ mask) for i in range(count)])  10.4 us
    ppermute x10, waiting for transfers between devices, swap(): return lax.ppermute(block, axis, [(i, i ^ mask) for i in range(count)])  4.38 us
    pallas_call x1, Pallas kernels, shards(): call(leaf_step, [VMEM] * 6, [shape((2, half, rank, old), BF16), shape((ha...  4.14 us
    pallas_call x1, Pallas kernels, shards(): call(parent_step, [VMEM] * 3, shape((half, rank, old), BF16), tables, 'pa...  3.73 us
    pallas_call x1, Pallas kernels, shards(): call(functools.partial(leaf_couple, boxes), [VMEM] * (4 + len(held)), [sh...  1.86 us
    unnamed x22, local copies, waits for them, and re-layouts  1.71 us
    pallas_call x1, Pallas kernels, shards(): call(middle_other, [VMEM] * 5, [shape((count, rank, points), BF16), half_...  1.16 us
    pallas_call x1, Pallas kernels, shards(): call(parent_couple, [VMEM] * (groups + 3), shape((half, parent_links, ran...  1.16 us
  transfers between devices with their start and end apart: 10, of which 5 were waited for; matrix products, arithmetic and copies ran while one was open for 0% of the time, Pallas kernels for 26%

profile of v4, /device:TPU:0, one launch (start us, length us, event | category | flops | bytes accessed | tf_op | source)
XLA Modules:
  0.0 31.0 jit_solution(17824070506795081934)
XLA Ops:
  0.6 0.0 copy-start
  0.6 1.7 %copy-done = bf16[12,6,128,128]{3,2,1,0:T(8,128)(2,1)S(1)} copy-done((bf16[12,6,128,128]{3,2,1,0:T(8,128)(2,1)S(1)}, bf16[12,6,128,128]{3,2,1,0:T(8,128)(2,1)}, u32[]{:S(2)}) %copy-start) | copy-done | bytes 2359320
  2.3 0.0 copy-start.4
  2.3 0.0 copy-start.3
  2.3 0.0 copy-start.8
  2.3 0.0 copy-start.9
  2.3 0.0 copy-start.5
  2.3 0.5 %sent_weights.1 = f32[6,128,128]{2,1,0:T(8,128)S(1)} custom-call(bf16[12,6,128,128]{3,2,1,0:T(8,128)(2,1)S(1)} %copy-done), custom_call_target="tpu_custom_call" | custom-call | flops 150994944 | bytes 1179648 | tf_op jit(solution)/shard_map/sent_weights/pallas_call | solution.py:385
  2.8 0.5 %collective-permute-start = (f32[6,128,128]{2,1,0:T(8,128)S(1)}, f32[6,128,128]{2,1,0:T(8,128)S(1)}, u32[]{:S(2)}, u32[]{:S(2)}) collective-permute-start(f32[6,128,128]{2,1,0:T(8,128)S(1)} %sent_weights.1), channel_id=1, source_target_pairs={{0,1},{1,0},{2,3},{3,2},{4,5},{5,4},{6,7},{7,6},{8,9},{9,8},{10,11... | collective-permute-start | bytes 1179656 | tf_op jit(solution)/shard_map/ppermute | solution.py:358
  3.3 0.0 copy-done.4
  3.3 0.4 %collective-permute-start.1 = (bf16[12,128,128]{2,1,0:T(8,128)(2,1)S(1)}, bf16[12,128,128]{2,1,0:T(8,128)(2,1)S(1)}, u32[]{:S(2)}, u32[]{:S(2)}) collective-permute-start(bf16[12,128,128]{2,1,0:T(8,128)(2,1)S(1)} %copy-done.4), channel_id=1, source_target_pairs={{0,1},{1,0},{2,3},{3,2},{4,5},{5,4},{6,7},{7,6},{8,9},{9,8},{10,11... | collective-permute-start | bytes 1179656 | tf_op jit(solution)/shard_map/ppermute | solution.py:358
  3.8 0.0 copy-done.3
  3.8 0.0 copy-done.6
  3.8 0.0 copy-done.7
  3.8 0.0 copy-done.8
  3.8 0.0 copy-done.9
  3.8 0.0 copy-start.10
  3.8 0.0 copy-start.1
  3.8 0.0 copy-start.2
  3.8 0.7 %kept_weights.1 = (f32[6,128,128]{2,1,0:T(8,128)S(1)}, f32[6,128,128]{2,1,0:T(8,128)S(1)}, s32[6,12]{1,0:T(8,128)S(1)}, s32[3,6]{1,0:T(4,128)S(1)}) custom-call(bf16[12,6,128,128]{3,2,1,0:T(8,128)(2,1)S(1)} %copy-done, bf16[6,3,128,128]{3,2,1,0:T(8,128)(2,1)S(1)} %copy-done.3, s32[6,12]{1,0:T(8,128)S(1)} %bitcast.4, s32[6,12]{1,0:T(8,128)S(1)} %bitcast.5, ...), custom_call_target="tpu_custom_call" | custom-call | flops 226492416 | bytes 4718592 | tf_op jit(solution)/shard_map/kept_weights/pallas_call | solution.py:390
  4.5 0.2 collective-permute-done.other
  4.7 0.6 %collective-permute-done.1.other_transfers = bf16[12,128,128]{2,1,0:T(8,128)(2,1)S(1)} collective-permute-done((bf16[12,128,128]{2,1,0:T(8,128)(2,1)S(1)}, bf16[12,128,128]{2,1,0:T(8,128)(2,1)S(1)}, u32[]{:S(2)}, u32[]{:S(2)}) %collective-permute-start.1) | collective-permute-done | bytes 393248 | tf_op jit(solution)/shard_map/ppermute | solution.py:358
  5.3 0.0 copy-done.5
  5.3 4.1 %leaf_step.1 = (bf16[2,6,64,128]{3,2,1,0:T(8,128)(2,1)S(1)}, f32[6,2,64,128]{3,2,1,0:T(8,128)S(1)}) custom-call(f32[6,128,128]{2,1,0:T(8,128)S(1)} %get-tuple-element.17.own, f32[6,128,128]{2,1,0:T(8,128)S(1)} %collective-permute-done.other, f32[6,128,128]{2,1,0:T(8,128)S(1)} %get-tuple-element.18.parent, bf16[12,128,128]{2,1,0:T(8,128)(2,1)S(1)} %copy-done.4, ...), custom_call_target="tpu_custom_call" | custom-call | flops 503316480 | bytes 786432 | tf_op jit(solution)/shard_map/leaf_step/pallas_call | solution.py:405
  9.4 0.4 %collective-permute-start.2 = (bf16[2,6,64,128]{3,2,1,0:T(8,128)(2,1)S(1)}, bf16[2,6,64,128]{3,2,1,0:T(8,128)(2,1)S(1)}, u32[]{:S(2)}, u32[]{:S(2)}) collective-permute-start(bf16[2,6,64,128]{3,2,1,0:T(8,128)(2,1)S(1)} %get-tuple-element.19.change.rest_0_), channel_id=1, source_target_pairs={{0,1},{1,0},{2,3},{3,2},{4,5},{5,4},{6,7},{7,6},{8,9},{9,8},{10,11... | collective-permute-start | bytes 589832 | tf_op jit(solution)/shard_map/ppermute | solution.py:358
  9.8 2.6 %collective-permute-start.3 = (bf16[2,6,64,128]{3,2,1,0:T(8,128)(2,1)S(1)}, bf16[2,6,64,128]{3,2,1,0:T(8,128)(2,1)S(1)}, u32[]{:S(2)}, u32[]{:S(2)}) collective-permute-start(bf16[2,6,64,128]{3,2,1,0:T(8,128)(2,1)S(1)} %get-tuple-element.19.change.rest_0_), channel_id=1, source_target_pairs={{0,2},{1,3},{2,0},{3,1},{4,6},{5,7},{6,4},{7,5},{8,10},{9,11},{10,... | collective-permute-start | bytes 589832 | tf_op jit(solution)/shard_map/ppermute | solution.py:358
  12.5 1.5 %collective-permute-start.4 = (bf16[2,6,64,128]{3,2,1,0:T(8,128)(2,1)S(1)}, bf16[2,6,64,128]{3,2,1,0:T(8,128)(2,1)S(1)}, u32[]{:S(2)}, u32[]{:S(2)}) collective-permute-start(bf16[2,6,64,128]{3,2,1,0:T(8,128)(2,1)S(1)} %get-tuple-element.19.change.rest_0_), channel_id=1, source_target_pairs={{0,4},{1,5},{2,6},{3,7},{4,0},{5,1},{6,2},{7,3},{8,12},{9,13},{10,... | collective-permute-start | bytes 589832 | tf_op jit(solution)/shard_map/ppermute | solution.py:358
  14.0 0.0 collective-permute-start.5
  14.0 0.0 copy-done.10
  14.0 3.7 %parent_step.1.parent_change.rest_0_ = bf16[6,64,128]{2,1,0:T(8,128)(2,1)S(1)} custom-call(f32[6,128,128]{2,1,0:T(8,128)S(1)} %get-tuple-element.18.parent, f32[6,2,64,128]{3,2,1,0:T(8,128)S(1)} %get-tuple-element.20.stacked, f32[64,128]{1,0:T(8,128)S(1)} %copy-done.10), custom_call_target="tpu_custom_call" | custom-call | flops 251658240 | bytes 786432 | tf_op jit(solution)/shard_map/parent_step/pallas_call | solution.py:413
  17.7 2.1 %collective-permute-start.7 = (bf16[6,64,128]{2,1,0:T(8,128)(2,1)S(1)}, bf16[6,64,128]{2,1,0:T(8,128)(2,1)S(1)}, u32[]{:S(2)}, u32[]{:S(2)}) collective-permute-start(bf16[6,64,128]{2,1,0:T(8,128)(2,1)S(1)} %parent_step.1.parent_change.rest_0_), channel_id=1, source_target_pairs={{0,8},{8,0},{16,24},{24,16},{1,9},{9,1},{17,25},{25,17},{2,10},{10... | collective-permute-start | bytes 294920 | tf_op jit(solution)/shard_map/ppermute | solution.py:358
  19.9 0.0 collective-permute-done.2._.swapped.rest_1_
  19.9 2.6 %collective-permute-start.8 = (bf16[6,64,128]{2,1,0:T(8,128)(2,1)S(1)}, bf16[6,64,128]{2,1,0:T(8,128)(2,1)S(1)}, u32[]{:S(2)}, u32[]{:S(2)}) collective-permute-start(bf16[6,64,128]{2,1,0:T(8,128)(2,1)S(1)} %parent_step.1.parent_change.rest_0_), channel_id=1, source_target_pairs={{0,16},{8,24},{16,0},{24,8},{1,17},{9,25},{17,1},{25,9},{2,18},{10... | collective-permute-start | bytes 294920 | tf_op jit(solution)/shard_map/ppermute | solution.py:358
  22.5 0.0 copy-done.1
  22.5 0.0 copy-done.2
  22.5 0.5 %middle_own.1 = (bf16[6,64,256]{2,1,0:T(8,128)(2,1)S(1)}, bf16[6,64,768]{2,1,0:T(8,128)(2,1)S(1)}, bf16[6,64,384]{2,1,0:T(8,128)(2,1)S(1)}, f32[8,128]{1,0:T(8,128)S(1)}) custom-call(bf16[2,6,64,128]{3,2,1,0:T(8,128)(2,1)S(1)} %get-tuple-element.19.change.rest_0_, bf16[6,64,128]{2,1,0:T(8,128)(2,1)S(1)} %parent_step.1.parent_change.rest_0_, ...), custom_call_target="tpu_custom_call" | custom-call | flops 17179869184 | bytes 98304 | tf_op jit(solution)/shard_map/middle_own/pallas_call | solution.py:422
  23.0 0.0 collective-permute-done.3.refs_1_.rest_2_
  23.0 0.1 collective-permute-start.9
  23.1 0.5 %collective-permute-done.4.refs_2_.rest_3_ = bf16[2,6,64,128]{3,2,1,0:T(8,128)(2,1)S(1)} collective-permute-done((bf16[2,6,64,128]{3,2,1,0:T(8,128)(2,1)S(1)}, bf16[2,6,64,128]{3,2,1,0:T(8,128)(2,1)S(1)}, u32[]{:S(2)}, u32[]{:S(2)}) %collective-permute-start.4) | collective-permute-done | bytes 196640 | tf_op jit(solution)/shard_map/ppermute | solution.py:358
  23.6 0.0 collective-permute-done.5.refs_3_.rest_4_
  23.6 0.1 collective-permute-start.6
  23.7 1.2 %middle_other.1 = (bf16[12,64,256]{2,1,0:T(8,128)(2,1)}, bf16[6,64,768]{2,1,0:T(8,128)(2,1)S(1)}) custom-call(bf16[2,6,64,128]{3,2,1,0:T(8,128)(2,1)S(1)} %collective-permute-done.2._.swapped.rest_1_, bf16[12,256,128]{2,1,0:T(8,128)(2,1)S(1)} %copy-done.2, bf16[12,6,128,128]{3,2,1,0:T(8,128)(2,1)S(1)} %copy-done.1, ...), custom_call_target="tpu_custom_call" | custom-call | flops 98304 | bytes 98304 | tf_op jit(solution)/shard_map/middle_other/pallas_call | solution.py:435
  24.9 0.8 %collective-permute-done.6.rest_5_ = bf16[6,6,64,128]{3,2,1,0:T(8,128)(2,1)S(1)} collective-permute-done((bf16[6,6,64,128]{3,2,1,0:T(8,128)(2,1)S(1)}, bf16[6,6,64,128]{3,2,1,0:T(8,128)(2,1)S(1)}, u32[]{:S(2)}, u32[]{:S(2)}) %collective-permute-start.6) | collective-permute-done | bytes 589856 | tf_op jit(solution)/shard_map/ppermute | solution.py:358
  25.7 1.9 %leaf_couple.1 = (bf16[12,6,4096]{2,1,0:T(8,128)(2,1)}, f32[8,128]{1,0:T(8,128)S(1)}) custom-call(s32[6,12]{1,0:T(8,128)S(1)} %get-tuple-element.24.table_in, bf16[6,64,768]{2,1,0:T(8,128)(2,1)S(1)} %get-tuple-element.25.own_half, bf16[6,64,768]{2,1,0:T(8,128)(2,1)S(1)} %get-tuple-element.26.other_half, f32[8,128]{1,0:T(8,128)S(1)} %pause.1._, ...), custom_call_target="tpu_custom_call" | custom-call | flops 17179869184 | bytes 1179648 | tf_op jit(solution)/shard_map/leaf_couple/pallas_call | solution.py:444
  27.6 0.0 collective-permute-done.7.rest_1_
  27.6 2.3 %collective-permute-done.8.rest_2_ = bf16[6,64,128]{2,1,0:T(8,128)(2,1)S(1)} collective-permute-done((bf16[6,64,128]{2,1,0:T(8,128)(2,1)S(1)}, bf16[6,64,128]{2,1,0:T(8,128)(2,1)S(1)}, u32[]{:S(2)}, u32[]{:S(2)}) %collective-permute-start.8) | collective-permute-done | bytes 98336 | tf_op jit(solution)/shard_map/ppermute | solution.py:358
  29.9 0.0 collective-permute-done.9.rest_3_
  29.9 1.2 %parent_couple.1 = bf16[6,3,4096]{2,1,0:T(4,128)(2,1)} custom-call(s32[3,6]{1,0:T(4,128)S(1)} %get-tuple-element.28.table_in, bf16[6,64,384]{2,1,0:T(8,128)(2,1)S(1)} %get-tuple-element.29.middle, f32[8,128]{1,0:T(8,128)S(1)} %get-tuple-element.30._, bf16[6,64,128]{2,1,0:T(8,128)(2,1)S(1)} %parent_step.1.parent_change.rest_0_, ...), custom_call_target="tpu_custom_call" | custom-call | flops 98304 | bytes 393216 | tf_op jit(solution)/shard_map/parent_couple/pallas_call | solution.py:453
  (4 shorter events, 0.0 us)
Async XLA Ops:
  0.6 1.7 %copy-start = (bf16[12,6,128,128]{3,2,1,0:T(8,128)(2,1)S(1)}, bf16[12,6,128,128]{3,2,1,0:T(8,128)(2,1)}, u32[]{:S(2)}) copy-start(bf16[12,6,128,128]{3,2,1,0:T(8,128)(2,1)} %blocks.7) | copy-start | bytes 7077892
  2.3 1.0 %copy-start.4 = (bf16[12,128,128]{2,1,0:T(8,128)(2,1)S(1)}, bf16[12,128,128]{2,1,0:T(8,128)(2,1)}, u32[]{:S(2)}) copy-start(bf16[12,128,128]{2,1,0:T(8,128)(2,1)} %transfers.1) | copy-start | bytes 1179652
  2.3 1.4 %copy-start.3 = (bf16[6,3,128,128]{3,2,1,0:T(8,128)(2,1)S(1)}, bf16[6,3,128,128]{3,2,1,0:T(8,128)(2,1)}, u32[]{:S(2)}) copy-start(bf16[6,3,128,128]{3,2,1,0:T(8,128)(2,1)} %parents.3) | copy-start | bytes 1769476
  2.3 1.4 %copy-start.6 = (s32[12,6]{0,1:T(8,128)S(1)}, s32[12,6]{0,1:T(8,128)}, u32[]{:S(2)}) copy-start(s32[12,6]{0,1:T(8,128)} %param.13) | copy-start | bytes 868
  2.3 1.5 %copy-start.7 = (s32[12,6]{0,1:T(8,128)S(1)}, s32[12,6]{0,1:T(8,128)}, u32[]{:S(2)}) copy-start(s32[12,6]{0,1:T(8,128)} %param.14) | copy-start | bytes 868
  2.3 1.4 %copy-start.8 = (s32[6,3]{0,1:T(4,128)S(1)}, s32[6,3]{0,1:T(4,128)}, u32[]{:S(2)}) copy-start(s32[6,3]{0,1:T(4,128)} %param.16) | copy-start | bytes 220
  2.3 1.4 %copy-start.9 = (s32[6,3]{0,1:T(4,128)S(1)}, s32[6,3]{0,1:T(4,128)}, u32[]{:S(2)}) copy-start(s32[6,3]{0,1:T(4,128)} %param.17) | copy-start | bytes 220
  2.3 2.9 %copy-start.5 = (f32[64,128]{1,0:T(8,128)S(1)}, f32[64,128]{1,0:T(8,128)}, u32[]{:S(2)}) copy-start(f32[64,128]{1,0:T(8,128)} %start.2) | copy-start | bytes 98308
  2.8 1.9 %collective-permute-start = (f32[6,128,128]{2,1,0:T(8,128)S(1)}, f32[6,128,128]{2,1,0:T(8,128)S(1)}, u32[]{:S(2)}, u32[]{:S(2)}) collective-permute-start(f32[6,128,128]{2,1,0:T(8,128)S(1)} %sent_weights.1), channel_id=1, source_target_pairs={{0,1},{1,0},{2,3},{3,2},{4,5},{5,4},{6,7},{7,6},{8,9},{9,8},{10,11... | collective-permute-start | bytes 1179656 | tf_op jit(solution)/shard_map/ppermute | solution.py:358
  3.3 1.9 %collective-permute-start.1 = (bf16[12,128,128]{2,1,0:T(8,128)(2,1)S(1)}, bf16[12,128,128]{2,1,0:T(8,128)(2,1)S(1)}, u32[]{:S(2)}, u32[]{:S(2)}) collective-permute-start(bf16[12,128,128]{2,1,0:T(8,128)(2,1)S(1)} %copy-done.4), channel_id=1, source_target_pairs={{0,1},{1,0},{2,3},{3,2},{4,5},{5,4},{6,7},{7,6},{8,9},{9,8},{10,11... | collective-permute-start | bytes 1179656 | tf_op jit(solution)/shard_map/ppermute | solution.py:358
  3.8 10.2 %copy-start.10 = (f32[64,128]{1,0:T(8,128)S(1)}, f32[64,128]{1,0:T(8,128)}, u32[]{:S(2)}) copy-start(f32[64,128]{1,0:T(8,128)} %start.3) | copy-start | bytes 98308
  3.8 18.7 %copy-start.1 = (bf16[12,6,128,128]{3,2,1,0:T(8,128)(2,1)S(1)}, bf16[12,6,128,128]{3,2,1,0:T(8,128)(2,1)}, u32[]{:S(2)}) copy-start(bf16[12,6,128,128]{3,2,1,0:T(8,128)(2,1)} %blocks.7) | copy-start | bytes 7077892
  3.8 18.7 %copy-start.2 = (bf16[12,256,128]{2,1,0:T(8,128)(2,1)S(1)}, bf16[12,256,128]{2,1,0:T(8,128)(2,1)}, u32[]{:S(2)}) copy-start(bf16[12,256,128]{2,1,0:T(8,128)(2,1)} %bases.3) | copy-start | bytes 2359300
  9.4 10.4 %collective-permute-start.2 = (bf16[2,6,64,128]{3,2,1,0:T(8,128)(2,1)S(1)}, bf16[2,6,64,128]{3,2,1,0:T(8,128)(2,1)S(1)}, u32[]{:S(2)}, u32[]{:S(2)}) collective-permute-start(bf16[2,6,64,128]{3,2,1,0:T(8,128)(2,1)S(1)} %get-tuple-element.19.change.rest_0_), channel_id=1, source_target_pairs={{0,1},{1,0},{2,3},{3,2},{4,5},{5,4},{6,7},{7,6},{8,9},{9,8},{10,11... | collective-permute-start | bytes 589832 | tf_op jit(solution)/shard_map/ppermute | solution.py:358
  9.8 13.2 %collective-permute-start.3 = (bf16[2,6,64,128]{3,2,1,0:T(8,128)(2,1)S(1)}, bf16[2,6,64,128]{3,2,1,0:T(8,128)(2,1)S(1)}, u32[]{:S(2)}, u32[]{:S(2)}) collective-permute-start(bf16[2,6,64,128]{3,2,1,0:T(8,128)(2,1)S(1)} %get-tuple-element.19.change.rest_0_), channel_id=1, source_target_pairs={{0,2},{1,3},{2,0},{3,1},{4,6},{5,7},{6,4},{7,5},{8,10},{9,11},{10,... | collective-permute-start | bytes 589832 | tf_op jit(solution)/shard_map/ppermute | solution.py:358
  12.5 11.1 %collective-permute-start.4 = (bf16[2,6,64,128]{3,2,1,0:T(8,128)(2,1)S(1)}, bf16[2,6,64,128]{3,2,1,0:T(8,128)(2,1)S(1)}, u32[]{:S(2)}, u32[]{:S(2)}) collective-permute-start(bf16[2,6,64,128]{3,2,1,0:T(8,128)(2,1)S(1)} %get-tuple-element.19.change.rest_0_), channel_id=1, source_target_pairs={{0,4},{1,5},{2,6},{3,7},{4,0},{5,1},{6,2},{7,3},{8,12},{9,13},{10,... | collective-permute-start | bytes 589832 | tf_op jit(solution)/shard_map/ppermute | solution.py:358
  14.0 9.6 %collective-permute-start.5 = (bf16[2,6,64,128]{3,2,1,0:T(8,128)(2,1)S(1)}, bf16[2,6,64,128]{3,2,1,0:T(8,128)(2,1)S(1)}, u32[]{:S(2)}, u32[]{:S(2)}) collective-permute-start(bf16[2,6,64,128]{3,2,1,0:T(8,128)(2,1)S(1)} %get-tuple-element.19.change.rest_0_), channel_id=1, source_target_pairs={{0,6},{1,7},{2,4},{3,5},{4,2},{5,3},{6,0},{7,1},{8,14},{9,15},{10,... | collective-permute-start | bytes 589832 | tf_op jit(solution)/shard_map/ppermute | solution.py:358
  17.7 9.8 %collective-permute-start.7 = (bf16[6,64,128]{2,1,0:T(8,128)(2,1)S(1)}, bf16[6,64,128]{2,1,0:T(8,128)(2,1)S(1)}, u32[]{:S(2)}, u32[]{:S(2)}) collective-permute-start(bf16[6,64,128]{2,1,0:T(8,128)(2,1)S(1)} %parent_step.1.parent_change.rest_0_), channel_id=1, source_target_pairs={{0,8},{8,0},{16,24},{24,16},{1,9},{9,1},{17,25},{25,17},{2,10},{10... | collective-permute-start | bytes 294920 | tf_op jit(solution)/shard_map/ppermute | solution.py:358
  19.9 10.0 %collective-permute-start.8 = (bf16[6,64,128]{2,1,0:T(8,128)(2,1)S(1)}, bf16[6,64,128]{2,1,0:T(8,128)(2,1)S(1)}, u32[]{:S(2)}, u32[]{:S(2)}) collective-permute-start(bf16[6,64,128]{2,1,0:T(8,128)(2,1)S(1)} %parent_step.1.parent_change.rest_0_), channel_id=1, source_target_pairs={{0,16},{8,24},{16,0},{24,8},{1,17},{9,25},{17,1},{25,9},{2,18},{10... | collective-permute-start | bytes 294920 | tf_op jit(solution)/shard_map/ppermute | solution.py:358
  23.0 6.9 %collective-permute-start.9 = (bf16[6,64,128]{2,1,0:T(8,128)(2,1)S(1)}, bf16[6,64,128]{2,1,0:T(8,128)(2,1)S(1)}, u32[]{:S(2)}, u32[]{:S(2)}) collective-permute-start(bf16[6,64,128]{2,1,0:T(8,128)(2,1)S(1)} %parent_step.1.parent_change.rest_0_), channel_id=1, source_target_pairs={{0,24},{8,16},{16,8},{24,0},{1,25},{9,17},{17,9},{25,1},{2,26},{10... | collective-permute-start | bytes 294920 | tf_op jit(solution)/shard_map/ppermute | solution.py:358
  23.6 2.1 %collective-permute-start.6 = (bf16[6,6,64,128]{3,2,1,0:T(8,128)(2,1)S(1)}, bf16[6,6,64,128]{3,2,1,0:T(8,128)(2,1)S(1)}, u32[]{:S(2)}, u32[]{:S(2)}) collective-permute-start(bf16[6,6,64,128]{3,2,1,0:T(8,128)(2,1)S(1)} %pack.1._), channel_id=1, source_target_pairs={{0,1},{1,0},{2,3},{3,2},{4,5},{5,4},{6,7},{7,6},{8,9},{9,8},{10,11... | collective-permute-start | bytes 1769480 | tf_op jit(solution)/shard_map/ppermute | solution.py:358

commit v5 on v4

--- a/solution.py
+++ b/solution.py
@@ -157,7 +157,7 @@
 
 
 def kept_weights(
-    blocks, parents, devs, slots, groups, parent_slots,
+    blocks, parents, devs, slots, groups, parent_slots, _,
     weight, parent_weight, leaf_table, parent_table,
 ):
     half = weight.shape[0]
@@ -388,13 +388,14 @@
     )(leaf_blocks)
     other = swap(sent, "sub", 1)
     own, parent_weight, leaf_table, parent_table = call(
-        kept_weights, [VMEM] * 6,
+        kept_weights, [VMEM] * 7,
         [weights, weights, shape((links, count), jnp.int32), shape((parent_links, half), jnp.int32)],
         [],
         "kept_weights", 8, 2 * (links + parent_links) * square * old, 8 * links * square,
     )(
         leaf_blocks, parent_blocks,
         leaf_partner_dev.T, leaf_partner_slot.T, parent_partner_group.T, parent_partner_slot.T,
+        other_transfers,
     )
     tables = [
         pltpu.VMEM((8 * rank, 2 * rank), F32),

time: 31.2 us -> 30.9 us (level)
  local copies, waits for them, and re-layouts: 1.71 us -> 2.12 us
  waiting for transfers between devices: 4.38 us -> 4.01 us
    unnamed x22, local copies, waits for them, and re-layouts: 1.71 us -> 2.12 us
    ppermute x10, waiting for transfers between devices: 4.38 us -> 4.01 us  [swap(): return lax.ppermute(block, axis, [(i, i ^ mask) for i in range(count)])]
  transfers between devices with their start and end apart: 10 -> 10, of which waited for: 5 -> 4; matrix products, arithmetic and copies ran while one was open for 0% -> 0% of each run, Pallas kernels for 26% -> 28%
where the time goes in v5:
time: 30.9 us; the launch traced here: 30.8 us
  Pallas kernels  13.8 us (45%)
  starting transfers between devices  10.1 us (33%)
  waiting for transfers between devices  4.01 us (13%)
  local copies, waits for them, and re-layouts  2.12 us (7%)
  between operations  0.77 us (2%)
    ppermute x10, starting transfers between devices, swap(): return lax.ppermute(block, axis, [(i, i ^ mask) for i in range(count)])  10.1 us
    pallas_call x1, Pallas kernels, shards(): call(leaf_step, [VMEM] * 6, [shape((2, half, rank, old), BF16), shape((ha...  4.14 us
    ppermute x10, waiting for transfers between devices, swap(): return lax.ppermute(block, axis, [(i, i ^ mask) for i in range(count)])  4.01 us
    pallas_call x1, Pallas kernels, shards(): call(parent_step, [VMEM] * 3, shape((half, rank, old), BF16), tables, 'pa...  3.73 us
    unnamed x22, local copies, waits for them, and re-layouts  2.12 us
    pallas_call x1, Pallas kernels, shards(): call(functools.partial(leaf_couple, boxes), [VMEM] * (4 + len(held)), [sh...  1.86 us
    pallas_call x1, Pallas kernels, shards(): call(middle_other, [VMEM] * 5, [shape((count, rank, points), BF16), half_...  1.17 us
    pallas_call x1, Pallas kernels, shards(): call(parent_couple, [VMEM] * (groups + 3), shape((half, parent_links, ran...  1.16 us
  transfers between devices with their start and end apart: 10, of which 4 were waited for; matrix products, arithmetic and copies ran while one was open for 0% of the time, Pallas kernels for 28%

profile of v5, /device:TPU:0, one launch (start us, length us, event | category | flops | bytes accessed | tf_op | source)
XLA Modules:
  0.0 30.8 jit_solution(463991680593965749)
XLA Ops:
  0.6 0.5 %collective-permute-start = (bf16[12,128,128]{2,1,0:T(8,128)(2,1)}, bf16[12,128,128]{2,1,0:T(8,128)(2,1)S(1)}, u32[]{:S(2)}, u32[]{:S(2)}) collective-permute-start(bf16[12,128,128]{2,1,0:T(8,128)(2,1)} %transfers.1), channel_id=1, source_target_pairs={{0,1},{1,0},{2,3},{3,2},{4,5},{5,4},{6,7},{7,6},{8,9},{9,8},{10,11... | collective-permute-start | bytes 1179656 | tf_op jit(solution)/shard_map/ppermute | solution.py:358
  1.1 0.0 copy-start
  1.2 1.7 %copy-done = bf16[12,6,128,128]{3,2,1,0:T(8,128)(2,1)S(1)} copy-done((bf16[12,6,128,128]{3,2,1,0:T(8,128)(2,1)S(1)}, bf16[12,6,128,128]{3,2,1,0:T(8,128)(2,1)}, u32[]{:S(2)}) %copy-start) | copy-done | bytes 2359320
  2.8 0.0 copy-start.3
  2.8 0.0 copy-start.6
  2.8 0.0 copy-start.9
  2.8 0.5 %sent_weights.1 = f32[6,128,128]{2,1,0:T(8,128)S(1)} custom-call(bf16[12,6,128,128]{3,2,1,0:T(8,128)(2,1)S(1)} %copy-done), custom_call_target="tpu_custom_call" | custom-call | flops 150994944 | bytes 1179648 | tf_op jit(solution)/shard_map/sent_weights/pallas_call | solution.py:385
  3.3 0.0 copy-start.4
  3.3 0.0 copy-start.5
  3.3 0.1 collective-permute-start.1
  3.5 0.0 collective-permute-done._.other_transfers
  3.5 0.4 %copy-done.3 = bf16[6,3,128,128]{3,2,1,0:T(8,128)(2,1)S(1)} copy-done((bf16[6,3,128,128]{3,2,1,0:T(8,128)(2,1)S(1)}, bf16[6,3,128,128]{3,2,1,0:T(8,128)(2,1)}, u32[]{:S(2)}) %copy-start.3) | copy-done | bytes 589848
  3.9 0.0 copy-done.6
  3.9 0.0 copy-done.7
  3.9 0.0 copy-done.8
  3.9 0.0 copy-done.9
  3.9 0.0 copy-start.10
  3.9 0.0 copy-start.1
  3.9 0.0 copy-start.2
  3.9 0.7 %kept_weights.1 = (f32[6,128,128]{2,1,0:T(8,128)S(1)}, f32[6,128,128]{2,1,0:T(8,128)S(1)}, s32[6,12]{1,0:T(8,128)S(1)}, s32[3,6]{1,0:T(4,128)S(1)}) custom-call(bf16[12,6,128,128]{3,2,1,0:T(8,128)(2,1)S(1)} %copy-done, bf16[6,3,128,128]{3,2,1,0:T(8,128)(2,1)S(1)} %copy-done.3, s32[6,12]{1,0:T(8,128)S(1)} %bitcast.4, s32[6,12]{1,0:T(8,128)S(1)} %bitcast.5, ...), custom_call_target="tpu_custom_call" | custom-call | flops 226492416 | bytes 4718592 | tf_op jit(solution)/shard_map/kept_weights/pallas_call | solution.py:390
  4.6 0.5 %collective-permute-done.1.other = f32[6,128,128]{2,1,0:T(8,128)S(1)} collective-permute-done((f32[6,128,128]{2,1,0:T(8,128)S(1)}, f32[6,128,128]{2,1,0:T(8,128)S(1)}, u32[]{:S(2)}, u32[]{:S(2)}) %collective-permute-start.1) | collective-permute-done | bytes 393248 | tf_op jit(solution)/shard_map/ppermute | solution.py:358
  5.1 0.0 copy-done.4
  5.1 0.0 copy-done.5
  5.1 4.1 %leaf_step.1 = (bf16[2,6,64,128]{3,2,1,0:T(8,128)(2,1)S(1)}, f32[6,2,64,128]{3,2,1,0:T(8,128)S(1)}) custom-call(f32[6,128,128]{2,1,0:T(8,128)S(1)} %get-tuple-element.17.own, f32[6,128,128]{2,1,0:T(8,128)S(1)} %collective-permute-done.1.other, f32[6,128,128]{2,1,0:T(8,128)S(1)} %get-tuple-element.18.parent, bf16[12,128,128]{2,1,0:T(8,128)(2,1)S(1)} %copy-done.4, ...), custom_call_target="tpu_custom_call" | custom-call | flops 503316480 | bytes 786432 | tf_op jit(solution)/shard_map/leaf_step/pallas_call | solution.py:406
  9.3 0.2 collective-permute-start.2
  9.5 2.9 %collective-permute-start.3 = (bf16[2,6,64,128]{3,2,1,0:T(8,128)(2,1)S(1)}, bf16[2,6,64,128]{3,2,1,0:T(8,128)(2,1)S(1)}, u32[]{:S(2)}, u32[]{:S(2)}) collective-permute-start(bf16[2,6,64,128]{3,2,1,0:T(8,128)(2,1)S(1)} %get-tuple-element.19.change.rest_0_), channel_id=1, source_target_pairs={{0,2},{1,3},{2,0},{3,1},{4,6},{5,7},{6,4},{7,5},{8,10},{9,11},{10,... | collective-permute-start | bytes 589832 | tf_op jit(solution)/shard_map/ppermute | solution.py:358
  12.3 1.5 %collective-permute-start.4 = (bf16[2,6,64,128]{3,2,1,0:T(8,128)(2,1)S(1)}, bf16[2,6,64,128]{3,2,1,0:T(8,128)(2,1)S(1)}, u32[]{:S(2)}, u32[]{:S(2)}) collective-permute-start(bf16[2,6,64,128]{3,2,1,0:T(8,128)(2,1)S(1)} %get-tuple-element.19.change.rest_0_), channel_id=1, source_target_pairs={{0,4},{1,5},{2,6},{3,7},{4,0},{5,1},{6,2},{7,3},{8,12},{9,13},{10,... | collective-permute-start | bytes 589832 | tf_op jit(solution)/shard_map/ppermute | solution.py:358
  13.9 0.0 collective-permute-start.5
  13.9 0.0 copy-done.10
  13.9 3.7 %parent_step.1.parent_change.rest_0_ = bf16[6,64,128]{2,1,0:T(8,128)(2,1)S(1)} custom-call(f32[6,128,128]{2,1,0:T(8,128)S(1)} %get-tuple-element.18.parent, f32[6,2,64,128]{3,2,1,0:T(8,128)S(1)} %get-tuple-element.20.stacked, f32[64,128]{1,0:T(8,128)S(1)} %copy-done.10), custom_call_target="tpu_custom_call" | custom-call | flops 251658240 | bytes 786432 | tf_op jit(solution)/shard_map/parent_step/pallas_call | solution.py:414
  17.6 2.1 %collective-permute-start.7 = (bf16[6,64,128]{2,1,0:T(8,128)(2,1)S(1)}, bf16[6,64,128]{2,1,0:T(8,128)(2,1)S(1)}, u32[]{:S(2)}, u32[]{:S(2)}) collective-permute-start(bf16[6,64,128]{2,1,0:T(8,128)(2,1)S(1)} %parent_step.1.parent_change.rest_0_), channel_id=1, source_target_pairs={{0,8},{8,0},{16,24},{24,16},{1,9},{9,1},{17,25},{25,17},{2,10},{10... | collective-permute-start | bytes 294920 | tf_op jit(solution)/shard_map/ppermute | solution.py:358
  19.7 0.0 collective-permute-done.2._.swapped.rest_1_
  19.7 2.6 %collective-permute-start.8 = (bf16[6,64,128]{2,1,0:T(8,128)(2,1)S(1)}, bf16[6,64,128]{2,1,0:T(8,128)(2,1)S(1)}, u32[]{:S(2)}, u32[]{:S(2)}) collective-permute-start(bf16[6,64,128]{2,1,0:T(8,128)(2,1)S(1)} %parent_step.1.parent_change.rest_0_), channel_id=1, source_target_pairs={{0,16},{8,24},{16,0},{24,8},{1,17},{9,25},{17,1},{25,9},{2,18},{10... | collective-permute-start | bytes 294920 | tf_op jit(solution)/shard_map/ppermute | solution.py:358
  22.3 0.0 copy-done.1
  22.3 0.0 copy-done.2
  22.3 0.5 %middle_own.1 = (bf16[6,64,256]{2,1,0:T(8,128)(2,1)S(1)}, bf16[6,64,768]{2,1,0:T(8,128)(2,1)S(1)}, bf16[6,64,384]{2,1,0:T(8,128)(2,1)S(1)}, f32[8,128]{1,0:T(8,128)S(1)}) custom-call(bf16[2,6,64,128]{3,2,1,0:T(8,128)(2,1)S(1)} %get-tuple-element.19.change.rest_0_, bf16[6,64,128]{2,1,0:T(8,128)(2,1)S(1)} %parent_step.1.parent_change.rest_0_, ...), custom_call_target="tpu_custom_call" | custom-call | flops 17179869184 | bytes 98304 | tf_op jit(solution)/shard_map/middle_own/pallas_call | solution.py:423
  22.9 0.0 collective-permute-done.3.refs_1_.rest_2_
  22.9 0.1 collective-permute-start.9
  23.0 0.3 collective-permute-done.4.refs_2_.rest_3_
  23.2 0.0 collective-permute-done.5.refs_3_.rest_4_
  23.3 0.1 collective-permute-start.6
  23.4 1.2 %middle_other.1 = (bf16[12,64,256]{2,1,0:T(8,128)(2,1)}, bf16[6,64,768]{2,1,0:T(8,128)(2,1)S(1)}) custom-call(bf16[2,6,64,128]{3,2,1,0:T(8,128)(2,1)S(1)} %collective-permute-done.2._.swapped.rest_1_, bf16[12,256,128]{2,1,0:T(8,128)(2,1)S(1)} %copy-done.2, bf16[12,6,128,128]{3,2,1,0:T(8,128)(2,1)S(1)} %copy-done.1, ...), custom_call_target="tpu_custom_call" | custom-call | flops 98304 | bytes 98304 | tf_op jit(solution)/shard_map/middle_other/pallas_call | solution.py:436
  24.5 0.8 %collective-permute-done.6.rest_5_ = bf16[6,6,64,128]{3,2,1,0:T(8,128)(2,1)S(1)} collective-permute-done((bf16[6,6,64,128]{3,2,1,0:T(8,128)(2,1)S(1)}, bf16[6,6,64,128]{3,2,1,0:T(8,128)(2,1)S(1)}, u32[]{:S(2)}, u32[]{:S(2)}) %collective-permute-start.6) | collective-permute-done | bytes 589856 | tf_op jit(solution)/shard_map/ppermute | solution.py:358
  25.3 1.9 %leaf_couple.1 = (bf16[12,6,4096]{2,1,0:T(8,128)(2,1)}, f32[8,128]{1,0:T(8,128)S(1)}) custom-call(s32[6,12]{1,0:T(8,128)S(1)} %get-tuple-element.24.table_in, bf16[6,64,768]{2,1,0:T(8,128)(2,1)S(1)} %get-tuple-element.25.own_half, bf16[6,64,768]{2,1,0:T(8,128)(2,1)S(1)} %get-tuple-element.26.other_half, f32[8,128]{1,0:T(8,128)S(1)} %pause.1._, ...), custom_call_target="tpu_custom_call" | custom-call | flops 17179869184 | bytes 1179648 | tf_op jit(solution)/shard_map/leaf_couple/pallas_call | solution.py:445
  27.2 0.0 collective-permute-done.7.rest_1_
  27.2 2.4 %collective-permute-done.8.rest_2_ = bf16[6,64,128]{2,1,0:T(8,128)(2,1)S(1)} collective-permute-done((bf16[6,64,128]{2,1,0:T(8,128)(2,1)S(1)}, bf16[6,64,128]{2,1,0:T(8,128)(2,1)S(1)}, u32[]{:S(2)}, u32[]{:S(2)}) %collective-permute-start.8) | collective-permute-done | bytes 98336 | tf_op jit(solution)/shard_map/ppermute | solution.py:358
  29.6 0.0 collective-permute-done.9.rest_3_
  29.6 1.2 %parent_couple.1 = bf16[6,3,4096]{2,1,0:T(4,128)(2,1)} custom-call(s32[3,6]{1,0:T(4,128)S(1)} %get-tuple-element.28.table_in, bf16[6,64,384]{2,1,0:T(8,128)(2,1)S(1)} %get-tuple-element.29.middle, f32[8,128]{1,0:T(8,128)S(1)} %get-tuple-element.30._, bf16[6,64,128]{2,1,0:T(8,128)(2,1)S(1)} %parent_step.1.parent_change.rest_0_, ...), custom_call_target="tpu_custom_call" | custom-call | flops 98304 | bytes 393216 | tf_op jit(solution)/shard_map/parent_couple/pallas_call | solution.py:454
  (4 shorter events, 0.0 us)
Async XLA Ops:
  0.6 2.8 %collective-permute-start = (bf16[12,128,128]{2,1,0:T(8,128)(2,1)}, bf16[12,128,128]{2,1,0:T(8,128)(2,1)S(1)}, u32[]{:S(2)}, u32[]{:S(2)}) collective-permute-start(bf16[12,128,128]{2,1,0:T(8,128)(2,1)} %transfers.1), channel_id=1, source_target_pairs={{0,1},{1,0},{2,3},{3,2},{4,5},{5,4},{6,7},{7,6},{8,9},{9,8},{10,11... | collective-permute-start | bytes 1179656 | tf_op jit(solution)/shard_map/ppermute | solution.py:358
  1.1 1.7 %copy-start = (bf16[12,6,128,128]{3,2,1,0:T(8,128)(2,1)S(1)}, bf16[12,6,128,128]{3,2,1,0:T(8,128)(2,1)}, u32[]{:S(2)}) copy-start(bf16[12,6,128,128]{3,2,1,0:T(8,128)(2,1)} %blocks.7) | copy-start | bytes 7077892
  2.8 1.1 %copy-start.3 = (bf16[6,3,128,128]{3,2,1,0:T(8,128)(2,1)S(1)}, bf16[6,3,128,128]{3,2,1,0:T(8,128)(2,1)}, u32[]{:S(2)}) copy-start(bf16[6,3,128,128]{3,2,1,0:T(8,128)(2,1)} %parents.3) | copy-start | bytes 1769476
  2.8 1.1 %copy-start.6 = (s32[12,6]{0,1:T(8,128)S(1)}, s32[12,6]{0,1:T(8,128)}, u32[]{:S(2)}) copy-start(s32[12,6]{0,1:T(8,128)} %param.13) | copy-start | bytes 868
  2.8 1.1 %copy-start.7 = (s32[12,6]{0,1:T(8,128)S(1)}, s32[12,6]{0,1:T(8,128)}, u32[]{:S(2)}) copy-start(s32[12,6]{0,1:T(8,128)} %param.14) | copy-start | bytes 868
  2.8 1.1 %copy-start.8 = (s32[6,3]{0,1:T(4,128)S(1)}, s32[6,3]{0,1:T(4,128)}, u32[]{:S(2)}) copy-start(s32[6,3]{0,1:T(4,128)} %param.16) | copy-start | bytes 220
  2.8 1.1 %copy-start.9 = (s32[6,3]{0,1:T(4,128)S(1)}, s32[6,3]{0,1:T(4,128)}, u32[]{:S(2)}) copy-start(s32[6,3]{0,1:T(4,128)} %param.17) | copy-start | bytes 220
  3.3 1.8 %copy-start.4 = (bf16[12,128,128]{2,1,0:T(8,128)(2,1)S(1)}, bf16[12,128,128]{2,1,0:T(8,128)(2,1)}, u32[]{:S(2)}) copy-start(bf16[12,128,128]{2,1,0:T(8,128)(2,1)} %transfers.1) | copy-start | bytes 1179652
  3.3 1.8 %copy-start.5 = (f32[64,128]{1,0:T(8,128)S(1)}, f32[64,128]{1,0:T(8,128)}, u32[]{:S(2)}) copy-start(f32[64,128]{1,0:T(8,128)} %start.2) | copy-start | bytes 98308
  3.3 1.8 %collective-permute-start.1 = (f32[6,128,128]{2,1,0:T(8,128)S(1)}, f32[6,128,128]{2,1,0:T(8,128)S(1)}, u32[]{:S(2)}, u32[]{:S(2)}) collective-permute-start(f32[6,128,128]{2,1,0:T(8,128)S(1)} %sent_weights.1), channel_id=1, source_target_pairs={{0,1},{1,0},{2,3},{3,2},{4,5},{5,4},{6,7},{7,6},{8,9},{9,8},{10,11... | collective-permute-start | bytes 1179656 | tf_op jit(solution)/shard_map/ppermute | solution.py:358
  3.9 10.0 %copy-start.10 = (f32[64,128]{1,0:T(8,128)S(1)}, f32[64,128]{1,0:T(8,128)}, u32[]{:S(2)}) copy-start(f32[64,128]{1,0:T(8,128)} %start.3) | copy-start | bytes 98308
  3.9 18.4 %copy-start.1 = (bf16[12,6,128,128]{3,2,1,0:T(8,128)(2,1)S(1)}, bf16[12,6,128,128]{3,2,1,0:T(8,128)(2,1)}, u32[]{:S(2)}) copy-start(bf16[12,6,128,128]{3,2,1,0:T(8,128)(2,1)} %blocks.7) | copy-start | bytes 7077892
  3.9 18.4 %copy-start.2 = (bf16[12,256,128]{2,1,0:T(8,128)(2,1)S(1)}, bf16[12,256,128]{2,1,0:T(8,128)(2,1)}, u32[]{:S(2)}) copy-start(bf16[12,256,128]{2,1,0:T(8,128)(2,1)} %bases.3) | copy-start | bytes 2359300
  9.3 10.4 %collective-permute-start.2 = (bf16[2,6,64,128]{3,2,1,0:T(8,128)(2,1)S(1)}, bf16[2,6,64,128]{3,2,1,0:T(8,128)(2,1)S(1)}, u32[]{:S(2)}, u32[]{:S(2)}) collective-permute-start(bf16[2,6,64,128]{3,2,1,0:T(8,128)(2,1)S(1)} %get-tuple-element.19.change.rest_0_), channel_id=1, source_target_pairs={{0,1},{1,0},{2,3},{3,2},{4,5},{5,4},{6,7},{7,6},{8,9},{9,8},{10,11... | collective-permute-start | bytes 589832 | tf_op jit(solution)/shard_map/ppermute | solution.py:358
  9.5 13.4 %collective-permute-start.3 = (bf16[2,6,64,128]{3,2,1,0:T(8,128)(2,1)S(1)}, bf16[2,6,64,128]{3,2,1,0:T(8,128)(2,1)S(1)}, u32[]{:S(2)}, u32[]{:S(2)}) collective-permute-start(bf16[2,6,64,128]{3,2,1,0:T(8,128)(2,1)S(1)} %get-tuple-element.19.change.rest_0_), channel_id=1, source_target_pairs={{0,2},{1,3},{2,0},{3,1},{4,6},{5,7},{6,4},{7,5},{8,10},{9,11},{10,... | collective-permute-start | bytes 589832 | tf_op jit(solution)/shard_map/ppermute | solution.py:358
  12.3 10.9 %collective-permute-start.4 = (bf16[2,6,64,128]{3,2,1,0:T(8,128)(2,1)S(1)}, bf16[2,6,64,128]{3,2,1,0:T(8,128)(2,1)S(1)}, u32[]{:S(2)}, u32[]{:S(2)}) collective-permute-start(bf16[2,6,64,128]{3,2,1,0:T(8,128)(2,1)S(1)} %get-tuple-element.19.change.rest_0_), channel_id=1, source_target_pairs={{0,4},{1,5},{2,6},{3,7},{4,0},{5,1},{6,2},{7,3},{8,12},{9,13},{10,... | collective-permute-start | bytes 589832 | tf_op jit(solution)/shard_map/ppermute | solution.py:358
  13.9 9.4 %collective-permute-start.5 = (bf16[2,6,64,128]{3,2,1,0:T(8,128)(2,1)S(1)}, bf16[2,6,64,128]{3,2,1,0:T(8,128)(2,1)S(1)}, u32[]{:S(2)}, u32[]{:S(2)}) collective-permute-start(bf16[2,6,64,128]{3,2,1,0:T(8,128)(2,1)S(1)} %get-tuple-element.19.change.rest_0_), channel_id=1, source_target_pairs={{0,6},{1,7},{2,4},{3,5},{4,2},{5,3},{6,0},{7,1},{8,14},{9,15},{10,... | collective-permute-start | bytes 589832 | tf_op jit(solution)/shard_map/ppermute | solution.py:358
  17.6 9.6 %collective-permute-start.7 = (bf16[6,64,128]{2,1,0:T(8,128)(2,1)S(1)}, bf16[6,64,128]{2,1,0:T(8,128)(2,1)S(1)}, u32[]{:S(2)}, u32[]{:S(2)}) collective-permute-start(bf16[6,64,128]{2,1,0:T(8,128)(2,1)S(1)} %parent_step.1.parent_change.rest_0_), channel_id=1, source_target_pairs={{0,8},{8,0},{16,24},{24,16},{1,9},{9,1},{17,25},{25,17},{2,10},{10... | collective-permute-start | bytes 294920 | tf_op jit(solution)/shard_map/ppermute | solution.py:358
  19.7 9.9 %collective-permute-start.8 = (bf16[6,64,128]{2,1,0:T(8,128)(2,1)S(1)}, bf16[6,64,128]{2,1,0:T(8,128)(2,1)S(1)}, u32[]{:S(2)}, u32[]{:S(2)}) collective-permute-start(bf16[6,64,128]{2,1,0:T(8,128)(2,1)S(1)} %parent_step.1.parent_change.rest_0_), channel_id=1, source_target_pairs={{0,16},{8,24},{16,0},{24,8},{1,17},{9,25},{17,1},{25,9},{2,18},{10... | collective-permute-start | bytes 294920 | tf_op jit(solution)/shard_map/ppermute | solution.py:358
  22.9 6.7 %collective-permute-start.9 = (bf16[6,64,128]{2,1,0:T(8,128)(2,1)S(1)}, bf16[6,64,128]{2,1,0:T(8,128)(2,1)S(1)}, u32[]{:S(2)}, u32[]{:S(2)}) collective-permute-start(bf16[6,64,128]{2,1,0:T(8,128)(2,1)S(1)} %parent_step.1.parent_change.rest_0_), channel_id=1, source_target_pairs={{0,24},{8,16},{16,8},{24,0},{1,25},{9,17},{17,9},{25,1},{2,26},{10... | collective-permute-start | bytes 294920 | tf_op jit(solution)/shard_map/ppermute | solution.py:358
  23.3 2.1 %collective-permute-start.6 = (bf16[6,6,64,128]{3,2,1,0:T(8,128)(2,1)S(1)}, bf16[6,6,64,128]{3,2,1,0:T(8,128)(2,1)S(1)}, u32[]{:S(2)}, u32[]{:S(2)}) collective-permute-start(bf16[6,6,64,128]{3,2,1,0:T(8,128)(2,1)S(1)} %pack.1._), channel_id=1, source_target_pairs={{0,1},{1,0},{2,3},{3,2},{4,5},{5,4},{6,7},{7,6},{8,9},{9,8},{10,11... | collective-permute-start | bytes 1769480 | tf_op jit(solution)/shard_map/ppermute | solution.py:358

commit v6 on v4

--- a/solution.py
+++ b/solution.py
@@ -157,21 +157,38 @@
 
 
 def kept_weights(
-    blocks, parents, devs, slots, groups, parent_slots,
-    weight, parent_weight, leaf_table, parent_table,
+    order, blocks, parents, devs, slots, groups, parent_slots, transfers, start_rows, _,
+    own_images, parent_weight, leaf_table, parent_table,
 ):
-    half = weight.shape[0]
+    half = own_images.shape[0]
     index = lax.axis_index("sub")
     member, chip = index & 1, index >> 1
     dev, slot = devs[...], slots[...]
     side = jnp.where(slot >= half, 1, 0)
     box = ((dev >> 1) ^ chip) * 2 + (side ^ member)
     leaf_table[...] = (box * 2 + ((dev & 1) ^ side)) * half + slot - side * half
-    parent_table[...] = (groups[...] ^ lax.axis_index("grp")) * half + parent_slots[...]
-    start = (lax.axis_index("sub") % 2) * half
-    for j in range(half):
-        weight[j] = gram_sum([blocks[start + j, c] for c in range(blocks.shape[1])])
+    apart = groups[...] ^ lax.axis_index("grp")
+    place = jnp.zeros_like(apart)
+    for at, mask in enumerate(order):
+        place = jnp.where(apart == mask, at, place)
+    parent_table[...] = place * half + parent_slots[...]
+    start = member * half
+    weights = []
+    for j in range(half):
         parent_weight[j] = gram_sum([parents[j, c] for c in range(parents.shape[1])])
+        weights.append(gram_sum([blocks[start + j, c] for c in range(blocks.shape[1])]))
+    moves = [transfers[start + j] for j in range(half)]
+    weights = descend(weights, moves, [parent_weight[j] for j in range(half)])
+    for j, image in enumerate(images_of(wide(start_rows[...]), weights)):
+        own_images[j] = image
+
+
+def descend(weights, moves, parents):
+    carried = [fold(dot(move, wide(parent))) for move, parent in zip(moves, parents)]
+    return [
+        weight + dot_t(wide(part), cat([move, move], 1))
+        for weight, part, move in zip(weights, carried, moves)
+    ]
 
 
 def images_of(starts, weights):
@@ -180,22 +197,21 @@
     return [fold(dot(wide(image), each)) for image, each in zip(images, folded)]
 
 
-def leaf_step(own, other, parent, transfers, other_transfers, start, change, stacked, grid, made, turned, stored):
+def leaf_step(
+    own_images, other, parent, transfers, other_transfers, start, change, stacked,
+    grid, made, turned, stored,
+):
     rank = start.shape[0]
-    half = own.shape[0]
+    half = other.shape[0]
     member = lax.axis_index("sub") % 2
     first = member * half
     moves = [(transfers[first + j], other_transfers[first + j]) for j in range(half)]
-    size = parent.shape[1]
-    carried = [fold(dot(cat(moves[j], 0), wide(parent[j]))) for j in range(half)]
-    weights = []
-    for j in range(half):
-        for at, base in enumerate((own[j], other[j])):
-            part = wide(carried[j][at * size : at * size + size])
-            weights.append(base + dot_t(part, cat([moves[j][at]] * 2, 1)))
-    images = images_of(wide(start[...]), weights)
-    for j in range(half):
-        store_gram(grid, stored, j, images[2 * j : 2 * j + 2], rank)
+    weights = descend(
+        [other[j] for j in range(half)], [move for _, move in moves], [parent[j] for j in range(half)]
+    )
+    others = images_of(wide(start[...]), weights)
+    for j in range(half):
+        store_gram(grid, stored, j, [own_images[j], others[j]], rank)
     eliminate(grid, made, turned, rank, half)
     found = [pair_rows(made, stored, j, rank).astype(BF16) for j in range(half)]
     for j in range(half):
@@ -358,6 +374,10 @@
     return lax.ppermute(block, axis, [(i, i ^ mask) for i in range(count)])
 
 
+def group_order(groups):
+    return (0, 2, 3, 1) if groups == 4 else tuple(range(groups))
+
+
 def shards(
     leaf_bases,
     leaf_transfers,
@@ -387,14 +407,16 @@
         "sent_weights", 8, 2 * links * square * old, 2 * links * square,
     )(leaf_blocks)
     other = swap(sent, "sub", 1)
+    order = group_order(groups)
     own, parent_weight, leaf_table, parent_table = call(
-        kept_weights, [VMEM] * 6,
-        [weights, weights, shape((links, count), jnp.int32), shape((parent_links, half), jnp.int32)],
+        functools.partial(kept_weights, order), [VMEM] * 9,
+        [shape((half, rank, old), F32), weights, shape((links, count), jnp.int32), shape((parent_links, half), jnp.int32)],
         [],
         "kept_weights", 8, 2 * (links + parent_links) * square * old, 8 * links * square,
     )(
         leaf_blocks, parent_blocks,
         leaf_partner_dev.T, leaf_partner_slot.T, parent_partner_group.T, parent_partner_slot.T,
+        leaf_transfers, leaf_start, other_transfers,
     )
     tables = [
         pltpu.VMEM((8 * rank, 2 * rank), F32),
@@ -415,7 +437,7 @@
         tables, "parent_step", 8, 20 * square * old, 8 * square,
     )(parent_weight, stacked, parent_start)
     parents_held = [parent_change] + [
-        swap(parent_change, "grp", m) for m in range(1, groups)
+        swap(parent_change, "grp", m) for m in order[1:]
     ]
     token = shape((8, 128), F32)
     half_shape = shape((half, rank, links * old), BF16)

time: 31.2 us -> 29.9 us (0.958)
  waiting for transfers between devices: 4.38 us -> 2.59 us
  local copies, waits for them, and re-layouts: 1.71 us -> 2.23 us
    ppermute x10, waiting for transfers between devices: 4.38 us -> 2.59 us  [swap(): return lax.ppermute(block, axis, [(i, i ^ mask) for i in range(count)])]
    pallas_call x1, Pallas kernels: 0.68 us -> 1.26 us  [shards(): call(functools.partial(kept_weights, order), [VMEM] * 9, [shape((half, ra...]
    unnamed x22, local copies, waits for them, and re-layouts: 1.71 us -> 2.23 us
    pallas_call x1, Pallas kernels: 4.14 us -> 3.77 us  [shards(): call(leaf_step, [VMEM] * 6, [shape((2, half, rank, old), BF16), shape((ha...]
  transfers between devices with their start and end apart: 10 -> 10, of which waited for: 5 -> 5; matrix products, arithmetic and copies ran while one was open for 0% -> 0% of each run, Pallas kernels for 26% -> 31%
where the time goes in v6:
time: 29.9 us; the launch traced here: 29.7 us
  Pallas kernels  14 us (47%)
  starting transfers between devices  10.1 us (34%)
  waiting for transfers between devices  2.59 us (9%)
  local copies, waits for them, and re-layouts  2.23 us (7%)
  between operations  0.78 us (3%)
    ppermute x10, starting transfers between devices, swap(): return lax.ppermute(block, axis, [(i, i ^ mask) for i in range(count)])  10.1 us
    pallas_call x1, Pallas kernels, shards(): call(leaf_step, [VMEM] * 6, [shape((2, half, rank, old), BF16), shape((ha...  3.77 us
    pallas_call x1, Pallas kernels, shards(): call(parent_step, [VMEM] * 3, shape((half, rank, old), BF16), tables, 'pa...  3.73 us
    ppermute x10, waiting for transfers between devices, swap(): return lax.ppermute(block, axis, [(i, i ^ mask) for i in range(count)])  2.59 us
    unnamed x22, local copies, waits for them, and re-layouts  2.23 us
    pallas_call x1, Pallas kernels, shards(): call(functools.partial(leaf_couple, boxes), [VMEM] * (4 + len(held)), [sh...  1.86 us
    pallas_call x1, Pallas kernels, shards(): call(functools.partial(kept_weights, order), [VMEM] * 9, [shape((half, ra...  1.26 us
    pallas_call x1, Pallas kernels, shards(): call(middle_other, [VMEM] * 5, [shape((count, rank, points), BF16), half_...  1.17 us
  transfers between devices with their start and end apart: 10, of which 5 were waited for; matrix products, arithmetic and copies ran while one was open for 0% of the time, Pallas kernels for 31%

profile of v6, /device:TPU:0, one launch (start us, length us, event | category | flops | bytes accessed | tf_op | source)
XLA Modules:
  0.0 29.7 jit_solution(169164070193378125)
XLA Ops:
  0.6 0.5 %collective-permute-start = (bf16[12,128,128]{2,1,0:T(8,128)(2,1)}, bf16[12,128,128]{2,1,0:T(8,128)(2,1)S(1)}, u32[]{:S(2)}, u32[]{:S(2)}) collective-permute-start(bf16[12,128,128]{2,1,0:T(8,128)(2,1)} %transfers.3), channel_id=1, source_target_pairs={{0,1},{1,0},{2,3},{3,2},{4,5},{5,4},{6,7},{7,6},{8,9},{9,8},{10,11... | collective-permute-start | bytes 1179656 | tf_op jit(solution)/shard_map/ppermute | solution.py:374
  1.2 1.7 %copy-done = bf16[12,6,128,128]{3,2,1,0:T(8,128)(2,1)S(1)} copy-done((bf16[12,6,128,128]{3,2,1,0:T(8,128)(2,1)S(1)}, bf16[12,6,128,128]{3,2,1,0:T(8,128)(2,1)}, u32[]{:S(2)}) %copy-start) | copy-done | bytes 2359320
  2.8 0.0 copy-start.3
  2.8 0.0 copy-start.4
  2.8 0.0 copy-start.6
  2.8 0.0 copy-start.7
  2.8 0.0 copy-start.8
  2.8 0.0 copy-start.9
  2.9 0.5 %sent_weights.1 = f32[6,128,128]{2,1,0:T(8,128)S(1)} custom-call(bf16[12,6,128,128]{3,2,1,0:T(8,128)(2,1)S(1)} %copy-done), custom_call_target="tpu_custom_call" | custom-call | flops 150994944 | bytes 1179648 | tf_op jit(solution)/shard_map/sent_weights/pallas_call | solution.py:405
  3.3 0.1 collective-permute-start.1
  3.5 0.0 collective-permute-done._.other_transfers
  3.5 0.4 %copy-done.3 = bf16[6,3,128,128]{3,2,1,0:T(8,128)(2,1)S(1)} copy-done((bf16[6,3,128,128]{3,2,1,0:T(8,128)(2,1)S(1)}, bf16[6,3,128,128]{3,2,1,0:T(8,128)(2,1)}, u32[]{:S(2)}) %copy-start.3) | copy-done | bytes 589848
  3.9 0.1 copy-done.4
  4.0 0.0 copy-done.5
  4.0 0.0 copy-done.6
  4.0 0.0 copy-done.7
  4.0 0.0 copy-done.8
  4.0 0.0 copy-done.9
  4.0 0.0 copy-start.10
  4.0 0.0 copy-start.1
  4.0 0.0 copy-start.2
  4.0 1.3 %kept_weights.1 = (f32[6,64,128]{2,1,0:T(8,128)S(1)}, f32[6,128,128]{2,1,0:T(8,128)S(1)}, s32[6,12]{1,0:T(8,128)S(1)}, s32[3,6]{1,0:T(4,128)S(1)}) custom-call(bf16[12,6,128,128]{3,2,1,0:T(8,128)(2,1)S(1)} %copy-done, bf16[6,3,128,128]{3,2,1,0:T(8,128)(2,1)S(1)} %copy-done.3, s32[6,12]{1,0:T(8,128)S(1)} %bitcast.4, s32[6,12]{1,0:T(8,128)S(1)} %bitcast.5, ...), custom_call_target="tpu_custom_call" | custom-call | flops 226492416 | bytes 4718592 | tf_op jit(solution)/shard_map/kept_weights/pallas_call | solution.py:411
  5.3 0.0 collective-permute-done.1.other
  5.3 3.8 %leaf_step.1 = (bf16[2,6,64,128]{3,2,1,0:T(8,128)(2,1)S(1)}, f32[6,2,64,128]{3,2,1,0:T(8,128)S(1)}) custom-call(f32[6,64,128]{2,1,0:T(8,128)S(1)} %get-tuple-element.17.own_images, f32[6,128,128]{2,1,0:T(8,128)S(1)} %collective-permute-done.1.other, f32[6,128,128]{2,1,0:T(8,128)S(1)} %get-tuple-element.18.parent, bf16[12,128,128]{2,1,0:T(8,128)(2,1)S(1)} %copy-done.4, ...), custom_call_target="tpu_custom_call" | custom-call | flops 503316480 | bytes 786432 | tf_op jit(solution)/shard_map/leaf_step/pallas_call | solution.py:427
  9.1 0.1 collective-permute-start.2
  9.2 2.9 %collective-permute-start.3 = (bf16[2,6,64,128]{3,2,1,0:T(8,128)(2,1)S(1)}, bf16[2,6,64,128]{3,2,1,0:T(8,128)(2,1)S(1)}, u32[]{:S(2)}, u32[]{:S(2)}) collective-permute-start(bf16[2,6,64,128]{3,2,1,0:T(8,128)(2,1)S(1)} %get-tuple-element.19.change.rest_0_), channel_id=1, source_target_pairs={{0,2},{1,3},{2,0},{3,1},{4,6},{5,7},{6,4},{7,5},{8,10},{9,11},{10,... | collective-permute-start | bytes 589832 | tf_op jit(solution)/shard_map/ppermute | solution.py:374
  12.2 1.5 %collective-permute-start.4 = (bf16[2,6,64,128]{3,2,1,0:T(8,128)(2,1)S(1)}, bf16[2,6,64,128]{3,2,1,0:T(8,128)(2,1)S(1)}, u32[]{:S(2)}, u32[]{:S(2)}) collective-permute-start(bf16[2,6,64,128]{3,2,1,0:T(8,128)(2,1)S(1)} %get-tuple-element.19.change.rest_0_), channel_id=1, source_target_pairs={{0,4},{1,5},{2,6},{3,7},{4,0},{5,1},{6,2},{7,3},{8,12},{9,13},{10,... | collective-permute-start | bytes 589832 | tf_op jit(solution)/shard_map/ppermute | solution.py:374
  13.7 0.0 collective-permute-start.5
  13.7 0.0 copy-done.10
  13.7 3.7 %parent_step.1.parent_change.rest_0_ = bf16[6,64,128]{2,1,0:T(8,128)(2,1)S(1)} custom-call(f32[6,128,128]{2,1,0:T(8,128)S(1)} %get-tuple-element.18.parent, f32[6,2,64,128]{3,2,1,0:T(8,128)S(1)} %get-tuple-element.20.stacked, f32[64,128]{1,0:T(8,128)S(1)} %copy-done.10), custom_call_target="tpu_custom_call" | custom-call | flops 251658240 | bytes 786432 | tf_op jit(solution)/shard_map/parent_step/pallas_call | solution.py:435
  17.4 3.1 %collective-permute-start.7 = (bf16[6,64,128]{2,1,0:T(8,128)(2,1)S(1)}, bf16[6,64,128]{2,1,0:T(8,128)(2,1)S(1)}, u32[]{:S(2)}, u32[]{:S(2)}) collective-permute-start(bf16[6,64,128]{2,1,0:T(8,128)(2,1)S(1)} %parent_step.1.parent_change.rest_0_), channel_id=1, source_target_pairs={{0,16},{8,24},{16,0},{24,8},{1,17},{9,25},{17,1},{25,9},{2,18},{10... | collective-permute-start | bytes 294920 | tf_op jit(solution)/shard_map/ppermute | solution.py:374
  20.6 0.0 collective-permute-done.2._.swapped.rest_1_
  20.6 1.3 %collective-permute-start.8 = (bf16[6,64,128]{2,1,0:T(8,128)(2,1)S(1)}, bf16[6,64,128]{2,1,0:T(8,128)(2,1)S(1)}, u32[]{:S(2)}, u32[]{:S(2)}) collective-permute-start(bf16[6,64,128]{2,1,0:T(8,128)(2,1)S(1)} %parent_step.1.parent_change.rest_0_), channel_id=1, source_target_pairs={{0,24},{8,16},{16,8},{24,0},{1,25},{9,17},{17,9},{25,1},{2,26},{10... | collective-permute-start | bytes 294920 | tf_op jit(solution)/shard_map/ppermute | solution.py:374
  21.9 0.0 copy-done.1
  21.9 0.0 copy-done.2
  21.9 0.5 %middle_own.1 = (bf16[6,64,256]{2,1,0:T(8,128)(2,1)S(1)}, bf16[6,64,768]{2,1,0:T(8,128)(2,1)S(1)}, bf16[6,64,384]{2,1,0:T(8,128)(2,1)S(1)}, f32[8,128]{1,0:T(8,128)S(1)}) custom-call(bf16[2,6,64,128]{3,2,1,0:T(8,128)(2,1)S(1)} %get-tuple-element.19.change.rest_0_, bf16[6,64,128]{2,1,0:T(8,128)(2,1)S(1)} %parent_step.1.parent_change.rest_0_, ...), custom_call_target="tpu_custom_call" | custom-call | flops 17179869184 | bytes 98304 | tf_op jit(solution)/shard_map/middle_own/pallas_call | solution.py:444
  22.5 0.0 collective-permute-done.3.refs_1_.rest_2_
  22.5 0.3 %collective-permute-start.9 = (bf16[6,64,128]{2,1,0:T(8,128)(2,1)S(1)}, bf16[6,64,128]{2,1,0:T(8,128)(2,1)S(1)}, u32[]{:S(2)}, u32[]{:S(2)}) collective-permute-start(bf16[6,64,128]{2,1,0:T(8,128)(2,1)S(1)} %parent_step.1.parent_change.rest_0_), channel_id=1, source_target_pairs={{0,8},{8,0},{16,24},{24,16},{1,9},{9,1},{17,25},{25,17},{2,10},{10... | collective-permute-start | bytes 294920 | tf_op jit(solution)/shard_map/ppermute | solution.py:374
  22.8 0.2 collective-permute-done.4.refs_2_.rest_3_
  23.0 0.0 collective-permute-done.5.refs_3_.rest_4_
  23.0 0.1 collective-permute-start.6
  23.1 1.2 %middle_other.1 = (bf16[12,64,256]{2,1,0:T(8,128)(2,1)}, bf16[6,64,768]{2,1,0:T(8,128)(2,1)S(1)}) custom-call(bf16[2,6,64,128]{3,2,1,0:T(8,128)(2,1)S(1)} %collective-permute-done.2._.swapped.rest_1_, bf16[12,256,128]{2,1,0:T(8,128)(2,1)S(1)} %copy-done.2, bf16[12,6,128,128]{3,2,1,0:T(8,128)(2,1)S(1)} %copy-done.1, ...), custom_call_target="tpu_custom_call" | custom-call | flops 98304 | bytes 98304 | tf_op jit(solution)/shard_map/middle_other/pallas_call | solution.py:457
  24.3 0.8 %collective-permute-done.6.rest_5_ = bf16[6,6,64,128]{3,2,1,0:T(8,128)(2,1)S(1)} collective-permute-done((bf16[6,6,64,128]{3,2,1,0:T(8,128)(2,1)S(1)}, bf16[6,6,64,128]{3,2,1,0:T(8,128)(2,1)S(1)}, u32[]{:S(2)}, u32[]{:S(2)}) %collective-permute-start.6) | collective-permute-done | bytes 589856 | tf_op jit(solution)/shard_map/ppermute | solution.py:374
  25.1 1.9 %leaf_couple.1 = (bf16[12,6,4096]{2,1,0:T(8,128)(2,1)}, f32[8,128]{1,0:T(8,128)S(1)}) custom-call(s32[6,12]{1,0:T(8,128)S(1)} %get-tuple-element.24.table_in, bf16[6,64,768]{2,1,0:T(8,128)(2,1)S(1)} %get-tuple-element.25.own_half, bf16[6,64,768]{2,1,0:T(8,128)(2,1)S(1)} %get-tuple-element.26.other_half, f32[8,128]{1,0:T(8,128)S(1)} %pause.1._, ...), custom_call_target="tpu_custom_call" | custom-call | flops 17179869184 | bytes 1179648 | tf_op jit(solution)/shard_map/leaf_couple/pallas_call | solution.py:466
  27.0 0.3 collective-permute-done.7.rest_1_
  27.3 0.5 %collective-permute-done.8.rest_2_ = bf16[6,64,128]{2,1,0:T(8,128)(2,1)S(1)} collective-permute-done((bf16[6,64,128]{2,1,0:T(8,128)(2,1)S(1)}, bf16[6,64,128]{2,1,0:T(8,128)(2,1)S(1)}, u32[]{:S(2)}, u32[]{:S(2)}) %collective-permute-start.8) | collective-permute-done | bytes 98336 | tf_op jit(solution)/shard_map/ppermute | solution.py:374
  27.8 0.8 %collective-permute-done.9.rest_3_ = bf16[6,64,128]{2,1,0:T(8,128)(2,1)S(1)} collective-permute-done((bf16[6,64,128]{2,1,0:T(8,128)(2,1)S(1)}, bf16[6,64,128]{2,1,0:T(8,128)(2,1)S(1)}, u32[]{:S(2)}, u32[]{:S(2)}) %collective-permute-start.9) | collective-permute-done | bytes 98336 | tf_op jit(solution)/shard_map/ppermute | solution.py:374
  28.5 1.2 %parent_couple.1 = bf16[6,3,4096]{2,1,0:T(4,128)(2,1)} custom-call(s32[3,6]{1,0:T(4,128)S(1)} %get-tuple-element.28.table_in, bf16[6,64,384]{2,1,0:T(8,128)(2,1)S(1)} %get-tuple-element.29.middle, f32[8,128]{1,0:T(8,128)S(1)} %get-tuple-element.30._, bf16[6,64,128]{2,1,0:T(8,128)(2,1)S(1)} %parent_step.1.parent_change.rest_0_, ...), custom_call_target="tpu_custom_call" | custom-call | flops 98304 | bytes 393216 | tf_op jit(solution)/shard_map/parent_couple/pallas_call | solution.py:475
  (4 shorter events, 0.0 us)
Async XLA Ops:
  0.6 2.8 %collective-permute-start = (bf16[12,128,128]{2,1,0:T(8,128)(2,1)}, bf16[12,128,128]{2,1,0:T(8,128)(2,1)S(1)}, u32[]{:S(2)}, u32[]{:S(2)}) collective-permute-start(bf16[12,128,128]{2,1,0:T(8,128)(2,1)} %transfers.3), channel_id=1, source_target_pairs={{0,1},{1,0},{2,3},{3,2},{4,5},{5,4},{6,7},{7,6},{8,9},{9,8},{10,11... | collective-permute-start | bytes 1179656 | tf_op jit(solution)/shard_map/ppermute | solution.py:374
  1.2 1.7 %copy-start = (bf16[12,6,128,128]{3,2,1,0:T(8,128)(2,1)S(1)}, bf16[12,6,128,128]{3,2,1,0:T(8,128)(2,1)}, u32[]{:S(2)}) copy-start(bf16[12,6,128,128]{3,2,1,0:T(8,128)(2,1)} %blocks.7) | copy-start | bytes 7077892
  2.8 1.1 %copy-start.3 = (bf16[6,3,128,128]{3,2,1,0:T(8,128)(2,1)S(1)}, bf16[6,3,128,128]{3,2,1,0:T(8,128)(2,1)}, u32[]{:S(2)}) copy-start(bf16[6,3,128,128]{3,2,1,0:T(8,128)(2,1)} %parents.3) | copy-start | bytes 1769476
  2.8 1.2 %copy-start.4 = (bf16[12,128,128]{2,1,0:T(8,128)(2,1)S(1)}, bf16[12,128,128]{2,1,0:T(8,128)(2,1)}, u32[]{:S(2)}) copy-start(bf16[12,128,128]{2,1,0:T(8,128)(2,1)} %transfers.3) | copy-start | bytes 1179652
  2.8 1.2 %copy-start.5 = (f32[64,128]{1,0:T(8,128)S(1)}, f32[64,128]{1,0:T(8,128)}, u32[]{:S(2)}) copy-start(f32[64,128]{1,0:T(8,128)} %start.2) | copy-start | bytes 98308
  2.8 1.2 %copy-start.6 = (s32[12,6]{0,1:T(8,128)S(1)}, s32[12,6]{0,1:T(8,128)}, u32[]{:S(2)}) copy-start(s32[12,6]{0,1:T(8,128)} %param.13) | copy-start | bytes 868
  2.8 1.2 %copy-start.7 = (s32[12,6]{0,1:T(8,128)S(1)}, s32[12,6]{0,1:T(8,128)}, u32[]{:S(2)}) copy-start(s32[12,6]{0,1:T(8,128)} %param.14) | copy-start | bytes 868
  2.8 1.2 %copy-start.8 = (s32[6,3]{0,1:T(4,128)S(1)}, s32[6,3]{0,1:T(4,128)}, u32[]{:S(2)}) copy-start(s32[6,3]{0,1:T(4,128)} %param.16) | copy-start | bytes 220
  2.8 1.2 %copy-start.9 = (s32[6,3]{0,1:T(4,128)S(1)}, s32[6,3]{0,1:T(4,128)}, u32[]{:S(2)}) copy-start(s32[6,3]{0,1:T(4,128)} %param.17) | copy-start | bytes 220
  3.3 2.0 %collective-permute-start.1 = (f32[6,128,128]{2,1,0:T(8,128)S(1)}, f32[6,128,128]{2,1,0:T(8,128)S(1)}, u32[]{:S(2)}, u32[]{:S(2)}) collective-permute-start(f32[6,128,128]{2,1,0:T(8,128)S(1)} %sent_weights.1), channel_id=1, source_target_pairs={{0,1},{1,0},{2,3},{3,2},{4,5},{5,4},{6,7},{7,6},{8,9},{9,8},{10,11... | collective-permute-start | bytes 1179656 | tf_op jit(solution)/shard_map/ppermute | solution.py:374
  4.0 9.7 %copy-start.10 = (f32[64,128]{1,0:T(8,128)S(1)}, f32[64,128]{1,0:T(8,128)}, u32[]{:S(2)}) copy-start(f32[64,128]{1,0:T(8,128)} %start.3) | copy-start | bytes 98308
  4.0 17.9 %copy-start.1 = (bf16[12,6,128,128]{3,2,1,0:T(8,128)(2,1)S(1)}, bf16[12,6,128,128]{3,2,1,0:T(8,128)(2,1)}, u32[]{:S(2)}) copy-start(bf16[12,6,128,128]{3,2,1,0:T(8,128)(2,1)} %blocks.7) | copy-start | bytes 7077892
  4.0 17.9 %copy-start.2 = (bf16[12,256,128]{2,1,0:T(8,128)(2,1)S(1)}, bf16[12,256,128]{2,1,0:T(8,128)(2,1)}, u32[]{:S(2)}) copy-start(bf16[12,256,128]{2,1,0:T(8,128)(2,1)} %bases.3) | copy-start | bytes 2359300
  9.1 11.5 %collective-permute-start.2 = (bf16[2,6,64,128]{3,2,1,0:T(8,128)(2,1)S(1)}, bf16[2,6,64,128]{3,2,1,0:T(8,128)(2,1)S(1)}, u32[]{:S(2)}, u32[]{:S(2)}) collective-permute-start(bf16[2,6,64,128]{3,2,1,0:T(8,128)(2,1)S(1)} %get-tuple-element.19.change.rest_0_), channel_id=1, source_target_pairs={{0,1},{1,0},{2,3},{3,2},{4,5},{5,4},{6,7},{7,6},{8,9},{9,8},{10,11... | collective-permute-start | bytes 589832 | tf_op jit(solution)/shard_map/ppermute | solution.py:374
  9.2 13.3 %collective-permute-start.3 = (bf16[2,6,64,128]{3,2,1,0:T(8,128)(2,1)S(1)}, bf16[2,6,64,128]{3,2,1,0:T(8,128)(2,1)S(1)}, u32[]{:S(2)}, u32[]{:S(2)}) collective-permute-start(bf16[2,6,64,128]{3,2,1,0:T(8,128)(2,1)S(1)} %get-tuple-element.19.change.rest_0_), channel_id=1, source_target_pairs={{0,2},{1,3},{2,0},{3,1},{4,6},{5,7},{6,4},{7,5},{8,10},{9,11},{10,... | collective-permute-start | bytes 589832 | tf_op jit(solution)/shard_map/ppermute | solution.py:374
  12.2 10.8 %collective-permute-start.4 = (bf16[2,6,64,128]{3,2,1,0:T(8,128)(2,1)S(1)}, bf16[2,6,64,128]{3,2,1,0:T(8,128)(2,1)S(1)}, u32[]{:S(2)}, u32[]{:S(2)}) collective-permute-start(bf16[2,6,64,128]{3,2,1,0:T(8,128)(2,1)S(1)} %get-tuple-element.19.change.rest_0_), channel_id=1, source_target_pairs={{0,4},{1,5},{2,6},{3,7},{4,0},{5,1},{6,2},{7,3},{8,12},{9,13},{10,... | collective-permute-start | bytes 589832 | tf_op jit(solution)/shard_map/ppermute | solution.py:374
  13.7 9.3 %collective-permute-start.5 = (bf16[2,6,64,128]{3,2,1,0:T(8,128)(2,1)S(1)}, bf16[2,6,64,128]{3,2,1,0:T(8,128)(2,1)S(1)}, u32[]{:S(2)}, u32[]{:S(2)}) collective-permute-start(bf16[2,6,64,128]{3,2,1,0:T(8,128)(2,1)S(1)} %get-tuple-element.19.change.rest_0_), channel_id=1, source_target_pairs={{0,6},{1,7},{2,4},{3,5},{4,2},{5,3},{6,0},{7,1},{8,14},{9,15},{10,... | collective-permute-start | bytes 589832 | tf_op jit(solution)/shard_map/ppermute | solution.py:374
  17.4 9.8 %collective-permute-start.7 = (bf16[6,64,128]{2,1,0:T(8,128)(2,1)S(1)}, bf16[6,64,128]{2,1,0:T(8,128)(2,1)S(1)}, u32[]{:S(2)}, u32[]{:S(2)}) collective-permute-start(bf16[6,64,128]{2,1,0:T(8,128)(2,1)S(1)} %parent_step.1.parent_change.rest_0_), channel_id=1, source_target_pairs={{0,16},{8,24},{16,0},{24,8},{1,17},{9,25},{17,1},{25,9},{2,18},{10... | collective-permute-start | bytes 294920 | tf_op jit(solution)/shard_map/ppermute | solution.py:374
  20.6 7.2 %collective-permute-start.8 = (bf16[6,64,128]{2,1,0:T(8,128)(2,1)S(1)}, bf16[6,64,128]{2,1,0:T(8,128)(2,1)S(1)}, u32[]{:S(2)}, u32[]{:S(2)}) collective-permute-start(bf16[6,64,128]{2,1,0:T(8,128)(2,1)S(1)} %parent_step.1.parent_change.rest_0_), channel_id=1, source_target_pairs={{0,24},{8,16},{16,8},{24,0},{1,25},{9,17},{17,9},{25,1},{2,26},{10... | collective-permute-start | bytes 294920 | tf_op jit(solution)/shard_map/ppermute | solution.py:374
  22.5 6.1 %collective-permute-start.9 = (bf16[6,64,128]{2,1,0:T(8,128)(2,1)S(1)}, bf16[6,64,128]{2,1,0:T(8,128)(2,1)S(1)}, u32[]{:S(2)}, u32[]{:S(2)}) collective-permute-start(bf16[6,64,128]{2,1,0:T(8,128)(2,1)S(1)} %parent_step.1.parent_change.rest_0_), channel_id=1, source_target_pairs={{0,8},{8,0},{16,24},{24,16},{1,9},{9,1},{17,25},{25,17},{2,10},{10... | collective-permute-start | bytes 294920 | tf_op jit(solution)/shard_map/ppermute | solution.py:374
  23.0 2.1 %collective-permute-start.6 = (bf16[6,6,64,128]{3,2,1,0:T(8,128)(2,1)S(1)}, bf16[6,6,64,128]{3,2,1,0:T(8,128)(2,1)S(1)}, u32[]{:S(2)}, u32[]{:S(2)}) collective-permute-start(bf16[6,6,64,128]{3,2,1,0:T(8,128)(2,1)S(1)} %pack.1._), channel_id=1, source_target_pairs={{0,1},{1,0},{2,3},{3,2},{4,5},{5,4},{6,7},{7,6},{8,9},{9,8},{10,11... | collective-permute-start | bytes 1769480 | tf_op jit(solution)/shard_map/ppermute | solution.py:374

commit v7 on v6

--- a/solution.py
+++ b/solution.py
@@ -336,7 +336,8 @@
 
 
 def parent_couple(table_in, middle, _, *rest):
-    near, (out, held, order) = rest[:-3], rest[-3:]
+    near, (out, held, order, done, sems) = rest[:-5], rest[-5:]
+    copies = []
     table = table_in[...]
     count, links = out.shape[0], out.shape[1]
     rank = middle.shape[1]
@@ -347,7 +348,11 @@
             order[p % 2, pl.ds(c, rank // 2, stride=8), :] = couple(
                 middle[p, :, c * 128 : c * 128 + 128], held[table[c, p]]
             )
-        write_rows(out, p, order.at[p % 2], links, rank // 2)
+        write_rows(done, p, order.at[p % 2], links, rank // 2)
+        copies.append(pltpu.make_async_copy(done.at[p], out.at[p], sems.at[p]))
+        copies[p].start()
+    for copy in copies:
+        copy.wait()
 
 
 VMEM = pl.BlockSpec(memory_space=pltpu.VMEM)
@@ -355,13 +360,13 @@
 HBM = pl.BlockSpec(memory_space=pltpu.HBM)
 
 
-def call(body, ins, out_shapes, scratch, name, mib, flops, moved):
+def call(body, ins, out_shapes, scratch, name, mib, flops, moved, out_specs=None):
     many = isinstance(out_shapes, list)
     return pl.pallas_call(
         body,
         out_shape=out_shapes,
         in_specs=ins,
-        out_specs=[VMEM] * len(out_shapes) if many else VMEM,
+        out_specs=out_specs or ([VMEM] * len(out_shapes) if many else VMEM),
         scratch_shapes=scratch,
         name=name,
         compiler_params=pltpu.CompilerParams(vmem_limit_bytes=mib * MIB),
@@ -478,8 +483,10 @@
         [
             pltpu.VMEM((groups * half, rank, old), BF16),
             pltpu.VMEM((2, 4 * rank, 2 * rank), F32),
+            pltpu.VMEM((half, parent_links, rank * rank), BF16),
+            dma((half,)),
         ],
-        "parent_couple", 4 + groups, square, 4 * square,
+        "parent_couple", 4 + groups, square, 4 * square, HBM,
     )(parent_table, parent_half, after_leaves, *parents_held)
     return (new_leaf_bases, new_leaf_blocks, new_parent_blocks)
 

time: 29.9 us -> 29.9 us (level)
  no operation moved by 1% of the time
where the time goes in v7:
time: 29.9 us; the launch traced here: 29.7 us
  Pallas kernels  14 us (47%)
  starting transfers between devices  10.1 us (34%)
  waiting for transfers between devices  2.59 us (9%)
  local copies, waits for them, and re-layouts  2.23 us (7%)
  between operations  0.78 us (3%)
    ppermute x10, starting transfers between devices, swap(): return lax.ppermute(block, axis, [(i, i ^ mask) for i in range(count)])  10.1 us
    pallas_call x1, Pallas kernels, shards(): call(leaf_step, [VMEM] * 6, [shape((2, half, rank, old), BF16), shape((ha...  3.77 us
    pallas_call x1, Pallas kernels, shards(): call(parent_step, [VMEM] * 3, shape((half, rank, old), BF16), tables, 'pa...  3.73 us
    ppermute x10, waiting for transfers between devices, swap(): return lax.ppermute(block, axis, [(i, i ^ mask) for i in range(count)])  2.59 us
    unnamed x22, local copies, waits for them, and re-layouts  2.23 us
    pallas_call x1, Pallas kernels, shards(): call(functools.partial(leaf_couple, boxes), [VMEM] * (4 + len(held)), [sh...  1.86 us
    pallas_call x1, Pallas kernels, shards(): call(functools.partial(kept_weights, order), [VMEM] * 9, [shape((half, ra...  1.26 us
    pallas_call x1, Pallas kernels, shards(): call(middle_other, [VMEM] * 5, [shape((count, rank, points), BF16), half_...  1.17 us
  transfers between devices with their start and end apart: 10, of which 5 were waited for; matrix products, arithmetic and copies ran while one was open for 0% of the time, Pallas kernels for 31%

profile of v7, /device:TPU:0, one launch (start us, length us, event | category | flops | bytes accessed | tf_op | source)
XLA Modules:
  0.0 29.7 jit_solution(7260934992969045274)
XLA Ops:
  0.6 0.5 %collective-permute-start = (bf16[12,128,128]{2,1,0:T(8,128)(2,1)}, bf16[12,128,128]{2,1,0:T(8,128)(2,1)S(1)}, u32[]{:S(2)}, u32[]{:S(2)}) collective-permute-start(bf16[12,128,128]{2,1,0:T(8,128)(2,1)} %transfers.3), channel_id=1, source_target_pairs={{0,1},{1,0},{2,3},{3,2},{4,5},{5,4},{6,7},{7,6},{8,9},{9,8},{10,11... | collective-permute-start | bytes 1179656 | tf_op jit(solution)/shard_map/ppermute | solution.py:379
  1.2 0.0 copy-start
  1.2 1.7 %copy-done = bf16[12,6,128,128]{3,2,1,0:T(8,128)(2,1)S(1)} copy-done((bf16[12,6,128,128]{3,2,1,0:T(8,128)(2,1)S(1)}, bf16[12,6,128,128]{3,2,1,0:T(8,128)(2,1)}, u32[]{:S(2)}) %copy-start) | copy-done | bytes 2359320
  2.8 0.0 copy-start.3
  2.8 0.0 copy-start.4
  2.8 0.0 copy-start.7
  2.8 0.0 copy-start.8
  2.8 0.0 copy-start.9
  2.9 0.5 %sent_weights.1 = f32[6,128,128]{2,1,0:T(8,128)S(1)} custom-call(bf16[12,6,128,128]{3,2,1,0:T(8,128)(2,1)S(1)} %copy-done), custom_call_target="tpu_custom_call" | custom-call | flops 150994944 | bytes 1179648 | tf_op jit(solution)/shard_map/sent_weights/pallas_call | solution.py:410
  3.3 0.1 collective-permute-start.1
  3.5 0.0 collective-permute-done._.other_transfers
  3.5 0.4 %copy-done.3 = bf16[6,3,128,128]{3,2,1,0:T(8,128)(2,1)S(1)} copy-done((bf16[6,3,128,128]{3,2,1,0:T(8,128)(2,1)S(1)}, bf16[6,3,128,128]{3,2,1,0:T(8,128)(2,1)}, u32[]{:S(2)}) %copy-start.3) | copy-done | bytes 589848
  3.9 0.1 copy-done.4
  4.0 0.0 copy-done.5
  4.0 0.0 copy-done.6
  4.0 0.0 copy-done.7
  4.0 0.0 copy-done.8
  4.0 0.0 copy-done.9
  4.0 0.0 copy-start.10
  4.0 0.0 copy-start.1
  4.0 0.0 copy-start.2
  4.0 1.3 %kept_weights.1 = (f32[6,64,128]{2,1,0:T(8,128)S(1)}, f32[6,128,128]{2,1,0:T(8,128)S(1)}, s32[6,12]{1,0:T(8,128)S(1)}, s32[3,6]{1,0:T(4,128)S(1)}) custom-call(bf16[12,6,128,128]{3,2,1,0:T(8,128)(2,1)S(1)} %copy-done, bf16[6,3,128,128]{3,2,1,0:T(8,128)(2,1)S(1)} %copy-done.3, s32[6,12]{1,0:T(8,128)S(1)} %bitcast.4, s32[6,12]{1,0:T(8,128)S(1)} %bitcast.5, ...), custom_call_target="tpu_custom_call" | custom-call | flops 226492416 | bytes 4718592 | tf_op jit(solution)/shard_map/kept_weights/pallas_call | solution.py:416
  5.3 0.0 collective-permute-done.1.other
  5.3 3.8 %leaf_step.1 = (bf16[2,6,64,128]{3,2,1,0:T(8,128)(2,1)S(1)}, f32[6,2,64,128]{3,2,1,0:T(8,128)S(1)}) custom-call(f32[6,64,128]{2,1,0:T(8,128)S(1)} %get-tuple-element.17.own_images, f32[6,128,128]{2,1,0:T(8,128)S(1)} %collective-permute-done.1.other, f32[6,128,128]{2,1,0:T(8,128)S(1)} %get-tuple-element.18.parent, bf16[12,128,128]{2,1,0:T(8,128)(2,1)S(1)} %copy-done.4, ...), custom_call_target="tpu_custom_call" | custom-call | flops 503316480 | bytes 786432 | tf_op jit(solution)/shard_map/leaf_step/pallas_call | solution.py:432
  9.1 0.1 collective-permute-start.2
  9.2 2.9 %collective-permute-start.3 = (bf16[2,6,64,128]{3,2,1,0:T(8,128)(2,1)S(1)}, bf16[2,6,64,128]{3,2,1,0:T(8,128)(2,1)S(1)}, u32[]{:S(2)}, u32[]{:S(2)}) collective-permute-start(bf16[2,6,64,128]{3,2,1,0:T(8,128)(2,1)S(1)} %get-tuple-element.19.change.rest_0_), channel_id=1, source_target_pairs={{0,2},{1,3},{2,0},{3,1},{4,6},{5,7},{6,4},{7,5},{8,10},{9,11},{10,... | collective-permute-start | bytes 589832 | tf_op jit(solution)/shard_map/ppermute | solution.py:379
  12.2 1.5 %collective-permute-start.4 = (bf16[2,6,64,128]{3,2,1,0:T(8,128)(2,1)S(1)}, bf16[2,6,64,128]{3,2,1,0:T(8,128)(2,1)S(1)}, u32[]{:S(2)}, u32[]{:S(2)}) collective-permute-start(bf16[2,6,64,128]{3,2,1,0:T(8,128)(2,1)S(1)} %get-tuple-element.19.change.rest_0_), channel_id=1, source_target_pairs={{0,4},{1,5},{2,6},{3,7},{4,0},{5,1},{6,2},{7,3},{8,12},{9,13},{10,... | collective-permute-start | bytes 589832 | tf_op jit(solution)/shard_map/ppermute | solution.py:379
  13.7 0.0 collective-permute-start.5
  13.7 0.0 copy-done.10
  13.7 3.7 %parent_step.1.parent_change.rest_0_ = bf16[6,64,128]{2,1,0:T(8,128)(2,1)S(1)} custom-call(f32[6,128,128]{2,1,0:T(8,128)S(1)} %get-tuple-element.18.parent, f32[6,2,64,128]{3,2,1,0:T(8,128)S(1)} %get-tuple-element.20.stacked, f32[64,128]{1,0:T(8,128)S(1)} %copy-done.10), custom_call_target="tpu_custom_call" | custom-call | flops 251658240 | bytes 786432 | tf_op jit(solution)/shard_map/parent_step/pallas_call | solution.py:440
  17.4 3.1 %collective-permute-start.7 = (bf16[6,64,128]{2,1,0:T(8,128)(2,1)S(1)}, bf16[6,64,128]{2,1,0:T(8,128)(2,1)S(1)}, u32[]{:S(2)}, u32[]{:S(2)}) collective-permute-start(bf16[6,64,128]{2,1,0:T(8,128)(2,1)S(1)} %parent_step.1.parent_change.rest_0_), channel_id=1, source_target_pairs={{0,16},{8,24},{16,0},{24,8},{1,17},{9,25},{17,1},{25,9},{2,18},{10... | collective-permute-start | bytes 294920 | tf_op jit(solution)/shard_map/ppermute | solution.py:379
  20.6 0.0 collective-permute-done.2._.swapped.rest_1_
  20.6 1.3 %collective-permute-start.8 = (bf16[6,64,128]{2,1,0:T(8,128)(2,1)S(1)}, bf16[6,64,128]{2,1,0:T(8,128)(2,1)S(1)}, u32[]{:S(2)}, u32[]{:S(2)}) collective-permute-start(bf16[6,64,128]{2,1,0:T(8,128)(2,1)S(1)} %parent_step.1.parent_change.rest_0_), channel_id=1, source_target_pairs={{0,24},{8,16},{16,8},{24,0},{1,25},{9,17},{17,9},{25,1},{2,26},{10... | collective-permute-start | bytes 294920 | tf_op jit(solution)/shard_map/ppermute | solution.py:379
  21.9 0.0 copy-done.1
  21.9 0.0 copy-done.2
  21.9 0.5 %middle_own.1 = (bf16[6,64,256]{2,1,0:T(8,128)(2,1)S(1)}, bf16[6,64,768]{2,1,0:T(8,128)(2,1)S(1)}, bf16[6,64,384]{2,1,0:T(8,128)(2,1)S(1)}, f32[8,128]{1,0:T(8,128)S(1)}) custom-call(bf16[2,6,64,128]{3,2,1,0:T(8,128)(2,1)S(1)} %get-tuple-element.19.change.rest_0_, bf16[6,64,128]{2,1,0:T(8,128)(2,1)S(1)} %parent_step.1.parent_change.rest_0_, ...), custom_call_target="tpu_custom_call" | custom-call | flops 17179869184 | bytes 98304 | tf_op jit(solution)/shard_map/middle_own/pallas_call | solution.py:449
  22.5 0.0 collective-permute-done.3.refs_1_.rest_2_
  22.5 0.3 %collective-permute-start.9 = (bf16[6,64,128]{2,1,0:T(8,128)(2,1)S(1)}, bf16[6,64,128]{2,1,0:T(8,128)(2,1)S(1)}, u32[]{:S(2)}, u32[]{:S(2)}) collective-permute-start(bf16[6,64,128]{2,1,0:T(8,128)(2,1)S(1)} %parent_step.1.parent_change.rest_0_), channel_id=1, source_target_pairs={{0,8},{8,0},{16,24},{24,16},{1,9},{9,1},{17,25},{25,17},{2,10},{10... | collective-permute-start | bytes 294920 | tf_op jit(solution)/shard_map/ppermute | solution.py:379
  22.8 0.2 collective-permute-done.4.refs_2_.rest_3_
  23.0 0.0 collective-permute-done.5.refs_3_.rest_4_
  23.0 0.1 collective-permute-start.6
  23.1 1.2 %middle_other.1 = (bf16[12,64,256]{2,1,0:T(8,128)(2,1)}, bf16[6,64,768]{2,1,0:T(8,128)(2,1)S(1)}) custom-call(bf16[2,6,64,128]{3,2,1,0:T(8,128)(2,1)S(1)} %collective-permute-done.2._.swapped.rest_1_, bf16[12,256,128]{2,1,0:T(8,128)(2,1)S(1)} %copy-done.2, bf16[12,6,128,128]{3,2,1,0:T(8,128)(2,1)S(1)} %copy-done.1, ...), custom_call_target="tpu_custom_call" | custom-call | flops 98304 | bytes 98304 | tf_op jit(solution)/shard_map/middle_other/pallas_call | solution.py:462
  24.3 0.8 %collective-permute-done.6.rest_5_ = bf16[6,6,64,128]{3,2,1,0:T(8,128)(2,1)S(1)} collective-permute-done((bf16[6,6,64,128]{3,2,1,0:T(8,128)(2,1)S(1)}, bf16[6,6,64,128]{3,2,1,0:T(8,128)(2,1)S(1)}, u32[]{:S(2)}, u32[]{:S(2)}) %collective-permute-start.6) | collective-permute-done | bytes 589856 | tf_op jit(solution)/shard_map/ppermute | solution.py:379
  25.1 1.9 %leaf_couple.1 = (bf16[12,6,4096]{2,1,0:T(8,128)(2,1)}, f32[8,128]{1,0:T(8,128)S(1)}) custom-call(s32[6,12]{1,0:T(8,128)S(1)} %get-tuple-element.24.table_in, bf16[6,64,768]{2,1,0:T(8,128)(2,1)S(1)} %get-tuple-element.25.own_half, bf16[6,64,768]{2,1,0:T(8,128)(2,1)S(1)} %get-tuple-element.26.other_half, f32[8,128]{1,0:T(8,128)S(1)} %pause.1._, ...), custom_call_target="tpu_custom_call" | custom-call | flops 17179869184 | bytes 1179648 | tf_op jit(solution)/shard_map/leaf_couple/pallas_call | solution.py:471
  27.0 0.3 collective-permute-done.7.rest_1_
  27.3 0.5 %collective-permute-done.8.rest_2_ = bf16[6,64,128]{2,1,0:T(8,128)(2,1)S(1)} collective-permute-done((bf16[6,64,128]{2,1,0:T(8,128)(2,1)S(1)}, bf16[6,64,128]{2,1,0:T(8,128)(2,1)S(1)}, u32[]{:S(2)}, u32[]{:S(2)}) %collective-permute-start.8) | collective-permute-done | bytes 98336 | tf_op jit(solution)/shard_map/ppermute | solution.py:379
  27.8 0.8 %collective-permute-done.9.rest_3_ = bf16[6,64,128]{2,1,0:T(8,128)(2,1)S(1)} collective-permute-done((bf16[6,64,128]{2,1,0:T(8,128)(2,1)S(1)}, bf16[6,64,128]{2,1,0:T(8,128)(2,1)S(1)}, u32[]{:S(2)}, u32[]{:S(2)}) %collective-permute-start.9) | collective-permute-done | bytes 98336 | tf_op jit(solution)/shard_map/ppermute | solution.py:379
  28.5 1.1 %parent_couple.1 = bf16[6,3,4096]{2,1,0:T(4,128)(2,1)} custom-call(s32[3,6]{1,0:T(4,128)S(1)} %get-tuple-element.28.table_in, bf16[6,64,384]{2,1,0:T(8,128)(2,1)S(1)} %get-tuple-element.29.middle, f32[8,128]{1,0:T(8,128)S(1)} %get-tuple-element.30._, bf16[6,64,128]{2,1,0:T(8,128)(2,1)S(1)} %parent_step.1.parent_change.rest_0_, ...), custom_call_target="tpu_custom_call" | custom-call | flops 98304 | bytes 393216 | tf_op jit(solution)/shard_map/parent_couple/pallas_call | solution.py:480
  (4 shorter events, 0.0 us)
Async XLA Ops:
  0.6 2.8 %collective-permute-start = (bf16[12,128,128]{2,1,0:T(8,128)(2,1)}, bf16[12,128,128]{2,1,0:T(8,128)(2,1)S(1)}, u32[]{:S(2)}, u32[]{:S(2)}) collective-permute-start(bf16[12,128,128]{2,1,0:T(8,128)(2,1)} %transfers.3), channel_id=1, source_target_pairs={{0,1},{1,0},{2,3},{3,2},{4,5},{5,4},{6,7},{7,6},{8,9},{9,8},{10,11... | collective-permute-start | bytes 1179656 | tf_op jit(solution)/shard_map/ppermute | solution.py:379
  1.2 1.7 %copy-start = (bf16[12,6,128,128]{3,2,1,0:T(8,128)(2,1)S(1)}, bf16[12,6,128,128]{3,2,1,0:T(8,128)(2,1)}, u32[]{:S(2)}) copy-start(bf16[12,6,128,128]{3,2,1,0:T(8,128)(2,1)} %blocks.7) | copy-start | bytes 7077892
  2.8 1.1 %copy-start.3 = (bf16[6,3,128,128]{3,2,1,0:T(8,128)(2,1)S(1)}, bf16[6,3,128,128]{3,2,1,0:T(8,128)(2,1)}, u32[]{:S(2)}) copy-start(bf16[6,3,128,128]{3,2,1,0:T(8,128)(2,1)} %parents.3) | copy-start | bytes 1769476
  2.8 1.2 %copy-start.4 = (bf16[12,128,128]{2,1,0:T(8,128)(2,1)S(1)}, bf16[12,128,128]{2,1,0:T(8,128)(2,1)}, u32[]{:S(2)}) copy-start(bf16[12,128,128]{2,1,0:T(8,128)(2,1)} %transfers.3) | copy-start | bytes 1179652
  2.8 1.2 %copy-start.5 = (f32[64,128]{1,0:T(8,128)S(1)}, f32[64,128]{1,0:T(8,128)}, u32[]{:S(2)}) copy-start(f32[64,128]{1,0:T(8,128)} %start.2) | copy-start | bytes 98308
  2.8 1.2 %copy-start.6 = (s32[12,6]{0,1:T(8,128)S(1)}, s32[12,6]{0,1:T(8,128)}, u32[]{:S(2)}) copy-start(s32[12,6]{0,1:T(8,128)} %param.13) | copy-start | bytes 868
  2.8 1.2 %copy-start.7 = (s32[12,6]{0,1:T(8,128)S(1)}, s32[12,6]{0,1:T(8,128)}, u32[]{:S(2)}) copy-start(s32[12,6]{0,1:T(8,128)} %param.14) | copy-start | bytes 868
  2.8 1.2 %copy-start.8 = (s32[6,3]{0,1:T(4,128)S(1)}, s32[6,3]{0,1:T(4,128)}, u32[]{:S(2)}) copy-start(s32[6,3]{0,1:T(4,128)} %param.16) | copy-start | bytes 220
  2.8 1.2 %copy-start.9 = (s32[6,3]{0,1:T(4,128)S(1)}, s32[6,3]{0,1:T(4,128)}, u32[]{:S(2)}) copy-start(s32[6,3]{0,1:T(4,128)} %param.17) | copy-start | bytes 220
  3.3 2.0 %collective-permute-start.1 = (f32[6,128,128]{2,1,0:T(8,128)S(1)}, f32[6,128,128]{2,1,0:T(8,128)S(1)}, u32[]{:S(2)}, u32[]{:S(2)}) collective-permute-start(f32[6,128,128]{2,1,0:T(8,128)S(1)} %sent_weights.1), channel_id=1, source_target_pairs={{0,1},{1,0},{2,3},{3,2},{4,5},{5,4},{6,7},{7,6},{8,9},{9,8},{10,11... | collective-permute-start | bytes 1179656 | tf_op jit(solution)/shard_map/ppermute | solution.py:379
  4.0 9.7 %copy-start.10 = (f32[64,128]{1,0:T(8,128)S(1)}, f32[64,128]{1,0:T(8,128)}, u32[]{:S(2)}) copy-start(f32[64,128]{1,0:T(8,128)} %start.3) | copy-start | bytes 98308
  4.0 17.9 %copy-start.1 = (bf16[12,6,128,128]{3,2,1,0:T(8,128)(2,1)S(1)}, bf16[12,6,128,128]{3,2,1,0:T(8,128)(2,1)}, u32[]{:S(2)}) copy-start(bf16[12,6,128,128]{3,2,1,0:T(8,128)(2,1)} %blocks.7) | copy-start | bytes 7077892
  4.0 17.9 %copy-start.2 = (bf16[12,256,128]{2,1,0:T(8,128)(2,1)S(1)}, bf16[12,256,128]{2,1,0:T(8,128)(2,1)}, u32[]{:S(2)}) copy-start(bf16[12,256,128]{2,1,0:T(8,128)(2,1)} %bases.3) | copy-start | bytes 2359300
  9.1 11.5 %collective-permute-start.2 = (bf16[2,6,64,128]{3,2,1,0:T(8,128)(2,1)S(1)}, bf16[2,6,64,128]{3,2,1,0:T(8,128)(2,1)S(1)}, u32[]{:S(2)}, u32[]{:S(2)}) collective-permute-start(bf16[2,6,64,128]{3,2,1,0:T(8,128)(2,1)S(1)} %get-tuple-element.19.change.rest_0_), channel_id=1, source_target_pairs={{0,1},{1,0},{2,3},{3,2},{4,5},{5,4},{6,7},{7,6},{8,9},{9,8},{10,11... | collective-permute-start | bytes 589832 | tf_op jit(solution)/shard_map/ppermute | solution.py:379
  9.2 13.3 %collective-permute-start.3 = (bf16[2,6,64,128]{3,2,1,0:T(8,128)(2,1)S(1)}, bf16[2,6,64,128]{3,2,1,0:T(8,128)(2,1)S(1)}, u32[]{:S(2)}, u32[]{:S(2)}) collective-permute-start(bf16[2,6,64,128]{3,2,1,0:T(8,128)(2,1)S(1)} %get-tuple-element.19.change.rest_0_), channel_id=1, source_target_pairs={{0,2},{1,3},{2,0},{3,1},{4,6},{5,7},{6,4},{7,5},{8,10},{9,11},{10,... | collective-permute-start | bytes 589832 | tf_op jit(solution)/shard_map/ppermute | solution.py:379
  12.2 10.8 %collective-permute-start.4 = (bf16[2,6,64,128]{3,2,1,0:T(8,128)(2,1)S(1)}, bf16[2,6,64,128]{3,2,1,0:T(8,128)(2,1)S(1)}, u32[]{:S(2)}, u32[]{:S(2)}) collective-permute-start(bf16[2,6,64,128]{3,2,1,0:T(8,128)(2,1)S(1)} %get-tuple-element.19.change.rest_0_), channel_id=1, source_target_pairs={{0,4},{1,5},{2,6},{3,7},{4,0},{5,1},{6,2},{7,3},{8,12},{9,13},{10,... | collective-permute-start | bytes 589832 | tf_op jit(solution)/shard_map/ppermute | solution.py:379
  13.7 9.3 %collective-permute-start.5 = (bf16[2,6,64,128]{3,2,1,0:T(8,128)(2,1)S(1)}, bf16[2,6,64,128]{3,2,1,0:T(8,128)(2,1)S(1)}, u32[]{:S(2)}, u32[]{:S(2)}) collective-permute-start(bf16[2,6,64,128]{3,2,1,0:T(8,128)(2,1)S(1)} %get-tuple-element.19.change.rest_0_), channel_id=1, source_target_pairs={{0,6},{1,7},{2,4},{3,5},{4,2},{5,3},{6,0},{7,1},{8,14},{9,15},{10,... | collective-permute-start | bytes 589832 | tf_op jit(solution)/shard_map/ppermute | solution.py:379
  17.4 9.8 %collective-permute-start.7 = (bf16[6,64,128]{2,1,0:T(8,128)(2,1)S(1)}, bf16[6,64,128]{2,1,0:T(8,128)(2,1)S(1)}, u32[]{:S(2)}, u32[]{:S(2)}) collective-permute-start(bf16[6,64,128]{2,1,0:T(8,128)(2,1)S(1)} %parent_step.1.parent_change.rest_0_), channel_id=1, source_target_pairs={{0,16},{8,24},{16,0},{24,8},{1,17},{9,25},{17,1},{25,9},{2,18},{10... | collective-permute-start | bytes 294920 | tf_op jit(solution)/shard_map/ppermute | solution.py:379
  20.6 7.2 %collective-permute-start.8 = (bf16[6,64,128]{2,1,0:T(8,128)(2,1)S(1)}, bf16[6,64,128]{2,1,0:T(8,128)(2,1)S(1)}, u32[]{:S(2)}, u32[]{:S(2)}) collective-permute-start(bf16[6,64,128]{2,1,0:T(8,128)(2,1)S(1)} %parent_step.1.parent_change.rest_0_), channel_id=1, source_target_pairs={{0,24},{8,16},{16,8},{24,0},{1,25},{9,17},{17,9},{25,1},{2,26},{10... | collective-permute-start | bytes 294920 | tf_op jit(solution)/shard_map/ppermute | solution.py:379
  22.5 6.1 %collective-permute-start.9 = (bf16[6,64,128]{2,1,0:T(8,128)(2,1)S(1)}, bf16[6,64,128]{2,1,0:T(8,128)(2,1)S(1)}, u32[]{:S(2)}, u32[]{:S(2)}) collective-permute-start(bf16[6,64,128]{2,1,0:T(8,128)(2,1)S(1)} %parent_step.1.parent_change.rest_0_), channel_id=1, source_target_pairs={{0,8},{8,0},{16,24},{24,16},{1,9},{9,1},{17,25},{25,17},{2,10},{10... | collective-permute-start | bytes 294920 | tf_op jit(solution)/shard_map/ppermute | solution.py:379
  23.0 2.1 %collective-permute-start.6 = (bf16[6,6,64,128]{3,2,1,0:T(8,128)(2,1)S(1)}, bf16[6,6,64,128]{3,2,1,0:T(8,128)(2,1)S(1)}, u32[]{:S(2)}, u32[]{:S(2)}) collective-permute-start(bf16[6,6,64,128]{3,2,1,0:T(8,128)(2,1)S(1)} %pack.1._), channel_id=1, source_target_pairs={{0,1},{1,0},{2,3},{3,2},{4,5},{5,4},{6,7},{7,6},{8,9},{9,8},{10,11... | collective-permute-start | bytes 1769480 | tf_op jit(solution)/shard_map/ppermute | solution.py:379
